TPU v7x, 256 devices: a whole 4x4x8 slice. The times are simulated.
256 devices in a mesh: rows: 32 (over z_hi, y, core), cols: 8 (over x, z_lo).
Axes of the slice: x: 4, y: 4, z: 8 (z_hi: 4, z_lo: 2; z = z_hi * 2 + z_lo), core: 2. Of those that a mesh axis runs over, the one named last changes fastest.
Arguments:
- queries: bfloat16 [1024, 16384], P(None, 'rows'), may hold values from -6 to 6
- inverse_gram: bfloat16 [16384, 16384], P('rows', 'cols'), may hold values from -2 to 2, as said below
- slab: bfloat16 [8192, 16384], P('rows', 'cols'), may hold values from -0.046875 to 0.046875
Outputs:
- scores: bfloat16 [1024, 8192], P('cols', 'rows')
Inputs may be any that keep to these rules, and one draw needn't show every extreme that they name: inverse_gram has a diagonal of 0.5 to 2 and small entries elsewhere.
All inputs are finite; a program needn't handle non-finite values.
Results may differ from a plain program's by a relative error of at most 0.0049.
Values may be sent and summed in bfloat16 or wider, within the bound.
No kernel may reach another device: no remote copies, remote signals or barrier semaphores. Data moves between devices by JAX's collectives and lax.ppermute only.
A program may use at most 64 MiB of HBM per device.

v0:
```python
import jax
import jax.numpy as jnp
from jax import lax
from jax.sharding import PartitionSpec as P


def local(queries, inverse_gram, slab):
    partial_images = jnp.dot(queries, inverse_gram, preferred_element_type=jnp.float32)
    images = lax.psum(partial_images, "rows").astype(jnp.bfloat16)
    partial_scores = lax.dot_general(
        images, slab, (((1,), (1,)), ((), ())), preferred_element_type=jnp.float32
    )
    summed = lax.psum_scatter(partial_scores, "cols", scatter_dimension=0, tiled=True)
    return summed.astype(jnp.bfloat16)


def solution(mesh):
    return jax.shard_map(
        local,
        mesh=mesh,
        in_specs=(P(None, "rows"), P("rows", "cols"), P("rows", "cols")),
        out_specs=P("cols", "rows"),
        check_vma=False,
    )
```

profile of v0, /device:TPU:1, one launch (start us, length us, event | category | flops | bytes accessed | tf_op | source)
XLA Modules:
  0.0 283.3 jit_solution(11196562205380409295)
XLA Ops:
  6.5 0.0 copy-start
  6.5 0.0 reduce-scatter.2.cloned.1.call-start
  6.5 1.6 copy-done
  8.1 6.8 %fusion.2 = f32[1024,2048]{1,0:T(8,128)} fusion(bf16[1024,512]{1,0:T(8,128)(2,1)} %param.3, bf16[512,2048]{1,0:T(8,128)(2,1)S(1)} %copy-done), kind=kOutput, calls=%fused_computation.2 | convolution fusion | flops 2147483648 | bytes 11534336 | tf_op jit(solution)/shard_map/dot_general | solution.py:8
  14.9 0.0 copy-start.1
  14.9 210.9 %all-reduce.1 = bf16[1024,2048]{1,0:T(8,128)(2,1)} all-reduce(f32[1024,2048]{1,0:T(8,128)} %fusion.2), channel_id=1, replica_groups=mesh['rows'=32,'cols'=8] {'rows'}, use_global_device_ids=true, to_apply=%region_0.0 | all-reduce | flops 2097152 | bytes 12582912 | tf_op jit(solution)/shard_map/psum | solution.py:9
  225.8 0.0 copy-done.1
  225.8 4.5 %fusion.3 = f32[1024,256]{1,0:T(8,128)} fusion(bf16[1024,2048]{1,0:T(8,128)(2,1)} %all-reduce.1, bf16[256,2048]{1,0:T(8,128)(2,1)S(1)} %copy-done.1), kind=kOutput, calls=%fused_computation.3 | convolution fusion | flops 1073741824 | bytes 6291456 | tf_op jit(solution)/shard_map/dot_general | solution.py:10
  230.3 0.0 reduce-scatter.2.cloned.1.call-update
  230.3 44.6 %reduce-scatter.2.cloned.1.call-done = f32[128,256]{1,0:T(8,128)} async-done(((f32[1024,256]{1,0:T(8,128)}), f32[128,256]{1,0:T(8,128)}) %reduce-scatter.2.cloned.1.call-update) | async-done | bytes 131088 | tf_op jit(solution)/shard_map/reduce_scatter | solution.py:13
  274.9 1.5 convert_element_type.7
Async XLA Ops:
  6.5 1.6 copy-start
  6.5 268.3 %reduce-scatter.2.cloned.1.call-start = ((), (), s32[]{:S(2)}) async-start(), calls=%async_computation.1 | async-start | bytes 1179648 | tf_op jit(solution)/shard_map/reduce_scatter | solution.py:13
  14.9 210.9 %copy-start.1 = (bf16[256,2048]{1,0:T(8,128)(2,1)S(1)}, bf16[256,2048]{1,0:T(8,128)(2,1)}, u32[]{:S(2)}) copy-start(bf16[256,2048]{1,0:T(8,128)(2,1)} %param.5) | copy-start | bytes 3145732
Sparse Core Ops, SparseCore 0:
  230.4 44.3 reduce-scatter.1
where the time goes:
time: 287 us; the launch traced here: 283 us
  blocking collectives  211 us (74%)
  waiting for transfers between devices  44.6 us (16%)
  between operations  13.4 us (5%)
  matrix products  11.3 us (4%)
    psum x1, blocking collectives, local(): images = lax.psum(partial_images, 'rows').astype(jnp.bfloat16)  211 us
    reduce_scatter x1, waiting for transfers between devices, local(): lax.psum_scatter(partial_scores, 'cols', scatter_dimension=0, tiled=True)  44.6 us
    dot_general x1, matrix products, local(): jnp.dot(queries, inverse_gram, preferred_element_type=jnp.float32)  6.79 us
  transfers between devices with their start and end apart: 1, of which 1 were waited for; matrix products, arithmetic and copies ran while one was open for 0% of the time, Pallas kernels for 0%

commit v1 on v0

v1 whole, which is shorter than its diff:
```python
import jax
import jax.numpy as jnp
from jax import lax
from jax.sharding import Mesh, PartitionSpec as P

F32, BF16 = jnp.float32, jnp.bfloat16
SWAP = [(0, 1), (1, 0)]
NEAR = [(0, 1), (1, 0), (2, 3), (3, 2)]
WRAP = [(0, 3), (3, 0), (1, 2), (2, 1)]


def shift(d):
    return [(i, (i + d) % 4) for i in range(4)]


def rolled(a, start):
    return lax.dynamic_slice_in_dim(jnp.concatenate([a, a]), start, a.shape[0], 0)


def dot(a, b):
    return jnp.dot(a, b, preferred_element_type=F32)


def columns(a, first):
    return lax.dynamic_slice_in_dim(a, first, 128, 1)


def local(queries, gram, slab, chunks=1):
    zh, y, k, x, zl = (lax.axis_index(n) for n in ("zh", "y", "core", "x", "zl"))
    a1, a2 = ((y + 1) // 2) % 2, y // 2
    b1, b2 = y // 2, y % 2
    order = []
    for half, (p, s, flip) in enumerate(((a1, b1, 0), (a2, b2, 1))):
        for part in (0, 1):
            first = 1 - s if part and flip else s
            for sub in (first, 1 - first):
                order.append(half * 4 + (1 - p if part else p) * 2 + sub)

    def half(a, core):
        return jnp.concatenate([columns(a, core * 1024 + o * 128) for o in order], axis=1)

    rows = rolled(queries.reshape(4, 2, 4, 32, 512), x)
    rows = rolled(rows.transpose(1, 0, 2, 3, 4), zl)
    rows = rolled(rows.transpose(2, 1, 0, 3, 4), zh)
    g_mine, g_other = half(gram, k), half(gram, 1 - k)
    s_mine, s_other = half(slab, k), half(slab, 1 - k)
    g_in = lax.ppermute(g_other, "core", SWAP)
    n = 32 // chunks
    outs = []
    q_in = lax.ppermute(rows, "core", SWAP)
    s_in = lax.ppermute(s_other, "core", SWAP)
    for c in range(chunks):
        q0 = rows[:, :, :, c * n:(c + 1) * n].reshape(32 * n, 512)
        q1 = q_in[:, :, :, c * n:(c + 1) * n].reshape(32 * n, 512)

        def part(lo, hi):
            return dot(q0, g_mine[:, lo:hi]) + dot(q1, g_in[:, lo:hi])

        got_a = lax.ppermute(part(256, 512).astype(BF16), "y", NEAR)
        got_b = lax.ppermute(part(768, 1024).astype(BF16), "y", WRAP)
        keep_a, keep_b = part(0, 256), part(512, 768)
        sum_a, sum_b = keep_a + got_a.astype(F32), keep_b + got_b.astype(F32)
        got_a = lax.ppermute(sum_a[:, 128:].astype(BF16), "y", WRAP)
        got_b = lax.ppermute(sum_b[:, 128:].astype(BF16), "y", NEAR)
        piece = jnp.concatenate([sum_a[:, :128] + got_a.astype(F32), sum_b[:, :128] + got_b.astype(F32)], axis=1)
        piece = piece.reshape(4, 8 * n, 256)
        own = piece[0]
        for d in (1, 2, 3):
            own = own + lax.ppermute(piece[d].astype(BF16), "zh", shift(d)).astype(F32)
        own = own.astype(BF16)
        z = jnp.concatenate([own] + [lax.ppermute(own, "zh", shift(-d)) for d in (1, 2, 3)], axis=0)
        za, zb = z[:, :128], z[:, 128:]
        aa = jnp.concatenate([za, lax.ppermute(za, "y", WRAP)], axis=1)
        bb = jnp.concatenate([zb, lax.ppermute(zb, "y", NEAR)], axis=1)
        images = jnp.concatenate([aa, lax.ppermute(aa, "y", NEAR), bb, lax.ppermute(bb, "y", WRAP)], axis=1)

        def scores(s):
            return lax.dot_general(images, s, (((1,), (1,)), ((), ())), preferred_element_type=F32)

        mine, other = scores(s_mine), scores(s_in)
        sc = mine + lax.ppermute(other, "core", SWAP)
        sc = sc.reshape(4, 4, 2, n, 256).transpose(1, 2, 0, 3, 4)
        own = sc[0]
        for d in (1, 2, 3):
            own = own + lax.ppermute(sc[d].astype(BF16), "x", shift(d)).astype(F32)
        own = own[0] + lax.ppermute(own[1].astype(BF16), "zl", SWAP).astype(F32)
        outs.append(own.astype(BF16))
    out = jnp.stack(outs, axis=1)
    out = rolled(out, (4 - zh) % 4)
    return out.reshape(128, 256)


def solution(mesh):
    fine = Mesh(mesh.devices.reshape(4, 4, 2, 4, 2), ("zh", "y", "core", "x", "zl"))
    rows, cols = ("zh", "y", "core"), ("x", "zl")
    return jax.shard_map(
        local,
        mesh=fine,
        in_specs=(P(None, rows), P(rows, cols), P(rows, cols)),
        out_specs=P(cols, rows),
        check_vma=False,
    )
```

time: 287 us -> 123 us (0.43); the launches traced: 283 us -> 123 us
  blocking collectives: 211 us -> 0 us
  starting transfers between devices: 0.01 us -> 45.9 us
  waiting for transfers between devices: 44.6 us -> 59.7 us
  between operations: 13.4 us -> 0.38 us
  local copies, waits for them, and re-layouts: 1.59 us -> 8.2 us
  matrix products: 11.3 us -> 5.46 us
    psum x1 -> x0, blocking collectives: 211 us -> none  [local(): images = lax.psum(partial_images, 'rows').astype(jnp.bfloat16)]
    ppermute x0 -> x22, waiting for transfers between devices: none -> 59.7 us  [the longest x1 13 us: local(): lax.ppermute(bb, 'y', WRAP)]
    ppermute x0 -> x22, starting transfers between devices: none -> 45.9 us  [the longest x1 12.3 us: local(): s_in = lax.ppermute(s_other, 'core', SWAP)]
    reduce_scatter x1 -> x0, waiting for transfers between devices: 44.6 us -> none  [local(): lax.psum_scatter(partial_scores, 'cols', scatter_dimension=0, tiled=True)]
    dot_general x2 -> x10, matrix products: 11.3 us -> 5.46 us  [the longest x8 3.93 us: dot(): return jnp.dot(a, b, preferred_element_type=F32)]
    unnamed x4 -> x23, local copies, waits for them, and re-layouts: 1.59 us -> 5.46 us
  transfers between devices with their start and end apart: 1 -> 22, of which waited for: 1 -> 15; matrix products, arithmetic and copies ran while one was open for 0% -> 9% of each run, Pallas kernels for 0% -> 0%
where the time goes in v1:
time: 123 us
  waiting for transfers between devices  59.7 us (49%)
  starting transfers between devices  45.9 us (37%)
  local copies, waits for them, and re-layouts  8.2 us (7%)
  matrix products  5.46 us (4%)
  other arithmetic  3.6 us (3%)
    ppermute x1, waiting for transfers between devices, local(): lax.ppermute(bb, 'y', WRAP)  13 us
    ppermute x1, starting transfers between devices, local(): s_in = lax.ppermute(s_other, 'core', SWAP)  12.3 us
    ppermute x1, waiting for transfers between devices, local(): got_a = lax.ppermute(part(256, 512).astype(BF16), 'y', NEAR)  11 us
    ppermute x3, starting transfers between devices, local(): own = own + lax.ppermute(piece[d].astype(BF16), 'zh', shift(d)).astype(F32)  8.96 us
    ppermute x3, waiting for transfers between devices, local(): own = own + lax.ppermute(sc[d].astype(BF16), 'x', shift(d)).astype(F32)  8.63 us
    ppermute x3, starting transfers between devices, local(): lax.ppermute(own, 'zh', shift(-d))  7.9 us
    ppermute x3, waiting for transfers between devices, local(): own = own + lax.ppermute(piece[d].astype(BF16), 'zh', shift(d)).astype(F32)  7.3 us
    ppermute x1, waiting for transfers between devices, local(): got_a = lax.ppermute(sum_a[:, 128:].astype(BF16), 'y', WRAP)  6.44 us
  transfers between devices with their start and end apart: 22, of which 15 were waited for; matrix products, arithmetic and copies ran while one was open for 9% of the time, Pallas kernels for 0%

profile of v1, /device:TPU:1, one launch (start us, length us, event | category | flops | bytes accessed | tf_op | source)
XLA Modules:
  0.0 123.2 jit_solution(15904285122879743434)
XLA Ops:
  0.0 1.6 %fusion.9 = bf16[2,4,4,32,512]{4,3,2,0,1:T(8,128)(2,1)S(1)} fusion(s32[]{:T(128)S(6)} %select_n.99, bf16[4,2,4,32,512]{4,3,2,1,0:T(8,128)(2,1)} %bitcast.67), kind=kLoop, calls=%fused_computation.23 | loop fusion | flops 524288 | bytes 2097156 | tf_op jit(solution)/shard_map/transpose | solution.py:43
  1.6 0.4 fusion.7
  2.0 0.4 fusion.5
  2.4 3.3 %collective-permute-start = (bf16[4,4,2,32,512]{4,3,0,2,1:T(8,128)(2,1)S(1)}, bf16[4,4,2,32,512]{4,3,0,2,1:T(8,128)(2,1)}, u32[]{:S(2)}, u32[]{:S(2)}) collective-permute-start(bf16[4,4,2,32,512]{4,3,0,2,1:T(8,128)(2,1)S(1)} %fusion.5), channel_id=1, source_target_pairs={{0,8},{8,0},{1,9},{9,1},{2,10},{10,2},{3,11},{11,3},{4,12},{12,4},... | collective-permute-start | bytes 3145736 | tf_op jit(solution)/shard_map/ppermute | solution.py:50
  5.7 0.7 dynamic-slice_dynamic-update-slice_fusion.7
  6.5 0.7 dynamic-slice_dynamic-update-slice_fusion.6
  7.2 0.7 dynamic-slice_dynamic-update-slice_fusion.5
  7.9 0.7 dynamic-slice_dynamic-update-slice_fusion.4
  8.6 0.7 dynamic-slice_dynamic-update-slice_fusion.3
  9.3 0.7 dynamic-slice_dynamic-update-slice_fusion.2
  10.0 0.7 dynamic-slice_dynamic-update-slice_fusion.1
  10.7 1.0 constant_dynamic-slice_fusion.1
  11.7 0.7 collective-permute-start.1
  12.5 0.5 fusion.22
  13.0 0.5 fusion.26
  13.5 0.5 fusion.34
  14.0 1.3 %copy.21 = bf16[4,4,2,32,512]{4,3,2,1,0:T(8,128)(2,1)S(1)} copy(bf16[4,4,2,32,512]{4,3,0,2,1:T(8,128)(2,1)} %collective-permute-done) | data formatting | bytes 2097152 | tf_op jit(solution)/shard_map/ppermute | solution.py:50
  15.3 0.5 fusion.2
  15.8 0.1 collective-permute-start.2
  15.9 0.5 fusion.3
  16.4 1.5 %collective-permute-start.4 = (bf16[1024,256]{0,1:T(8,128)(2,1)S(1)}, bf16[1024,256]{0,1:T(8,128)(2,1)S(1)}, u32[]{:S(2)}, u32[]{:S(2)}) collective-permute-start(bf16[1024,256]{0,1:T(8,128)(2,1)S(1)} %fusion.3), channel_id=1, source_target_pairs={{0,48},{48,0},{16,32},{32,16},{1,49},{49,1},{17,33},{33,17},{2,50}... | collective-permute-start | bytes 1572872 | tf_op jit(solution)/shard_map/ppermute | solution.py:60
  17.9 0.5 fusion.30
  18.4 11.0 %collective-permute-done.2 = bf16[1024,256]{0,1:T(8,128)(2,1)S(1)} collective-permute-done((bf16[1024,256]{0,1:T(8,128)(2,1)S(1)}, bf16[1024,256]{0,1:T(8,128)(2,1)S(1)}, u32[]{:S(2)}, u32[]{:S(2)}) %collective-permute-start.2) | collective-permute-done | bytes 524320 | tf_op jit(solution)/shard_map/ppermute | solution.py:59
  29.5 0.5 fusion.1
  30.0 1.1 collective-permute-start.3
  31.1 0.2 collective-permute-done.4
  31.3 0.5 fusion
  31.8 0.1 collective-permute-start.5
  31.9 6.4 %collective-permute-done.3 = bf16[1024,128]{0,1:T(8,128)(2,1)S(1)} collective-permute-done((bf16[1024,128]{0,1:T(8,128)(2,1)S(1)}, bf16[1024,128]{0,1:T(8,128)(2,1)S(1)}, u32[]{:S(2)}, u32[]{:S(2)}) %collective-permute-start.3) | collective-permute-done | bytes 262176 | tf_op jit(solution)/shard_map/ppermute | solution.py:63
  38.4 0.4 collective-permute-done.5
  38.9 0.1 fusion.4
  39.0 5.7 %collective-permute-start.8 = (bf16[256,256]{0,1:T(8,128)(2,1)S(1)}, bf16[256,256]{0,1:T(8,128)(2,1)S(1)}, u32[]{:S(2)}, u32[]{:S(2)}) collective-permute-start(bf16[256,256]{0,1:T(8,128)(2,1)S(1)} %get-tuple-element.33), channel_id=1, source_target_pairs={{0,192},{64,0},{128,64},{192,128},{1,193},{65,1},{129,65},{193,129... | collective-permute-start | bytes 393224 | tf_op jit(solution)/shard_map/ppermute | solution.py:69
  44.7 1.0 collective-permute-start.7
  45.7 2.3 %collective-permute-start.6 = (bf16[256,256]{0,1:T(8,128)(2,1)S(1)}, bf16[256,256]{0,1:T(8,128)(2,1)S(1)}, u32[]{:S(2)}, u32[]{:S(2)}) collective-permute-start(bf16[256,256]{0,1:T(8,128)(2,1)S(1)} %get-tuple-element.32), channel_id=1, source_target_pairs={{0,64},{64,128},{128,192},{192,0},{1,65},{65,129},{129,193},{193,1... | collective-permute-start | bytes 393224 | tf_op jit(solution)/shard_map/ppermute | solution.py:69
  48.1 6.9 %collective-permute-done.8 = bf16[256,256]{0,1:T(8,128)(2,1)S(1)} collective-permute-done((bf16[256,256]{0,1:T(8,128)(2,1)S(1)}, bf16[256,256]{0,1:T(8,128)(2,1)S(1)}, u32[]{:S(2)}, u32[]{:S(2)}) %collective-permute-start.8) | collective-permute-done | bytes 131104 | tf_op jit(solution)/shard_map/ppermute | solution.py:69
  55.0 0.4 collective-permute-done.6
  55.4 0.1 fusion.14
  55.4 1.8 %collective-permute-start.11 = (bf16[256,256]{0,1:T(8,128)(2,1)S(1)}, bf16[256,256]{0,1:T(8,128)(2,1)S(1)}, u32[]{:S(2)}, u32[]{:S(2)}) collective-permute-start(bf16[256,256]{0,1:T(8,128)(2,1)S(1)} %fusion.14), channel_id=1, source_target_pairs={{0,64},{64,128},{128,192},{192,0},{1,65},{65,129},{129,193},{193,1... | collective-permute-start | bytes 393224 | tf_op jit(solution)/shard_map/ppermute | solution.py:71
  57.2 4.7 %collective-permute-start.10 = (bf16[256,256]{0,1:T(8,128)(2,1)S(1)}, bf16[256,256]{0,1:T(8,128)(2,1)S(1)}, u32[]{:S(2)}, u32[]{:S(2)}) collective-permute-start(bf16[256,256]{0,1:T(8,128)(2,1)S(1)} %fusion.14), channel_id=1, source_target_pairs={{0,128},{64,192},{128,0},{192,64},{1,129},{65,193},{129,1},{193,65... | collective-permute-start | bytes 393224 | tf_op jit(solution)/shard_map/ppermute | solution.py:71
  61.9 1.5 %collective-permute-start.9 = (bf16[256,256]{0,1:T(8,128)(2,1)S(1)}, bf16[256,256]{0,1:T(8,128)(2,1)S(1)}, u32[]{:S(2)}, u32[]{:S(2)}) collective-permute-start(bf16[256,256]{0,1:T(8,128)(2,1)S(1)} %fusion.14), channel_id=1, source_target_pairs={{0,192},{64,0},{128,64},{192,128},{1,193},{65,1},{129,65},{193,129... | collective-permute-start | bytes 393224 | tf_op jit(solution)/shard_map/ppermute | solution.py:71
  63.5 2.8 %collective-permute-done.10 = bf16[256,256]{0,1:T(8,128)(2,1)S(1)} collective-permute-done((bf16[256,256]{0,1:T(8,128)(2,1)S(1)}, bf16[256,256]{0,1:T(8,128)(2,1)S(1)}, u32[]{:S(2)}, u32[]{:S(2)}) %collective-permute-start.10) | collective-permute-done | bytes 131104 | tf_op jit(solution)/shard_map/ppermute | solution.py:71
  66.3 0.6 collective-permute-done.9
  66.9 0.1 fusion.47
  67.0 1.4 %collective-permute-start.12 = (bf16[1024,128]{0,1:T(8,128)(2,1)S(1)}, bf16[1024,128]{0,1:T(8,128)(2,1)S(1)}, u32[]{:S(2)}, u32[]{:S(2)}) collective-permute-start(bf16[1024,128]{0,1:T(8,128)(2,1)S(1)} %get-tuple-element.31), channel_id=1, source_target_pairs={{0,48},{48,0},{16,32},{32,16},{1,49},{49,1},{17,33},{33,17},{2,50}... | collective-permute-start | bytes 786440 | tf_op jit(solution)/shard_map/ppermute | solution.py:73
  68.7 0.1 collective-permute-start.14
  68.8 4.9 %collective-permute-done.12 = bf16[1024,128]{0,1:T(8,128)(2,1)S(1)} collective-permute-done((bf16[1024,128]{0,1:T(8,128)(2,1)S(1)}, bf16[1024,128]{0,1:T(8,128)(2,1)S(1)}, u32[]{:S(2)}, u32[]{:S(2)}) %collective-permute-start.12) | collective-permute-done | bytes 262176 | tf_op jit(solution)/shard_map/ppermute | solution.py:73
  73.7 0.1 collective-permute-start.13
  74.0 12.3 %collective-permute-start.16 = (bf16[256,1024]{1,0:T(8,128)(2,1)S(1)}, bf16[256,1024]{1,0:T(8,128)(2,1)S(1)}, u32[]{:S(2)}, u32[]{:S(2)}) collective-permute-start(bf16[256,1024]{1,0:T(8,128)(2,1)S(1)} %dynamic-slice_dynamic-update-slice_fusion.8), channel_id=1, source_target_pairs={{0,8},{8,0},{1,9},{9,1},{2,10},{10,2},{3,11},{11,3},{4,12},{12,4},... | collective-permute-start | bytes 1572872 | tf_op jit(solution)/shard_map/ppermute | solution.py:51
  86.4 1.4 %collective-permute-start.15 = (bf16[1024,256]{0,1:T(8,128)(2,1)S(1)}, bf16[1024,256]{0,1:T(8,128)(2,1)S(1)}, u32[]{:S(2)}, u32[]{:S(2)}) collective-permute-start(bf16[1024,256]{0,1:T(8,128)(2,1)S(1)} %pad_maximum_fusion.3), channel_id=1, source_target_pairs={{0,48},{48,0},{16,32},{32,16},{1,49},{49,1},{17,33},{33,17},{2,50}... | collective-permute-start | bytes 1572872 | tf_op jit(solution)/shard_map/ppermute | solution.py:75
  87.9 13.0 %collective-permute-done.15 = bf16[1024,256]{0,1:T(8,128)(2,1)S(1)} collective-permute-done((bf16[1024,256]{0,1:T(8,128)(2,1)S(1)}, bf16[1024,256]{0,1:T(8,128)(2,1)S(1)}, u32[]{:S(2)}, u32[]{:S(2)}) %collective-permute-start.15) | collective-permute-done | bytes 524320 | tf_op jit(solution)/shard_map/ppermute | solution.py:75
  100.9 0.8 fusion.49
  101.7 1.2 collective-permute-start.17
  102.9 2.3 %collective-permute-done.17 = f32[1024,256]{1,0:T(8,128)S(1)} collective-permute-done((f32[1024,256]{1,0:T(8,128)S(1)}, f32[1024,256]{1,0:T(8,128)S(1)}, u32[]{:S(2)}, u32[]{:S(2)}) %collective-permute-start.17) | collective-permute-done | bytes 1048608 | tf_op jit(solution)/shard_map/ppermute | solution.py:81
  105.2 0.8 convolution_add_fusion.4
  106.0 0.1 convert.22
  106.1 2.6 %collective-permute-start.20 = (bf16[2,4,32,256]{3,2,0,1:T(8,128)(2,1)S(1)}, bf16[2,4,32,256]{3,2,0,1:T(8,128)(2,1)S(1)}, u32[]{:S(2)}, u32[]{:S(2)}) collective-permute-start(bf16[2,4,32,256]{3,2,0,1:T(8,128)(2,1)S(1)} %get-tuple-element.27), channel_id=1, source_target_pairs={{0,6},{2,0},{4,2},{6,4},{1,7},{3,1},{5,3},{7,5},{8,14},{10,8},{12,... | collective-permute-start | bytes 393224 | tf_op jit(solution)/shard_map/ppermute | solution.py:85
  108.7 0.5 collective-permute-start.19
  109.1 0.6 collective-permute-start.18
  109.7 4.1 %collective-permute-done.20 = bf16[2,4,32,256]{3,2,0,1:T(8,128)(2,1)S(1)} collective-permute-done((bf16[2,4,32,256]{3,2,0,1:T(8,128)(2,1)S(1)}, bf16[2,4,32,256]{3,2,0,1:T(8,128)(2,1)S(1)}, u32[]{:S(2)}, u32[]{:S(2)}) %collective-permute-start.20) | collective-permute-done | bytes 131104 | tf_op jit(solution)/shard_map/ppermute | solution.py:85
  113.8 0.7 collective-permute-done.19
  114.5 3.9 %collective-permute-done.18 = bf16[2,4,32,256]{3,2,0,1:T(8,128)(2,1)S(1)} collective-permute-done((bf16[2,4,32,256]{3,2,0,1:T(8,128)(2,1)S(1)}, bf16[2,4,32,256]{3,2,0,1:T(8,128)(2,1)S(1)}, u32[]{:S(2)}, u32[]{:S(2)}) %collective-permute-start.18) | collective-permute-done | bytes 131104 | tf_op jit(solution)/shard_map/ppermute | solution.py:85
  118.5 2.0 %collective-permute-start.21 = (bf16[4,32,256]{2,1,0:T(8,128)(2,1)S(1)}, bf16[4,32,256]{2,1,0:T(8,128)(2,1)S(1)}, u32[]{:S(2)}, u32[]{:S(2)}) collective-permute-start(bf16[4,32,256]{2,1,0:T(8,128)(2,1)S(1)} %fusion.42), channel_id=1, source_target_pairs={{0,1},{1,0},{2,3},{3,2},{4,5},{5,4},{6,7},{7,6},{8,9},{9,8},{10,11... | collective-permute-start | bytes 196616 | tf_op jit(solution)/shard_map/ppermute | solution.py:86
  120.5 2.0 %collective-permute-done.21 = bf16[4,32,256]{2,1,0:T(8,128)(2,1)S(1)} collective-permute-done((bf16[4,32,256]{2,1,0:T(8,128)(2,1)S(1)}, bf16[4,32,256]{2,1,0:T(8,128)(2,1)S(1)}, u32[]{:S(2)}, u32[]{:S(2)}) %collective-permute-start.21) | collective-permute-done | bytes 65568 | tf_op jit(solution)/shard_map/ppermute | solution.py:86
  122.5 0.7 fusion.40
  (39 shorter events, 1.2 us)
Async XLA Ops:
  1.6 4.1 %copy-start = (bf16[512,2048]{1,0:T(8,128)(2,1)S(1)}, bf16[512,2048]{1,0:T(8,128)(2,1)}, u32[]{:S(2)}) copy-start(bf16[512,2048]{1,0:T(8,128)(2,1)} %param.4) | copy-start | bytes 6291460
  2.4 11.6 %collective-permute-start = (bf16[4,4,2,32,512]{4,3,0,2,1:T(8,128)(2,1)S(1)}, bf16[4,4,2,32,512]{4,3,0,2,1:T(8,128)(2,1)}, u32[]{:S(2)}, u32[]{:S(2)}) collective-permute-start(bf16[4,4,2,32,512]{4,3,0,2,1:T(8,128)(2,1)S(1)} %fusion.5), channel_id=1, source_target_pairs={{0,8},{8,0},{1,9},{9,1},{2,10},{10,2},{3,11},{11,3},{4,12},{12,4},... | collective-permute-start | bytes 3145736 | tf_op jit(solution)/shard_map/ppermute | solution.py:50
  11.7 3.6 %collective-permute-start.1 = (bf16[512,1024]{1,0:T(8,128)(2,1)}, bf16[512,1024]{1,0:T(8,128)(2,1)S(1)}, u32[]{:S(2)}, u32[]{:S(2)}) collective-permute-start(bf16[512,1024]{1,0:T(8,128)(2,1)} %get-tuple-element.10), channel_id=1, source_target_pairs={{0,8},{8,0},{1,9},{9,1},{2,10},{10,2},{3,11},{11,3},{4,12},{12,4},... | collective-permute-start | bytes 3145736 | tf_op jit(solution)/shard_map/ppermute | solution.py:47
  15.8 13.6 %collective-permute-start.2 = (bf16[1024,256]{0,1:T(8,128)(2,1)S(1)}, bf16[1024,256]{0,1:T(8,128)(2,1)S(1)}, u32[]{:S(2)}, u32[]{:S(2)}) collective-permute-start(bf16[1024,256]{0,1:T(8,128)(2,1)S(1)} %fusion.2), channel_id=1, source_target_pairs={{0,16},{16,0},{32,48},{48,32},{1,17},{17,1},{33,49},{49,33},{2,18}... | collective-permute-start | bytes 1572872 | tf_op jit(solution)/shard_map/ppermute | solution.py:59
  16.4 14.9 %collective-permute-start.4 = (bf16[1024,256]{0,1:T(8,128)(2,1)S(1)}, bf16[1024,256]{0,1:T(8,128)(2,1)S(1)}, u32[]{:S(2)}, u32[]{:S(2)}) collective-permute-start(bf16[1024,256]{0,1:T(8,128)(2,1)S(1)} %fusion.3), channel_id=1, source_target_pairs={{0,48},{48,0},{16,32},{32,16},{1,49},{49,1},{17,33},{33,17},{2,50}... | collective-permute-start | bytes 1572872 | tf_op jit(solution)/shard_map/ppermute | solution.py:60
  30.0 8.4 %collective-permute-start.3 = (bf16[1024,128]{0,1:T(8,128)(2,1)S(1)}, bf16[1024,128]{0,1:T(8,128)(2,1)S(1)}, u32[]{:S(2)}, u32[]{:S(2)}) collective-permute-start(bf16[1024,128]{0,1:T(8,128)(2,1)S(1)} %slice.171), channel_id=1, source_target_pairs={{0,48},{48,0},{16,32},{32,16},{1,49},{49,1},{17,33},{33,17},{2,50}... | collective-permute-start | bytes 786440 | tf_op jit(solution)/shard_map/ppermute | solution.py:63
  31.8 7.0 %collective-permute-start.5 = (bf16[1024,128]{0,1:T(8,128)(2,1)S(1)}, bf16[1024,128]{0,1:T(8,128)(2,1)S(1)}, u32[]{:S(2)}, u32[]{:S(2)}) collective-permute-start(bf16[1024,128]{0,1:T(8,128)(2,1)S(1)} %slice.170), channel_id=1, source_target_pairs={{0,16},{16,0},{32,48},{48,32},{1,17},{17,1},{33,49},{49,33},{2,18}... | collective-permute-start | bytes 786440 | tf_op jit(solution)/shard_map/ppermute | solution.py:64
  38.4 9.6 %copy-start.1 = (bf16[256,2048]{1,0:T(8,128)(2,1)S(1)}, bf16[256,2048]{1,0:T(8,128)(2,1)}, u32[]{:S(2)}) copy-start(bf16[256,2048]{1,0:T(8,128)(2,1)} %param.5) | copy-start | bytes 3145732
  39.0 15.9 %collective-permute-start.8 = (bf16[256,256]{0,1:T(8,128)(2,1)S(1)}, bf16[256,256]{0,1:T(8,128)(2,1)S(1)}, u32[]{:S(2)}, u32[]{:S(2)}) collective-permute-start(bf16[256,256]{0,1:T(8,128)(2,1)S(1)} %get-tuple-element.33), channel_id=1, source_target_pairs={{0,192},{64,0},{128,64},{192,128},{1,193},{65,1},{129,65},{193,129... | collective-permute-start | bytes 393224 | tf_op jit(solution)/shard_map/ppermute | solution.py:69
  44.7 10.3 %collective-permute-start.7 = (bf16[256,256]{0,1:T(8,128)(2,1)S(1)}, bf16[256,256]{0,1:T(8,128)(2,1)S(1)}, u32[]{:S(2)}, u32[]{:S(2)}) collective-permute-start(bf16[256,256]{0,1:T(8,128)(2,1)S(1)} %get-tuple-element.34), channel_id=1, source_target_pairs={{0,128},{64,192},{128,0},{192,64},{1,129},{65,193},{129,1},{193,65... | collective-permute-start | bytes 393224 | tf_op jit(solution)/shard_map/ppermute | solution.py:69
  45.7 9.6 %collective-permute-start.6 = (bf16[256,256]{0,1:T(8,128)(2,1)S(1)}, bf16[256,256]{0,1:T(8,128)(2,1)S(1)}, u32[]{:S(2)}, u32[]{:S(2)}) collective-permute-start(bf16[256,256]{0,1:T(8,128)(2,1)S(1)} %get-tuple-element.32), channel_id=1, source_target_pairs={{0,64},{64,128},{128,192},{192,0},{1,65},{65,129},{129,193},{193,1... | collective-permute-start | bytes 393224 | tf_op jit(solution)/shard_map/ppermute | solution.py:69
  55.4 8.0 %collective-permute-start.11 = (bf16[256,256]{0,1:T(8,128)(2,1)S(1)}, bf16[256,256]{0,1:T(8,128)(2,1)S(1)}, u32[]{:S(2)}, u32[]{:S(2)}) collective-permute-start(bf16[256,256]{0,1:T(8,128)(2,1)S(1)} %fusion.14), channel_id=1, source_target_pairs={{0,64},{64,128},{128,192},{192,0},{1,65},{65,129},{129,193},{193,1... | collective-permute-start | bytes 393224 | tf_op jit(solution)/shard_map/ppermute | solution.py:71
  57.2 9.1 %collective-permute-start.10 = (bf16[256,256]{0,1:T(8,128)(2,1)S(1)}, bf16[256,256]{0,1:T(8,128)(2,1)S(1)}, u32[]{:S(2)}, u32[]{:S(2)}) collective-permute-start(bf16[256,256]{0,1:T(8,128)(2,1)S(1)} %fusion.14), channel_id=1, source_target_pairs={{0,128},{64,192},{128,0},{192,64},{1,129},{65,193},{129,1},{193,65... | collective-permute-start | bytes 393224 | tf_op jit(solution)/shard_map/ppermute | solution.py:71
  61.9 5.0 %collective-permute-start.9 = (bf16[256,256]{0,1:T(8,128)(2,1)S(1)}, bf16[256,256]{0,1:T(8,128)(2,1)S(1)}, u32[]{:S(2)}, u32[]{:S(2)}) collective-permute-start(bf16[256,256]{0,1:T(8,128)(2,1)S(1)} %fusion.14), channel_id=1, source_target_pairs={{0,192},{64,0},{128,64},{192,128},{1,193},{65,1},{129,65},{193,129... | collective-permute-start | bytes 393224 | tf_op jit(solution)/shard_map/ppermute | solution.py:71
  67.0 6.7 %collective-permute-start.12 = (bf16[1024,128]{0,1:T(8,128)(2,1)S(1)}, bf16[1024,128]{0,1:T(8,128)(2,1)S(1)}, u32[]{:S(2)}, u32[]{:S(2)}) collective-permute-start(bf16[1024,128]{0,1:T(8,128)(2,1)S(1)} %get-tuple-element.31), channel_id=1, source_target_pairs={{0,48},{48,0},{16,32},{32,16},{1,49},{49,1},{17,33},{33,17},{2,50}... | collective-permute-start | bytes 786440 | tf_op jit(solution)/shard_map/ppermute | solution.py:73
  68.7 17.7 %collective-permute-start.14 = (bf16[1024,128]{0,1:T(8,128)(2,1)S(1)}, bf16[1024,128]{0,1:T(8,128)(2,1)S(1)}, u32[]{:S(2)}, u32[]{:S(2)}) collective-permute-start(bf16[1024,128]{0,1:T(8,128)(2,1)S(1)} %get-tuple-element.29), channel_id=1, source_target_pairs={{0,16},{16,0},{32,48},{48,32},{1,17},{17,1},{33,49},{49,33},{2,18}... | collective-permute-start | bytes 786440 | tf_op jit(solution)/shard_map/ppermute | solution.py:74
  73.7 14.1 %collective-permute-start.13 = (bf16[1024,256]{0,1:T(8,128)(2,1)S(1)}, bf16[1024,256]{0,1:T(8,128)(2,1)S(1)}, u32[]{:S(2)}, u32[]{:S(2)}) collective-permute-start(bf16[1024,256]{0,1:T(8,128)(2,1)S(1)} %pad_maximum_fusion.2), channel_id=1, source_target_pairs={{0,16},{16,0},{32,48},{48,32},{1,17},{17,1},{33,49},{49,33},{2,18}... | collective-permute-start | bytes 1572872 | tf_op jit(solution)/shard_map/ppermute | solution.py:75
  74.0 26.9 %collective-permute-start.16 = (bf16[256,1024]{1,0:T(8,128)(2,1)S(1)}, bf16[256,1024]{1,0:T(8,128)(2,1)S(1)}, u32[]{:S(2)}, u32[]{:S(2)}) collective-permute-start(bf16[256,1024]{1,0:T(8,128)(2,1)S(1)} %dynamic-slice_dynamic-update-slice_fusion.8), channel_id=1, source_target_pairs={{0,8},{8,0},{1,9},{9,1},{2,10},{10,2},{3,11},{11,3},{4,12},{12,4},... | collective-permute-start | bytes 1572872 | tf_op jit(solution)/shard_map/ppermute | solution.py:51
  86.4 14.5 %collective-permute-start.15 = (bf16[1024,256]{0,1:T(8,128)(2,1)S(1)}, bf16[1024,256]{0,1:T(8,128)(2,1)S(1)}, u32[]{:S(2)}, u32[]{:S(2)}) collective-permute-start(bf16[1024,256]{0,1:T(8,128)(2,1)S(1)} %pad_maximum_fusion.3), channel_id=1, source_target_pairs={{0,48},{48,0},{16,32},{32,16},{1,49},{49,1},{17,33},{33,17},{2,50}... | collective-permute-start | bytes 1572872 | tf_op jit(solution)/shard_map/ppermute | solution.py:75
  101.7 3.5 %collective-permute-start.17 = (f32[1024,256]{1,0:T(8,128)S(1)}, f32[1024,256]{1,0:T(8,128)S(1)}, u32[]{:S(2)}, u32[]{:S(2)}) collective-permute-start(f32[1024,256]{1,0:T(8,128)S(1)} %fusion.49), channel_id=1, source_target_pairs={{0,8},{8,0},{1,9},{9,1},{2,10},{10,2},{3,11},{11,3},{4,12},{12,4},... | collective-permute-start | bytes 3145736 | tf_op jit(solution)/shard_map/ppermute | solution.py:81
  106.1 7.7 %collective-permute-start.20 = (bf16[2,4,32,256]{3,2,0,1:T(8,128)(2,1)S(1)}, bf16[2,4,32,256]{3,2,0,1:T(8,128)(2,1)S(1)}, u32[]{:S(2)}, u32[]{:S(2)}) collective-permute-start(bf16[2,4,32,256]{3,2,0,1:T(8,128)(2,1)S(1)} %get-tuple-element.27), channel_id=1, source_target_pairs={{0,6},{2,0},{4,2},{6,4},{1,7},{3,1},{5,3},{7,5},{8,14},{10,8},{12,... | collective-permute-start | bytes 393224 | tf_op jit(solution)/shard_map/ppermute | solution.py:85
  108.7 5.9 %collective-permute-start.19 = (bf16[2,4,32,256]{3,2,0,1:T(8,128)(2,1)S(1)}, bf16[2,4,32,256]{3,2,0,1:T(8,128)(2,1)S(1)}, u32[]{:S(2)}, u32[]{:S(2)}) collective-permute-start(bf16[2,4,32,256]{3,2,0,1:T(8,128)(2,1)S(1)} %get-tuple-element.28), channel_id=1, source_target_pairs={{0,4},{2,6},{4,0},{6,2},{1,5},{3,7},{5,1},{7,3},{8,12},{10,14},{12... | collective-permute-start | bytes 393224 | tf_op jit(solution)/shard_map/ppermute | solution.py:85
  109.1 9.2 %collective-permute-start.18 = (bf16[2,4,32,256]{3,2,0,1:T(8,128)(2,1)S(1)}, bf16[2,4,32,256]{3,2,0,1:T(8,128)(2,1)S(1)}, u32[]{:S(2)}, u32[]{:S(2)}) collective-permute-start(bf16[2,4,32,256]{3,2,0,1:T(8,128)(2,1)S(1)} %get-tuple-element.26), channel_id=1, source_target_pairs={{0,2},{2,4},{4,6},{6,0},{1,3},{3,5},{5,7},{7,1},{8,10},{10,12},{12... | collective-permute-start | bytes 393224 | tf_op jit(solution)/shard_map/ppermute | solution.py:85
  118.5 4.1 %collective-permute-start.21 = (bf16[4,32,256]{2,1,0:T(8,128)(2,1)S(1)}, bf16[4,32,256]{2,1,0:T(8,128)(2,1)S(1)}, u32[]{:S(2)}, u32[]{:S(2)}) collective-permute-start(bf16[4,32,256]{2,1,0:T(8,128)(2,1)S(1)} %fusion.42), channel_id=1, source_target_pairs={{0,1},{1,0},{2,3},{3,2},{4,5},{5,4},{6,7},{7,6},{8,9},{9,8},{10,11... | collective-permute-start | bytes 196616 | tf_op jit(solution)/shard_map/ppermute | solution.py:86

commit v2 on v0

v2 whole, which is shorter than its diff:
```python
import jax
import jax.numpy as jnp
from jax import lax
from jax.sharding import Mesh, PartitionSpec as P

F32, BF16 = jnp.float32, jnp.bfloat16
AXES = ("zh", "y", "core", "x", "zl")
CHUNKS = 2
SWAP = [(0, 1), (1, 0)]
NEAR = [(0, 1), (1, 0), (2, 3), (3, 2)]
WRAP = [(0, 3), (3, 0), (1, 2), (2, 1)]


def by_core(first, second):
    return [(2 * s, 2 * d) for s, d in first] + [(2 * s + 1, 2 * d + 1) for s, d in second]


STEP1, STEP2 = by_core(NEAR, WRAP), by_core(WRAP, NEAR)


def dot(a, b):
    return jnp.dot(a, b, preferred_element_type=F32)


def dot_t(a, b):
    return lax.dot_general(a, b, (((1,), (1,)), ((), ())), preferred_element_type=F32)


def cut(a, i, size):
    return lax.dynamic_slice_in_dim(a, i * size, size, 1)


def local(queries, gram, slab):
    y, k = lax.axis_index("y"), lax.axis_index("core")
    p = jnp.where(k == 0, ((y + 1) // 2) % 2, y // 2)
    s = jnp.where(k == 0, y // 2, y % 2)
    t = jnp.where(k == 0, s, 1 - s)
    n = 512 // CHUNKS
    r = 64 // CHUNKS

    g_in = lax.ppermute(gram, "core", SWAP)
    rows = queries.reshape(8, 2, CHUNKS, r, 512)

    def for_core(core):
        picked = lax.dynamic_index_in_dim(rows, core, 1, keepdims=False)
        return picked.transpose(1, 0, 2, 3).reshape(CHUNKS, n, 512)

    q_mine = for_core(k)
    q_in = lax.ppermute(for_core(1 - k), "core", SWAP)
    s_in = lax.ppermute(slab, "core", SWAP)
    both = jnp.where(k == 0, jnp.concatenate([slab, s_in]), jnp.concatenate([s_in, slab]))
    s_cut = [cut(both, i, 512) for i in (2 * p + s, 2 * p + 1 - s, 2 * (1 - p) + t, 2 * (1 - p) + 1 - t)]
    outs = []
    for c in range(CHUNKS):
        part = dot(q_mine[c], gram) + dot(q_in[c], g_in)
        got = lax.ppermute(cut(part, 1 - p, 1024).astype(BF16), ("y", "core"), STEP1)
        part = cut(part, p, 1024) + got.astype(F32)
        got = lax.ppermute(cut(part, 1 - s, 512).astype(BF16), ("y", "core"), STEP2)
        piece = cut(part, s, 512) + got.astype(F32)
        piece = piece + lax.ppermute(piece.astype(BF16), ("zh", "core"), STEP1).astype(F32)
        piece = piece + lax.ppermute(piece.astype(BF16), ("zh", "core"), STEP2).astype(F32)
        i0 = piece.astype(BF16)
        i1 = lax.ppermute(i0, ("y", "core"), STEP2)
        i23 = lax.ppermute(jnp.concatenate([i0, i1], axis=1), ("y", "core"), STEP1)
        images = (i0, i1, i23[:, :512], i23[:, 512:])
        sc = sum(dot_t(i, b) for i, b in zip(images, s_cut))
        sc = sc.astype(BF16).reshape(8, r, 2, 256).transpose(2, 0, 1, 3).reshape(16, r, 256)
        sc = lax.all_to_all(sc, ("core", "x", "zl"), 0, 0, tiled=True)
        outs.append(sc.reshape(2, 8, r, 256).astype(F32).sum(axis=1).astype(BF16))
    return jnp.stack(outs, axis=1).reshape(128, 256)


def solution(mesh):
    fine = Mesh(mesh.devices.reshape(4, 4, 2, 4, 2), AXES)
    rows, cols = ("zh", "y", "core"), ("x", "zl")
    return jax.shard_map(
        local,
        mesh=fine,
        in_specs=(P(None, rows), P(rows, cols), P(rows, cols)),
        out_specs=P(cols, rows),
        check_vma=False,
    )
```

time: 287 us -> 101 us (0.35); the launches traced: 283 us -> 101 us
  blocking collectives: 211 us -> 0 us
  starting transfers between devices: 0.01 us -> 38.5 us
  between operations: 13.4 us -> 0.31 us
  other arithmetic: 1.54 us -> 8.96 us
  waiting for transfers between devices: 44.6 us -> 38.1 us
  local copies, waits for them, and re-layouts: 1.59 us -> 5.34 us
    psum x1 -> x0, blocking collectives: 211 us -> none  [local(): images = lax.psum(partial_images, 'rows').astype(jnp.bfloat16)]
    reduce_scatter x1 -> x0, waiting for transfers between devices: 44.6 us -> none  [local(): lax.psum_scatter(partial_scores, 'cols', scatter_dimension=0, tiled=True)]
    ppermute x0 -> x15, waiting for transfers between devices: none -> 28.8 us  [the longest x2 8.34 us: local(): lax.ppermute(piece.astype(BF16), ('zh', 'core'), STEP2).astype(F32)]
    ppermute x0 -> x15, starting transfers between devices: none -> 26.4 us  [the longest x2 7.96 us: local(): lax.ppermute(piece.astype(BF16), ('zh', 'core'), STEP1).astype(F32)]
    all_to_all x0 -> x2, starting transfers between devices: none -> 12.1 us  [local(): sc = lax.all_to_all(sc, ('core', 'x', 'zl'), 0, 0, tiled=True)]
    all_to_all x0 -> x2, waiting for transfers between devices: none -> 9.37 us  [local(): sc = lax.all_to_all(sc, ('core', 'x', 'zl'), 0, 0, tiled=True)]
    dot_general x2 -> x12, matrix products: 11.3 us -> 9.36 us  [the longest x4 4.71 us: dot(): return jnp.dot(a, b, preferred_element_type=F32)]
  transfers between devices with their start and end apart: 1 -> 17, of which waited for: 1 -> 10; matrix products, arithmetic and copies ran while one was open for 0% -> 21% of each run, Pallas kernels for 0% -> 0%
where the time goes in v2:
time: 101 us
  starting transfers between devices  38.5 us (38%)
  waiting for transfers between devices  38.1 us (38%)
  matrix products  9.36 us (9%)
  other arithmetic  8.96 us (9%)
  local copies, waits for them, and re-layouts  5.34 us (5%)
    all_to_all x2, starting transfers between devices, local(): sc = lax.all_to_all(sc, ('core', 'x', 'zl'), 0, 0, tiled=True)  12.1 us
    all_to_all x2, waiting for transfers between devices, local(): sc = lax.all_to_all(sc, ('core', 'x', 'zl'), 0, 0, tiled=True)  9.37 us
    ppermute x2, waiting for transfers between devices, local(): lax.ppermute(piece.astype(BF16), ('zh', 'core'), STEP2).astype(F32)  8.34 us
    ppermute x2, waiting for transfers between devices, local(): lax.ppermute(cut(part, 1 - p, 1024).astype(BF16), ('y', 'core'), STEP1)  8.23 us
    ppermute x2, starting transfers between devices, local(): lax.ppermute(piece.astype(BF16), ('zh', 'core'), STEP1).astype(F32)  7.96 us
    ppermute x2, waiting for transfers between devices, local(): i23 = lax.ppermute(jnp.concatenate([i0, i1], axis=1), ('y', 'core'), STEP1)  6.5 us
    ppermute x2, starting transfers between devices, local(): lax.ppermute(piece.astype(BF16), ('zh', 'core'), STEP2).astype(F32)  6.14 us
    dot_general x4, matrix products, dot(): return jnp.dot(a, b, preferred_element_type=F32)  4.71 us
  transfers between devices with their start and end apart: 17, of which 10 were waited for; matrix products, arithmetic and copies ran while one was open for 21% of the time, Pallas kernels for 0%

profile of v2, /device:TPU:1, one launch (start us, length us, event | category | flops | bytes accessed | tf_op | source)
XLA Modules:
  0.0 100.6 jit_solution(11298401275335578613)
XLA Ops:
  0.0 3.2 %collective-permute-start.1 = (bf16[512,2048]{1,0:T(8,128)(2,1)}, bf16[512,2048]{1,0:T(8,128)(2,1)S(1)}, u32[]{:S(2)}, u32[]{:S(2)}) collective-permute-start(bf16[512,2048]{1,0:T(8,128)(2,1)} %param.4), channel_id=1, source_target_pairs={{0,8},{8,0},{1,9},{9,1},{2,10},{10,2},{3,11},{11,3},{4,12},{12,4},... | collective-permute-start | bytes 6291464 | tf_op jit(solution)/shard_map/ppermute | solution.py:41
  3.2 1.3 %constant_dynamic-slice_fusion = (bf16[8,1,2,32,512]{4,3,2,1,0:T(8,128)(2,1)S(1)}, bf16[2,8,32,512]{3,2,0,1:T(8,128)(2,1)S(1)}) fusion(bf16[8,2,2,32,512]{4,3,2,1,0:T(8,128)(2,1)} %bitcast.43, s32[]{:T(128)S(6)} %select_n.72, s32[]{:T(128)S(6)} %select_n.71), kind=kLoop, calls=%fused_computation.61 | loop fusion | bytes 2097160 | tf_op jit(solution)/shard_map/jit(dynamic_index_in_dim)/dynamic_slice | solution.py:45
  4.5 0.8 copy.7
  5.4 0.0 collective-permute-start
  5.4 0.0 copy-start
  5.4 2.4 %fusion.37 = f32[256,2048]{1,0:T(8,128)S(1)} fusion(bf16[256,512]{1,0:T(8,128)(2,1)S(1)} %bitcast.42, bf16[512,2048]{1,0:T(8,128)(2,1)} %param.4), kind=kOutput, calls=%fused_computation.63 | convolution fusion | flops 536870912 | bytes 4456448 | tf_op jit(solution)/shard_map/dot_general | solution.py:22
  7.9 0.7 fusion.38
  8.6 0.0 collective-permute-done
  8.7 0.8 convolution_add_fusion.1
  9.4 0.1 dynamic-slice_convert_fusion.1
  9.5 1.1 %collective-permute-start.2 = (bf16[256,1024]{1,0:T(8,128)(2,1)S(1)}, bf16[256,1024]{1,0:T(8,128)(2,1)}, u32[]{:S(2)}, u32[]{:S(2)}) collective-permute-start(bf16[256,1024]{1,0:T(8,128)(2,1)S(1)} %dynamic-slice_convert_fusion.1), channel_id=1, source_target_pairs={{0,16},{16,0},{32,48},{48,32},{8,56},{56,8},{24,40},{40,24},{1,17}... | collective-permute-start | bytes 1572872 | tf_op jit(solution)/shard_map/ppermute | solution.py:56
  10.6 0.8 convolution_add_fusion
  11.4 1.3 %copy-done.1 = f32[256,2048]{1,0:T(8,128)} copy-done((f32[256,2048]{1,0:T(8,128)}, f32[256,2048]{1,0:T(8,128)S(1)}, u32[]{:S(2)}) %copy-start.1) | copy-done | bytes 2097176
  12.7 0.1 dynamic-slice_convert_fusion
  12.8 1.8 %collective-permute-start.9 = (bf16[256,1024]{1,0:T(8,128)(2,1)S(1)}, bf16[256,1024]{1,0:T(8,128)(2,1)S(1)}, u32[]{:S(2)}, u32[]{:S(2)}) collective-permute-start(bf16[256,1024]{1,0:T(8,128)(2,1)S(1)} %dynamic-slice_convert_fusion), channel_id=1, source_target_pairs={{0,16},{16,0},{32,48},{48,32},{8,56},{56,8},{24,40},{40,24},{1,17}... | collective-permute-start | bytes 1572872 | tf_op jit(solution)/shard_map/ppermute | solution.py:56
  14.6 4.4 %collective-permute-done.2 = bf16[256,1024]{1,0:T(8,128)(2,1)} collective-permute-done((bf16[256,1024]{1,0:T(8,128)(2,1)S(1)}, bf16[256,1024]{1,0:T(8,128)(2,1)}, u32[]{:S(2)}, u32[]{:S(2)}) %collective-permute-start.2) | collective-permute-done | bytes 524320 | tf_op jit(solution)/shard_map/ppermute | solution.py:56
  19.0 1.5 %convert_add_fusion.1 = f32[256,1024]{1,0:T(8,128)S(1)} fusion(bf16[256,1024]{1,0:T(8,128)(2,1)} %collective-permute-done.2, f32[256,2048]{1,0:T(8,128)} %copy-done.3, s32[]{:T(128)S(6)} %select_n.77), kind=kLoop, calls=%fused_computation.13 | loop fusion | flops 524288 | bytes 2621444 | tf_op jit(solution)/shard_map/add | solution.py:57
  20.5 0.1 collective-permute-start.3
  20.6 3.8 %collective-permute-done.9 = bf16[256,1024]{1,0:T(8,128)(2,1)S(1)} collective-permute-done((bf16[256,1024]{1,0:T(8,128)(2,1)S(1)}, bf16[256,1024]{1,0:T(8,128)(2,1)S(1)}, u32[]{:S(2)}, u32[]{:S(2)}) %collective-permute-start.9) | collective-permute-done | bytes 524320 | tf_op jit(solution)/shard_map/ppermute | solution.py:56
  24.5 0.2 convert_add_fusion
  24.7 0.1 collective-permute-start.10
  24.8 2.5 %collective-permute-done.3 = bf16[256,512]{1,0:T(8,128)(2,1)S(1)} collective-permute-done((bf16[256,512]{1,0:T(8,128)(2,1)S(1)}, bf16[256,512]{1,0:T(8,128)(2,1)S(1)}, u32[]{:S(2)}, u32[]{:S(2)}) %collective-permute-start.3) | collective-permute-done | bytes 262176 | tf_op jit(solution)/shard_map/ppermute | solution.py:58
  27.3 0.1 fusion.26
  27.4 4.4 %collective-permute-start.4 = (bf16[256,512]{1,0:T(8,128)(2,1)S(1)}, bf16[256,512]{1,0:T(8,128)(2,1)S(1)}, u32[]{:S(2)}, u32[]{:S(2)}) collective-permute-start(bf16[256,512]{1,0:T(8,128)(2,1)S(1)} %fusion.26), channel_id=1, source_target_pairs={{0,64},{64,0},{128,192},{192,128},{8,200},{200,8},{72,136},{136,72... | collective-permute-start | bytes 786440 | tf_op jit(solution)/shard_map/ppermute | solution.py:60
  31.8 0.1 fusion.27
  31.9 3.6 %collective-permute-start.11 = (bf16[256,512]{1,0:T(8,128)(2,1)S(1)}, bf16[256,512]{1,0:T(8,128)(2,1)S(1)}, u32[]{:S(2)}, u32[]{:S(2)}) collective-permute-start(bf16[256,512]{1,0:T(8,128)(2,1)S(1)} %fusion.27), channel_id=1, source_target_pairs={{0,64},{64,0},{128,192},{192,128},{8,200},{200,8},{72,136},{136,72... | collective-permute-start | bytes 786440 | tf_op jit(solution)/shard_map/ppermute | solution.py:60
  35.4 2.8 %collective-permute-done.4 = bf16[256,512]{1,0:T(8,128)(2,1)S(1)} collective-permute-done((bf16[256,512]{1,0:T(8,128)(2,1)S(1)}, bf16[256,512]{1,0:T(8,128)(2,1)S(1)}, u32[]{:S(2)}, u32[]{:S(2)}) %collective-permute-start.4) | collective-permute-done | bytes 262176 | tf_op jit(solution)/shard_map/ppermute | solution.py:60
  38.3 0.8 fusion.20
  39.1 4.1 %collective-permute-start.5 = (bf16[256,512]{1,0:T(8,128)(2,1)}, bf16[256,512]{1,0:T(8,128)(2,1)}, u32[]{:S(2)}, u32[]{:S(2)}) collective-permute-start(bf16[256,512]{1,0:T(8,128)(2,1)} %fusion.20), channel_id=1, source_target_pairs={{0,192},{192,0},{64,128},{128,64},{8,72},{72,8},{136,200},{200,136... | collective-permute-start | bytes 786440 | tf_op jit(solution)/shard_map/ppermute | solution.py:61
  43.2 0.3 collective-permute-done.11
  43.5 0.1 fusion.21
  43.6 2.0 %collective-permute-start.12 = (bf16[256,512]{1,0:T(8,128)(2,1)S(1)}, bf16[256,512]{1,0:T(8,128)(2,1)}, u32[]{:S(2)}, u32[]{:S(2)}) collective-permute-start(bf16[256,512]{1,0:T(8,128)(2,1)S(1)} %fusion.21), channel_id=1, source_target_pairs={{0,192},{192,0},{64,128},{128,64},{8,72},{72,8},{136,200},{200,136... | collective-permute-start | bytes 786440 | tf_op jit(solution)/shard_map/ppermute | solution.py:61
  45.7 3.0 %collective-permute-done.5 = bf16[256,512]{1,0:T(8,128)(2,1)} collective-permute-done((bf16[256,512]{1,0:T(8,128)(2,1)}, bf16[256,512]{1,0:T(8,128)(2,1)}, u32[]{:S(2)}, u32[]{:S(2)}) %collective-permute-start.5) | collective-permute-done | bytes 262176 | tf_op jit(solution)/shard_map/ppermute | solution.py:61
  48.7 1.1 %add_convert_fusion.1 = bf16[256,512]{1,0:T(8,128)(2,1)S(1)} fusion(bf16[256,512]{1,0:T(8,128)(2,1)} %collective-permute-done.5, bf16[256,512]{1,0:T(8,128)(2,1)S(1)} %collective-permute-done.4, bf16[256,512]{1,0:T(8,128)(2,1)S(1)} %collective-permute-done.3, f32[256,1024]{1,0:T(8,128)S(1)} %convert_add_fusion.1, s32[]{:T(128)S(6)} %select_n.81), kind=kLoop, calls=%fused_computation.21 | loop fusion | flops 917504 | bytes 1572868 | tf_op jit(solution)/shard_map/convert_element_type | solution.py:62
  49.8 0.9 collective-permute-start.7
  50.7 5.3 %collective-permute-done.12 = bf16[256,512]{1,0:T(8,128)(2,1)} collective-permute-done((bf16[256,512]{1,0:T(8,128)(2,1)S(1)}, bf16[256,512]{1,0:T(8,128)(2,1)}, u32[]{:S(2)}, u32[]{:S(2)}) %collective-permute-start.12) | collective-permute-done | bytes 262176 | tf_op jit(solution)/shard_map/ppermute | solution.py:61
  56.0 1.1 %add_convert_fusion = bf16[256,512]{1,0:T(8,128)(2,1)S(1)} fusion(bf16[256,512]{1,0:T(8,128)(2,1)} %collective-permute-done.12, bf16[256,512]{1,0:T(8,128)(2,1)S(1)} %collective-permute-done.11, bf16[256,512]{1,0:T(8,128)(2,1)S(1)} %collective-permute-done.10, f32[256,1024]{1,0:T(8,128)S(1)} %convert_add_fusion, s32[]{:T(128)S(6)} %select_n.81), kind=kLoop, calls=%fused_computation.17 | loop fusion | flops 917504 | bytes 1572868 | tf_op jit(solution)/shard_map/convert_element_type | solution.py:62
  57.1 0.8 collective-permute-start.13
  57.9 2.4 %maximum_select_fusion = bf16[512,2048]{1,0:T(8,128)(2,1)S(1)} fusion(bf16[256,2048]{1,0:T(8,128)(2,1)} %collective-permute-done.6, bf16[256,2048]{1,0:T(8,128)(2,1)S(1)} %copy-done.4, pred[]{:T(512)S(6)} %eq.5), kind=kLoop, calls=%fused_computation.2 | loop fusion | flops 9437184 | bytes 4194305 | tf_op jit(solution)/shard_map/jit(_where)/select_n | solution.py:51
  60.4 0.0 collective-permute-done.7
  60.4 0.1 pad_maximum_fusion
  60.4 2.9 %collective-permute-start.8 = (bf16[256,1024]{1,0:T(8,128)(2,1)S(1)}, bf16[256,1024]{1,0:T(8,128)(2,1)S(1)}, u32[]{:S(2)}, u32[]{:S(2)}) collective-permute-start(bf16[256,1024]{1,0:T(8,128)(2,1)S(1)} %pad_maximum_fusion), channel_id=1, source_target_pairs={{0,16},{16,0},{32,48},{48,32},{8,56},{56,8},{24,40},{40,24},{1,17}... | collective-permute-start | bytes 1572872 | tf_op jit(solution)/shard_map/ppermute | solution.py:64
  63.4 0.0 collective-permute-done.13
  63.4 0.9 pad_maximum_fusion.1
  64.2 1.3 %collective-permute-start.14 = (bf16[256,1024]{1,0:T(8,128)(2,1)}, bf16[256,1024]{1,0:T(8,128)(2,1)}, u32[]{:S(2)}, u32[]{:S(2)}) collective-permute-start(bf16[256,1024]{1,0:T(8,128)(2,1)} %pad_maximum_fusion.1), channel_id=1, source_target_pairs={{0,16},{16,0},{32,48},{48,32},{8,56},{56,8},{24,40},{40,24},{1,17}... | collective-permute-start | bytes 1572872 | tf_op jit(solution)/shard_map/ppermute | solution.py:64
  65.6 0.3 fusion.16
  65.9 0.3 fusion.14
  66.3 6.5 %collective-permute-done.8 = bf16[256,1024]{1,0:T(8,128)(2,1)S(1)} collective-permute-done((bf16[256,1024]{1,0:T(8,128)(2,1)S(1)}, bf16[256,1024]{1,0:T(8,128)(2,1)S(1)}, u32[]{:S(2)}, u32[]{:S(2)}) %collective-permute-start.8) | collective-permute-done | bytes 524320 | tf_op jit(solution)/shard_map/ppermute | solution.py:64
  72.8 0.3 fusion.12
  73.1 0.3 fusion.8
  73.4 0.4 fusion.4
  73.8 0.1 reshape.34
  73.9 0.8 copy.5
  74.6 7.2 %all-to-all-start = ((bf16[16,32,256]{2,1,0:T(8,128)(2,1)}), bf16[16,32,256]{2,1,0:T(8,128)(2,1)S(1)}, u32[]{:S(2)}, u32[]{:S(2)}) async-start(bf16[16,32,256]{2,1,0:T(8,128)(2,1)} %bitcast.9), calls=%async_computation | async-start | bytes 524288 | tf_op jit(solution)/shard_map/all_to_all | solution.py:68
  81.9 0.0 collective-permute-done.14
  81.9 1.3 %fusion.10 = f32[256,512]{1,0:T(8,128)S(1)} fusion(bf16[512,2048]{1,0:T(8,128)(2,1)S(1)} %maximum_select_fusion, s32[]{:T(128)S(6)} %select_n.88, bf16[256,1024]{1,0:T(8,128)(2,1)} %collective-permute-done.14), kind=kOutput, calls=%fused_computation.30 | convolution fusion | flops 134217728 | bytes 1310724 | tf_op jit(solution)/shard_map/dot_general | solution.py:26
  83.2 1.3 %fusion.6 = f32[256,512]{1,0:T(8,128)S(1)} fusion(bf16[512,2048]{1,0:T(8,128)(2,1)S(1)} %maximum_select_fusion, s32[]{:T(128)S(6)} %select_n.89, bf16[256,1024]{1,0:T(8,128)(2,1)} %collective-permute-done.14), kind=kOutput, calls=%fused_computation.26 | convolution fusion | flops 134217728 | bytes 1310724 | tf_op jit(solution)/shard_map/dot_general | solution.py:26
  84.5 0.3 fusion.5
  84.8 0.1 reshape.37
  84.9 0.7 copy.6
  85.6 2.8 %all-to-all-done = bf16[16,32,256]{2,1,0:T(8,128)(2,1)S(1)} async-done(((bf16[16,32,256]{2,1,0:T(8,128)(2,1)}), bf16[16,32,256]{2,1,0:T(8,128)(2,1)S(1)}, u32[]{:S(2)}, u32[]{:S(2)}) %all-to-all-start) | async-done | bytes 262176 | tf_op jit(solution)/shard_map/all_to_all | solution.py:68
  88.5 4.9 %all-to-all-start.1 = ((bf16[16,32,256]{2,1,0:T(8,128)(2,1)}), bf16[16,32,256]{2,1,0:T(8,128)(2,1)S(1)}, u32[]{:S(2)}, u32[]{:S(2)}) async-start(bf16[16,32,256]{2,1,0:T(8,128)(2,1)} %bitcast.16), calls=%async_computation.1 | async-start | bytes 524288 | tf_op jit(solution)/shard_map/all_to_all | solution.py:68
  93.4 6.6 %all-to-all-done.1 = bf16[16,32,256]{2,1,0:T(8,128)(2,1)S(1)} async-done(((bf16[16,32,256]{2,1,0:T(8,128)(2,1)}), bf16[16,32,256]{2,1,0:T(8,128)(2,1)S(1)}, u32[]{:S(2)}, u32[]{:S(2)}) %all-to-all-start.1) | async-done | bytes 262176 | tf_op jit(solution)/shard_map/all_to_all | solution.py:68
  100.0 0.6 pad_maximum_fusion.2
  (17 shorter events, 0.2 us)
Async XLA Ops:
  0.0 8.6 %collective-permute-start.1 = (bf16[512,2048]{1,0:T(8,128)(2,1)}, bf16[512,2048]{1,0:T(8,128)(2,1)S(1)}, u32[]{:S(2)}, u32[]{:S(2)}) collective-permute-start(bf16[512,2048]{1,0:T(8,128)(2,1)} %param.4), channel_id=1, source_target_pairs={{0,8},{8,0},{1,9},{9,1},{2,10},{10,2},{3,11},{11,3},{4,12},{12,4},... | collective-permute-start | bytes 6291464 | tf_op jit(solution)/shard_map/ppermute | solution.py:41
  5.4 3.3 %collective-permute-start = (bf16[2,256,512]{2,1,0:T(8,128)(2,1)}, bf16[2,256,512]{2,1,0:T(8,128)(2,1)S(1)}, u32[]{:S(2)}, u32[]{:S(2)}) collective-permute-start(bf16[2,256,512]{2,1,0:T(8,128)(2,1)} %bitcast.6), channel_id=1, source_target_pairs={{0,8},{8,0},{1,9},{9,1},{2,10},{10,2},{3,11},{11,3},{4,12},{12,4},... | collective-permute-start | bytes 1572872 | tf_op jit(solution)/shard_map/ppermute | solution.py:49
  5.4 2.5 %copy-start = (bf16[512,2048]{1,0:T(8,128)(2,1)S(1)}, bf16[512,2048]{1,0:T(8,128)(2,1)}, u32[]{:S(2)}) copy-start(bf16[512,2048]{1,0:T(8,128)(2,1)} %param.4) | copy-start | bytes 6291460
  9.4 1.9 %copy-start.3 = (f32[256,2048]{1,0:T(8,128)}, f32[256,2048]{1,0:T(8,128)S(1)}, u32[]{:S(2)}) copy-start(f32[256,2048]{1,0:T(8,128)S(1)} %convolution_add_fusion.1) | copy-start | bytes 6291460
  9.5 9.4 %collective-permute-start.2 = (bf16[256,1024]{1,0:T(8,128)(2,1)S(1)}, bf16[256,1024]{1,0:T(8,128)(2,1)}, u32[]{:S(2)}, u32[]{:S(2)}) collective-permute-start(bf16[256,1024]{1,0:T(8,128)(2,1)S(1)} %dynamic-slice_convert_fusion.1), channel_id=1, source_target_pairs={{0,16},{16,0},{32,48},{48,32},{8,56},{56,8},{24,40},{40,24},{1,17}... | collective-permute-start | bytes 1572872 | tf_op jit(solution)/shard_map/ppermute | solution.py:56
  11.4 1.3 %copy-start.1 = (f32[256,2048]{1,0:T(8,128)}, f32[256,2048]{1,0:T(8,128)S(1)}, u32[]{:S(2)}) copy-start(f32[256,2048]{1,0:T(8,128)S(1)} %convolution_add_fusion) | copy-start | bytes 6291460
  12.8 11.7 %collective-permute-start.9 = (bf16[256,1024]{1,0:T(8,128)(2,1)S(1)}, bf16[256,1024]{1,0:T(8,128)(2,1)S(1)}, u32[]{:S(2)}, u32[]{:S(2)}) collective-permute-start(bf16[256,1024]{1,0:T(8,128)(2,1)S(1)} %dynamic-slice_convert_fusion), channel_id=1, source_target_pairs={{0,16},{16,0},{32,48},{48,32},{8,56},{56,8},{24,40},{40,24},{1,17}... | collective-permute-start | bytes 1572872 | tf_op jit(solution)/shard_map/ppermute | solution.py:56
  14.6 9.9 %copy-start.2 = (f32[256,2048]{1,0:T(8,128)S(1)}, f32[256,2048]{1,0:T(8,128)}, u32[]{:S(2)}) copy-start(f32[256,2048]{1,0:T(8,128)} %copy-done.1) | copy-start | bytes 6291460
  20.5 6.8 %collective-permute-start.3 = (bf16[256,512]{1,0:T(8,128)(2,1)S(1)}, bf16[256,512]{1,0:T(8,128)(2,1)S(1)}, u32[]{:S(2)}, u32[]{:S(2)}) collective-permute-start(bf16[256,512]{1,0:T(8,128)(2,1)S(1)} %dynamic-slice_convert_fusion.3), channel_id=1, source_target_pairs={{0,48},{48,0},{16,32},{32,16},{8,24},{24,8},{40,56},{56,40},{1,49}... | collective-permute-start | bytes 786440 | tf_op jit(solution)/shard_map/ppermute | solution.py:58
  24.7 7.1 %collective-permute-start.10 = (bf16[256,512]{1,0:T(8,128)(2,1)S(1)}, bf16[256,512]{1,0:T(8,128)(2,1)S(1)}, u32[]{:S(2)}, u32[]{:S(2)}) collective-permute-start(bf16[256,512]{1,0:T(8,128)(2,1)S(1)} %dynamic-slice_convert_fusion.2), channel_id=1, source_target_pairs={{0,48},{48,0},{16,32},{32,16},{8,24},{24,8},{40,56},{56,40},{1,49}... | collective-permute-start | bytes 786440 | tf_op jit(solution)/shard_map/ppermute | solution.py:58
  27.4 10.9 %collective-permute-start.4 = (bf16[256,512]{1,0:T(8,128)(2,1)S(1)}, bf16[256,512]{1,0:T(8,128)(2,1)S(1)}, u32[]{:S(2)}, u32[]{:S(2)}) collective-permute-start(bf16[256,512]{1,0:T(8,128)(2,1)S(1)} %fusion.26), channel_id=1, source_target_pairs={{0,64},{64,0},{128,192},{192,128},{8,200},{200,8},{72,136},{136,72... | collective-permute-start | bytes 786440 | tf_op jit(solution)/shard_map/ppermute | solution.py:60
  31.8 26.2 %collective-permute-start.6 = (bf16[256,2048]{1,0:T(8,128)(2,1)}, bf16[256,2048]{1,0:T(8,128)(2,1)}, u32[]{:S(2)}, u32[]{:S(2)}) collective-permute-start(bf16[256,2048]{1,0:T(8,128)(2,1)} %param.5), channel_id=1, source_target_pairs={{0,8},{8,0},{1,9},{9,1},{2,10},{10,2},{3,11},{11,3},{4,12},{12,4},... | collective-permute-start | bytes 3145736 | tf_op jit(solution)/shard_map/ppermute | solution.py:50
  31.9 11.7 %collective-permute-start.11 = (bf16[256,512]{1,0:T(8,128)(2,1)S(1)}, bf16[256,512]{1,0:T(8,128)(2,1)S(1)}, u32[]{:S(2)}, u32[]{:S(2)}) collective-permute-start(bf16[256,512]{1,0:T(8,128)(2,1)S(1)} %fusion.27), channel_id=1, source_target_pairs={{0,64},{64,0},{128,192},{192,128},{8,200},{200,8},{72,136},{136,72... | collective-permute-start | bytes 786440 | tf_op jit(solution)/shard_map/ppermute | solution.py:60
  39.1 9.6 %collective-permute-start.5 = (bf16[256,512]{1,0:T(8,128)(2,1)}, bf16[256,512]{1,0:T(8,128)(2,1)}, u32[]{:S(2)}, u32[]{:S(2)}) collective-permute-start(bf16[256,512]{1,0:T(8,128)(2,1)} %fusion.20), channel_id=1, source_target_pairs={{0,192},{192,0},{64,128},{128,64},{8,72},{72,8},{136,200},{200,136... | collective-permute-start | bytes 786440 | tf_op jit(solution)/shard_map/ppermute | solution.py:61
  43.6 12.4 %collective-permute-start.12 = (bf16[256,512]{1,0:T(8,128)(2,1)S(1)}, bf16[256,512]{1,0:T(8,128)(2,1)}, u32[]{:S(2)}, u32[]{:S(2)}) collective-permute-start(bf16[256,512]{1,0:T(8,128)(2,1)S(1)} %fusion.21), channel_id=1, source_target_pairs={{0,192},{192,0},{64,128},{128,64},{8,72},{72,8},{136,200},{200,136... | collective-permute-start | bytes 786440 | tf_op jit(solution)/shard_map/ppermute | solution.py:61
  45.7 12.3 %copy-start.4 = (bf16[256,2048]{1,0:T(8,128)(2,1)S(1)}, bf16[256,2048]{1,0:T(8,128)(2,1)}, u32[]{:S(2)}) copy-start(bf16[256,2048]{1,0:T(8,128)(2,1)} %param.5) | copy-start | bytes 3145732
  49.8 10.6 %collective-permute-start.7 = (bf16[256,512]{1,0:T(8,128)(2,1)S(1)}, bf16[256,512]{1,0:T(8,128)(2,1)S(1)}, u32[]{:S(2)}, u32[]{:S(2)}) collective-permute-start(bf16[256,512]{1,0:T(8,128)(2,1)S(1)} %add_convert_fusion.1), channel_id=1, source_target_pairs={{0,48},{48,0},{16,32},{32,16},{8,24},{24,8},{40,56},{56,40},{1,49}... | collective-permute-start | bytes 786440 | tf_op jit(solution)/shard_map/ppermute | solution.py:63
  57.1 6.3 %collective-permute-start.13 = (bf16[256,512]{1,0:T(8,128)(2,1)S(1)}, bf16[256,512]{1,0:T(8,128)(2,1)S(1)}, u32[]{:S(2)}, u32[]{:S(2)}) collective-permute-start(bf16[256,512]{1,0:T(8,128)(2,1)S(1)} %add_convert_fusion), channel_id=1, source_target_pairs={{0,48},{48,0},{16,32},{32,16},{8,24},{24,8},{40,56},{56,40},{1,49}... | collective-permute-start | bytes 786440 | tf_op jit(solution)/shard_map/ppermute | solution.py:63
  60.4 12.3 %collective-permute-start.8 = (bf16[256,1024]{1,0:T(8,128)(2,1)S(1)}, bf16[256,1024]{1,0:T(8,128)(2,1)S(1)}, u32[]{:S(2)}, u32[]{:S(2)}) collective-permute-start(bf16[256,1024]{1,0:T(8,128)(2,1)S(1)} %pad_maximum_fusion), channel_id=1, source_target_pairs={{0,16},{16,0},{32,48},{48,32},{8,56},{56,8},{24,40},{40,24},{1,17}... | collective-permute-start | bytes 1572872 | tf_op jit(solution)/shard_map/ppermute | solution.py:64
  64.2 17.7 %collective-permute-start.14 = (bf16[256,1024]{1,0:T(8,128)(2,1)}, bf16[256,1024]{1,0:T(8,128)(2,1)}, u32[]{:S(2)}, u32[]{:S(2)}) collective-permute-start(bf16[256,1024]{1,0:T(8,128)(2,1)} %pad_maximum_fusion.1), channel_id=1, source_target_pairs={{0,16},{16,0},{32,48},{48,32},{8,56},{56,8},{24,40},{40,24},{1,17}... | collective-permute-start | bytes 1572872 | tf_op jit(solution)/shard_map/ppermute | solution.py:64
  74.6 13.8 %all-to-all-start = ((bf16[16,32,256]{2,1,0:T(8,128)(2,1)}), bf16[16,32,256]{2,1,0:T(8,128)(2,1)S(1)}, u32[]{:S(2)}, u32[]{:S(2)}) async-start(bf16[16,32,256]{2,1,0:T(8,128)(2,1)} %bitcast.9), calls=%async_computation | async-start | bytes 524288 | tf_op jit(solution)/shard_map/all_to_all | solution.py:68
  88.5 11.5 %all-to-all-start.1 = ((bf16[16,32,256]{2,1,0:T(8,128)(2,1)}), bf16[16,32,256]{2,1,0:T(8,128)(2,1)S(1)}, u32[]{:S(2)}, u32[]{:S(2)}) async-start(bf16[16,32,256]{2,1,0:T(8,128)(2,1)} %bitcast.16), calls=%async_computation.1 | async-start | bytes 524288 | tf_op jit(solution)/shard_map/all_to_all | solution.py:68

commit v3 on v2

--- a/solution.py
+++ b/solution.py
@@ -34,7 +34,6 @@
     y, k = lax.axis_index("y"), lax.axis_index("core")
     p = jnp.where(k == 0, ((y + 1) // 2) % 2, y // 2)
     s = jnp.where(k == 0, y // 2, y % 2)
-    t = jnp.where(k == 0, s, 1 - s)
     n = 512 // CHUNKS
     r = 64 // CHUNKS
 
@@ -49,25 +48,26 @@
     q_in = lax.ppermute(for_core(1 - k), "core", SWAP)
     s_in = lax.ppermute(slab, "core", SWAP)
     both = jnp.where(k == 0, jnp.concatenate([slab, s_in]), jnp.concatenate([s_in, slab]))
-    s_cut = [cut(both, i, 512) for i in (2 * p + s, 2 * p + 1 - s, 2 * (1 - p) + t, 2 * (1 - p) + 1 - t)]
+    s_kept, s_other = cut(both, p, 1024), cut(both, 1 - p, 1024)
     outs = []
     for c in range(CHUNKS):
         part = dot(q_mine[c], gram) + dot(q_in[c], g_in)
         got = lax.ppermute(cut(part, 1 - p, 1024).astype(BF16), ("y", "core"), STEP1)
         part = cut(part, p, 1024) + got.astype(F32)
-        got = lax.ppermute(cut(part, 1 - s, 512).astype(BF16), ("y", "core"), STEP2)
+        second = cut(part, 1 - s, 512).astype(BF16)
+        got = lax.ppermute(second, ("y", "core"), STEP2)
         piece = cut(part, s, 512) + got.astype(F32)
         piece = piece + lax.ppermute(piece.astype(BF16), ("zh", "core"), STEP1).astype(F32)
         piece = piece + lax.ppermute(piece.astype(BF16), ("zh", "core"), STEP2).astype(F32)
         i0 = piece.astype(BF16)
         i1 = lax.ppermute(i0, ("y", "core"), STEP2)
-        i23 = lax.ppermute(jnp.concatenate([i0, i1], axis=1), ("y", "core"), STEP1)
-        images = (i0, i1, i23[:, :512], i23[:, 512:])
-        sc = sum(dot_t(i, b) for i, b in zip(images, s_cut))
-        sc = sc.astype(BF16).reshape(8, r, 2, 256).transpose(2, 0, 1, 3).reshape(16, r, 256)
-        sc = lax.all_to_all(sc, ("core", "x", "zl"), 0, 0, tiled=True)
-        outs.append(sc.reshape(2, 8, r, 256).astype(F32).sum(axis=1).astype(BF16))
-    return jnp.stack(outs, axis=1).reshape(128, 256)
+        kept = jnp.where(s == 0, jnp.concatenate([i0, i1], axis=1), jnp.concatenate([i1, i0], axis=1))
+        other = lax.ppermute(kept, ("y", "core"), STEP1)
+        sc = dot_t(kept, s_kept) + dot_t(other, s_other)
+        outs.append(sc.astype(BF16).reshape(8, r, 2, 256).transpose(2, 0, 1, 3))
+    sc = jnp.stack(outs, axis=2).reshape(16, 64, 256)
+    sc = lax.all_to_all(sc, ("core", "x", "zl"), 0, 0, tiled=True)
+    return sc.reshape(2, 8, 64, 256).astype(F32).sum(axis=1).astype(BF16).reshape(128, 256)
 
 
 def solution(mesh):

time: 101 us -> 96.2 us (0.952)
  blocking collectives: 0 us -> 17.8 us
  starting transfers between devices: 38.5 us -> 27.6 us
  waiting for transfers between devices: 38.1 us -> 32.2 us
  other arithmetic: 8.96 us -> 6.48 us
  matrix products: 9.36 us -> 7.68 us
  local copies, waits for them, and re-layouts: 5.34 us -> 3.95 us
    all_to_all x0 -> x1, blocking collectives: none -> 17.8 us  [local(): sc = lax.all_to_all(sc, ('core', 'x', 'zl'), 0, 0, tiled=True)]
    all_to_all x2 -> x0, starting transfers between devices: 12.1 us -> none  [local(): sc = lax.all_to_all(sc, ('core', 'x', 'zl'), 0, 0, tiled=True)]
    all_to_all x2 -> x0, waiting for transfers between devices: 9.37 us -> none  [local(): sc = lax.all_to_all(sc, ('core', 'x', 'zl'), 0, 0, tiled=True)]
    convert_element_type x2, other arithmetic: 2.18 us -> 0.28 us  [local(): i0 = piece.astype(BF16)]
    ppermute x2, waiting for transfers between devices: 3.17 us -> 4.9 us  [local(): lax.ppermute(piece.astype(BF16), ('zh', 'core'), STEP1).astype(F32)]
    dot_general x8 -> x4, matrix products: 4.65 us -> 2.97 us  [dot_t(): lax.dot_general(a, b, (((1,), (1,)), ((), ())), preferred_element_type=F32)]
    ppermute x4, starting transfers between devices: 4.44 us -> 5.99 us  [the longest x2 5.81 us: local(): other = lax.ppermute(kept, ('y', 'core'), STEP1)]
    reshape x4 -> x2, local copies, waits for them, and re-layouts: 1.63 us -> 0.13 us  [local(): outs.append(sc.astype(BF16).reshape(8, r, 2, 256).transpose(2, 0, 1, 3))]
  transfers between devices with their start and end apart: 17 -> 15, of which waited for: 10 -> 10; matrix products, arithmetic and copies ran while one was open for 21% -> 14% of each run, Pallas kernels for 0% -> 0%
where the time goes in v3:
time: 96.2 us; the launch traced here: 96 us
  waiting for transfers between devices  32.2 us (33%)
  starting transfers between devices  27.6 us (29%)
  blocking collectives  17.8 us (19%)
  matrix products  7.68 us (8%)
  other arithmetic  6.48 us (7%)
  local copies, waits for them, and re-layouts  3.95 us (4%)
    all_to_all x1, blocking collectives, local(): sc = lax.all_to_all(sc, ('core', 'x', 'zl'), 0, 0, tiled=True)  17.8 us
    ppermute x2, waiting for transfers between devices, local(): lax.ppermute(piece.astype(BF16), ('zh', 'core'), STEP2).astype(F32)  8.78 us
    ppermute x2, waiting for transfers between devices, local(): lax.ppermute(cut(part, 1 - p, 1024).astype(BF16), ('y', 'core'), STEP1)  8.22 us
    ppermute x2, starting transfers between devices, local(): lax.ppermute(piece.astype(BF16), ('zh', 'core'), STEP1).astype(F32)  7.04 us
    ppermute x2, waiting for transfers between devices, local(): other = lax.ppermute(kept, ('y', 'core'), STEP1)  6.3 us
    ppermute x2, starting transfers between devices, local(): lax.ppermute(piece.astype(BF16), ('zh', 'core'), STEP2).astype(F32)  6.27 us
    ppermute x2, starting transfers between devices, local(): other = lax.ppermute(kept, ('y', 'core'), STEP1)  5.81 us
    ppermute x2, waiting for transfers between devices, local(): lax.ppermute(piece.astype(BF16), ('zh', 'core'), STEP1).astype(F32)  4.9 us
  transfers between devices with their start and end apart: 15, of which 10 were waited for; matrix products, arithmetic and copies ran while one was open for 14% of the time, Pallas kernels for 0%

profile of v3, /device:TPU:1, one launch (start us, length us, event | category | flops | bytes accessed | tf_op | source)
XLA Modules:
  0.0 96.0 jit_solution(6290146859951985543)
XLA Ops:
  0.0 3.2 %collective-permute-start.1 = (bf16[512,2048]{1,0:T(8,128)(2,1)}, bf16[512,2048]{1,0:T(8,128)(2,1)S(1)}, u32[]{:S(2)}, u32[]{:S(2)}) collective-permute-start(bf16[512,2048]{1,0:T(8,128)(2,1)} %param.4), channel_id=1, source_target_pairs={{0,8},{8,0},{1,9},{9,1},{2,10},{10,2},{3,11},{11,3},{4,12},{12,4},... | collective-permute-start | bytes 6291464 | tf_op jit(solution)/shard_map/ppermute | solution.py:40
  3.2 1.3 %constant_dynamic-slice_fusion = (bf16[8,1,2,32,512]{4,3,2,1,0:T(8,128)(2,1)S(1)}, bf16[2,8,32,512]{3,2,0,1:T(8,128)(2,1)S(1)}) fusion(bf16[8,2,2,32,512]{4,3,2,1,0:T(8,128)(2,1)} %bitcast.43, s32[]{:T(128)S(6)} %select_n.75, s32[]{:T(128)S(6)} %select_n.74), kind=kLoop, calls=%fused_computation.42 | loop fusion | bytes 2097160 | tf_op jit(solution)/shard_map/jit(dynamic_index_in_dim)/dynamic_slice | solution.py:44
  4.5 0.8 copy.7
  5.4 0.0 collective-permute-start
  5.4 0.0 copy-start
  5.4 2.4 %fusion.17 = f32[256,2048]{1,0:T(8,128)S(1)} fusion(bf16[256,512]{1,0:T(8,128)(2,1)S(1)} %bitcast.42, bf16[512,2048]{1,0:T(8,128)(2,1)} %param.4), kind=kOutput, calls=%fused_computation.44 | convolution fusion | flops 536870912 | bytes 4456448 | tf_op jit(solution)/shard_map/dot_general | solution.py:22
  7.9 0.7 fusion.18
  8.6 0.0 collective-permute-done
  8.6 0.0 collective-permute-done.1
  8.7 0.8 convolution_add_fusion.1
  9.4 0.1 dynamic-slice_convert_fusion.1
  9.5 1.1 %collective-permute-start.2 = (bf16[256,1024]{1,0:T(8,128)(2,1)S(1)}, bf16[256,1024]{1,0:T(8,128)(2,1)}, u32[]{:S(2)}, u32[]{:S(2)}) collective-permute-start(bf16[256,1024]{1,0:T(8,128)(2,1)S(1)} %dynamic-slice_convert_fusion.1), channel_id=1, source_target_pairs={{0,16},{16,0},{32,48},{48,32},{8,56},{56,8},{24,40},{40,24},{1,17}... | collective-permute-start | bytes 1572872 | tf_op jit(solution)/shard_map/ppermute | solution.py:55
  10.6 0.8 convolution_add_fusion
  11.4 0.0 copy-done.3
  11.4 0.0 copy-start.1
  11.4 1.3 %copy-done.1 = f32[256,2048]{1,0:T(8,128)} copy-done((f32[256,2048]{1,0:T(8,128)}, f32[256,2048]{1,0:T(8,128)S(1)}, u32[]{:S(2)}) %copy-start.1) | copy-done | bytes 2097176
  12.7 0.1 dynamic-slice_convert_fusion
  12.8 1.8 %collective-permute-start.9 = (bf16[256,1024]{1,0:T(8,128)(2,1)S(1)}, bf16[256,1024]{1,0:T(8,128)(2,1)S(1)}, u32[]{:S(2)}, u32[]{:S(2)}) collective-permute-start(bf16[256,1024]{1,0:T(8,128)(2,1)S(1)} %dynamic-slice_convert_fusion), channel_id=1, source_target_pairs={{0,16},{16,0},{32,48},{48,32},{8,56},{56,8},{24,40},{40,24},{1,17}... | collective-permute-start | bytes 1572872 | tf_op jit(solution)/shard_map/ppermute | solution.py:55
  14.6 4.4 %collective-permute-done.2 = bf16[256,1024]{1,0:T(8,128)(2,1)} collective-permute-done((bf16[256,1024]{1,0:T(8,128)(2,1)S(1)}, bf16[256,1024]{1,0:T(8,128)(2,1)}, u32[]{:S(2)}, u32[]{:S(2)}) %collective-permute-start.2) | collective-permute-done | bytes 524320 | tf_op jit(solution)/shard_map/ppermute | solution.py:55
  19.0 1.5 %convert_add_fusion.1 = f32[256,1024]{1,0:T(8,128)S(1)} fusion(bf16[256,1024]{1,0:T(8,128)(2,1)} %collective-permute-done.2, f32[256,2048]{1,0:T(8,128)} %copy-done.3, s32[]{:T(128)S(6)} %select_n.79), kind=kLoop, calls=%fused_computation.9 | loop fusion | flops 524288 | bytes 2621444 | tf_op jit(solution)/shard_map/add | solution.py:56
  20.5 0.1 collective-permute-start.3
  20.6 3.8 %collective-permute-done.9 = bf16[256,1024]{1,0:T(8,128)(2,1)S(1)} collective-permute-done((bf16[256,1024]{1,0:T(8,128)(2,1)S(1)}, bf16[256,1024]{1,0:T(8,128)(2,1)S(1)}, u32[]{:S(2)}, u32[]{:S(2)}) %collective-permute-start.9) | collective-permute-done | bytes 524320 | tf_op jit(solution)/shard_map/ppermute | solution.py:55
  24.5 0.0 copy-done.2
  24.5 0.2 convert_add_fusion
  24.7 0.1 collective-permute-start.10
  24.8 2.5 %collective-permute-done.3 = bf16[256,512]{1,0:T(8,128)(2,1)S(1)} collective-permute-done((bf16[256,512]{1,0:T(8,128)(2,1)S(1)}, bf16[256,512]{1,0:T(8,128)(2,1)S(1)}, u32[]{:S(2)}, u32[]{:S(2)}) %collective-permute-start.3) | collective-permute-done | bytes 262176 | tf_op jit(solution)/shard_map/ppermute | solution.py:58
  27.3 0.1 fusion.10
  27.4 4.4 %collective-permute-start.4 = (bf16[256,512]{1,0:T(8,128)(2,1)S(1)}, bf16[256,512]{1,0:T(8,128)(2,1)S(1)}, u32[]{:S(2)}, u32[]{:S(2)}) collective-permute-start(bf16[256,512]{1,0:T(8,128)(2,1)S(1)} %fusion.10), channel_id=1, source_target_pairs={{0,64},{64,0},{128,192},{192,128},{8,200},{200,8},{72,136},{136,72... | collective-permute-start | bytes 786440 | tf_op jit(solution)/shard_map/ppermute | solution.py:60
  31.8 0.0 collective-permute-done.10
  31.8 0.1 fusion.11
  31.9 2.7 %collective-permute-start.11 = (bf16[256,512]{1,0:T(8,128)(2,1)S(1)}, bf16[256,512]{1,0:T(8,128)(2,1)S(1)}, u32[]{:S(2)}, u32[]{:S(2)}) collective-permute-start(bf16[256,512]{1,0:T(8,128)(2,1)S(1)} %fusion.11), channel_id=1, source_target_pairs={{0,64},{64,0},{128,192},{192,128},{8,200},{200,8},{72,136},{136,72... | collective-permute-start | bytes 786440 | tf_op jit(solution)/shard_map/ppermute | solution.py:60
  34.5 3.7 %collective-permute-done.4 = bf16[256,512]{1,0:T(8,128)(2,1)S(1)} collective-permute-done((bf16[256,512]{1,0:T(8,128)(2,1)S(1)}, bf16[256,512]{1,0:T(8,128)(2,1)S(1)}, u32[]{:S(2)}, u32[]{:S(2)}) %collective-permute-start.4) | collective-permute-done | bytes 262176 | tf_op jit(solution)/shard_map/ppermute | solution.py:60
  38.3 0.1 fusion.8
  38.4 4.2 %collective-permute-start.5 = (bf16[256,512]{1,0:T(8,128)(2,1)S(1)}, bf16[256,512]{1,0:T(8,128)(2,1)S(1)}, u32[]{:S(2)}, u32[]{:S(2)}) collective-permute-start(bf16[256,512]{1,0:T(8,128)(2,1)S(1)} %fusion.8), channel_id=1, source_target_pairs={{0,192},{192,0},{64,128},{128,64},{8,72},{72,8},{136,200},{200,136... | collective-permute-start | bytes 786440 | tf_op jit(solution)/shard_map/ppermute | solution.py:61
  42.6 0.0 collective-permute-start.7
  42.6 1.2 %collective-permute-done.11 = bf16[256,512]{1,0:T(8,128)(2,1)S(1)} collective-permute-done((bf16[256,512]{1,0:T(8,128)(2,1)S(1)}, bf16[256,512]{1,0:T(8,128)(2,1)S(1)}, u32[]{:S(2)}, u32[]{:S(2)}) %collective-permute-start.11) | collective-permute-done | bytes 262176 | tf_op jit(solution)/shard_map/ppermute | solution.py:60
  43.7 0.1 fusion.9
  43.9 2.1 %collective-permute-start.12 = (bf16[256,512]{1,0:T(8,128)(2,1)S(1)}, bf16[256,512]{1,0:T(8,128)(2,1)S(1)}, u32[]{:S(2)}, u32[]{:S(2)}) collective-permute-start(bf16[256,512]{1,0:T(8,128)(2,1)S(1)} %fusion.9), channel_id=1, source_target_pairs={{0,192},{192,0},{64,128},{128,64},{8,72},{72,8},{136,200},{200,136... | collective-permute-start | bytes 786440 | tf_op jit(solution)/shard_map/ppermute | solution.py:61
  45.9 3.1 %collective-permute-done.5 = bf16[256,512]{1,0:T(8,128)(2,1)S(1)} collective-permute-done((bf16[256,512]{1,0:T(8,128)(2,1)S(1)}, bf16[256,512]{1,0:T(8,128)(2,1)S(1)}, u32[]{:S(2)}, u32[]{:S(2)}) %collective-permute-start.5) | collective-permute-done | bytes 262176 | tf_op jit(solution)/shard_map/ppermute | solution.py:61
  49.0 0.1 add_convert_fusion.1
  49.2 0.6 collective-permute-start.6
  49.8 5.7 %collective-permute-done.12 = bf16[256,512]{1,0:T(8,128)(2,1)S(1)} collective-permute-done((bf16[256,512]{1,0:T(8,128)(2,1)S(1)}, bf16[256,512]{1,0:T(8,128)(2,1)S(1)}, u32[]{:S(2)}, u32[]{:S(2)}) %collective-permute-start.12) | collective-permute-done | bytes 262176 | tf_op jit(solution)/shard_map/ppermute | solution.py:61
  55.4 0.1 add_convert_fusion
  55.6 1.6 %collective-permute-start.13 = (bf16[256,512]{1,0:T(8,128)(2,1)S(1)}, bf16[256,512]{1,0:T(8,128)(2,1)S(1)}, u32[]{:S(2)}, u32[]{:S(2)}) collective-permute-start(bf16[256,512]{1,0:T(8,128)(2,1)S(1)} %add_convert_fusion), channel_id=1, source_target_pairs={{0,48},{48,0},{16,32},{32,16},{8,24},{24,8},{40,56},{56,40},{1,49}... | collective-permute-start | bytes 786440 | tf_op jit(solution)/shard_map/ppermute | solution.py:63
  57.2 0.0 collective-permute-done.6
  57.2 0.1 maximum_select_fusion.1
  57.3 2.4 %collective-permute-start.8 = (bf16[256,1024]{1,0:T(8,128)(2,1)S(1)}, bf16[256,1024]{1,0:T(8,128)(2,1)S(1)}, u32[]{:S(2)}, u32[]{:S(2)}) collective-permute-start(bf16[256,1024]{1,0:T(8,128)(2,1)S(1)} %maximum_select_fusion.1), channel_id=1, source_target_pairs={{0,16},{16,0},{32,48},{48,32},{8,56},{56,8},{24,40},{40,24},{1,17}... | collective-permute-start | bytes 1572872 | tf_op jit(solution)/shard_map/ppermute | solution.py:65
  59.8 1.5 %collective-permute-done.13 = bf16[256,512]{1,0:T(8,128)(2,1)S(1)} collective-permute-done((bf16[256,512]{1,0:T(8,128)(2,1)S(1)}, bf16[256,512]{1,0:T(8,128)(2,1)S(1)}, u32[]{:S(2)}, u32[]{:S(2)}) %collective-permute-start.13) | collective-permute-done | bytes 262176 | tf_op jit(solution)/shard_map/ppermute | solution.py:63
  61.2 0.1 maximum_select_fusion.2
  61.4 3.4 %collective-permute-start.14 = (bf16[256,1024]{1,0:T(8,128)(2,1)S(1)}, bf16[256,1024]{1,0:T(8,128)(2,1)}, u32[]{:S(2)}, u32[]{:S(2)}) collective-permute-start(bf16[256,1024]{1,0:T(8,128)(2,1)S(1)} %maximum_select_fusion.2), channel_id=1, source_target_pairs={{0,16},{16,0},{32,48},{48,32},{8,56},{56,8},{24,40},{40,24},{1,17}... | collective-permute-start | bytes 1572872 | tf_op jit(solution)/shard_map/ppermute | solution.py:65
  64.7 0.0 collective-permute-done.7
  64.7 3.1 %maximum_select_fusion = bf16[512,2048]{1,0:T(8,128)(2,1)S(1)} fusion(bf16[256,2048]{1,0:T(8,128)(2,1)} %collective-permute-done.7, bf16[256,2048]{1,0:T(8,128)(2,1)} %param.5, pred[]{:T(512)S(6)} %eq.12), kind=kLoop, calls=%fused_computation.2 | loop fusion | flops 9437184 | bytes 4194305 | tf_op jit(solution)/shard_map/jit(_where)/select_n | solution.py:50
  67.9 1.6 %collective-permute-done.8 = bf16[256,1024]{1,0:T(8,128)(2,1)S(1)} collective-permute-done((bf16[256,1024]{1,0:T(8,128)(2,1)S(1)}, bf16[256,1024]{1,0:T(8,128)(2,1)S(1)}, u32[]{:S(2)}, u32[]{:S(2)}) %collective-permute-start.8) | collective-permute-done | bytes 524320 | tf_op jit(solution)/shard_map/ppermute | solution.py:65
  69.5 0.5 fusion.4
  70.0 0.5 fusion
  70.5 0.1 reshape.28
  70.5 4.7 %collective-permute-done.14 = bf16[256,1024]{1,0:T(8,128)(2,1)} collective-permute-done((bf16[256,1024]{1,0:T(8,128)(2,1)S(1)}, bf16[256,1024]{1,0:T(8,128)(2,1)}, u32[]{:S(2)}, u32[]{:S(2)}) %collective-permute-start.14) | collective-permute-done | bytes 524320 | tf_op jit(solution)/shard_map/ppermute | solution.py:65
  75.2 1.5 %fusion.2 = f32[256,512]{1,0:T(8,128)S(1)} fusion(bf16[256,1024]{1,0:T(8,128)(2,1)} %collective-permute-done.14, bf16[512,2048]{1,0:T(8,128)(2,1)S(1)} %maximum_select_fusion, s32[]{:T(128)S(6)} %select_n.80), kind=kOutput, calls=%fused_computation.11 | convolution fusion | flops 268435456 | bytes 2097156 | tf_op jit(solution)/shard_map/dot_general | solution.py:26
  76.7 0.5 fusion.1
  77.2 0.1 reshape.29
  77.3 0.1 copy_bitcast_fusion
  77.4 0.1 pad_maximum_fusion
  77.5 17.8 %all_to_all.5 = bf16[16,64,256]{2,1,0:T(8,128)(2,1)S(1)} all-to-all(bf16[16,64,256]{2,1,0:T(8,128)(2,1)S(1)} %bitcast.40), channel_id=1, replica_groups=mesh['zh'=4,'y'=4,'core'=2,'x'=4,'zl'=2] {'core','x','zl'}, dimensions={0} | all-to-all | bytes 1048576 | tf_op jit(solution)/shard_map/all_to_all | solution.py:69
  95.3 0.7 bitcast_reduce_fusion
  (6 shorter events, 0.1 us)
Async XLA Ops:
  0.0 8.7 %collective-permute-start.1 = (bf16[512,2048]{1,0:T(8,128)(2,1)}, bf16[512,2048]{1,0:T(8,128)(2,1)S(1)}, u32[]{:S(2)}, u32[]{:S(2)}) collective-permute-start(bf16[512,2048]{1,0:T(8,128)(2,1)} %param.4), channel_id=1, source_target_pairs={{0,8},{8,0},{1,9},{9,1},{2,10},{10,2},{3,11},{11,3},{4,12},{12,4},... | collective-permute-start | bytes 6291464 | tf_op jit(solution)/shard_map/ppermute | solution.py:40
  5.4 3.3 %collective-permute-start = (bf16[2,256,512]{2,1,0:T(8,128)(2,1)}, bf16[2,256,512]{2,1,0:T(8,128)(2,1)S(1)}, u32[]{:S(2)}, u32[]{:S(2)}) collective-permute-start(bf16[2,256,512]{2,1,0:T(8,128)(2,1)} %bitcast.6), channel_id=1, source_target_pairs={{0,8},{8,0},{1,9},{9,1},{2,10},{10,2},{3,11},{11,3},{4,12},{12,4},... | collective-permute-start | bytes 1572872 | tf_op jit(solution)/shard_map/ppermute | solution.py:48
  5.4 2.5 %copy-start = (bf16[512,2048]{1,0:T(8,128)(2,1)S(1)}, bf16[512,2048]{1,0:T(8,128)(2,1)}, u32[]{:S(2)}) copy-start(bf16[512,2048]{1,0:T(8,128)(2,1)} %param.4) | copy-start | bytes 6291460
  9.4 1.9 %copy-start.3 = (f32[256,2048]{1,0:T(8,128)}, f32[256,2048]{1,0:T(8,128)S(1)}, u32[]{:S(2)}) copy-start(f32[256,2048]{1,0:T(8,128)S(1)} %convolution_add_fusion.1) | copy-start | bytes 6291460
  9.5 9.4 %collective-permute-start.2 = (bf16[256,1024]{1,0:T(8,128)(2,1)S(1)}, bf16[256,1024]{1,0:T(8,128)(2,1)}, u32[]{:S(2)}, u32[]{:S(2)}) collective-permute-start(bf16[256,1024]{1,0:T(8,128)(2,1)S(1)} %dynamic-slice_convert_fusion.1), channel_id=1, source_target_pairs={{0,16},{16,0},{32,48},{48,32},{8,56},{56,8},{24,40},{40,24},{1,17}... | collective-permute-start | bytes 1572872 | tf_op jit(solution)/shard_map/ppermute | solution.py:55
  11.4 1.3 %copy-start.1 = (f32[256,2048]{1,0:T(8,128)}, f32[256,2048]{1,0:T(8,128)S(1)}, u32[]{:S(2)}) copy-start(f32[256,2048]{1,0:T(8,128)S(1)} %convolution_add_fusion) | copy-start | bytes 6291460
  12.8 11.7 %collective-permute-start.9 = (bf16[256,1024]{1,0:T(8,128)(2,1)S(1)}, bf16[256,1024]{1,0:T(8,128)(2,1)S(1)}, u32[]{:S(2)}, u32[]{:S(2)}) collective-permute-start(bf16[256,1024]{1,0:T(8,128)(2,1)S(1)} %dynamic-slice_convert_fusion), channel_id=1, source_target_pairs={{0,16},{16,0},{32,48},{48,32},{8,56},{56,8},{24,40},{40,24},{1,17}... | collective-permute-start | bytes 1572872 | tf_op jit(solution)/shard_map/ppermute | solution.py:55
  14.6 9.9 %copy-start.2 = (f32[256,2048]{1,0:T(8,128)S(1)}, f32[256,2048]{1,0:T(8,128)}, u32[]{:S(2)}) copy-start(f32[256,2048]{1,0:T(8,128)} %copy-done.1) | copy-start | bytes 6291460
  20.5 6.8 %collective-permute-start.3 = (bf16[256,512]{1,0:T(8,128)(2,1)S(1)}, bf16[256,512]{1,0:T(8,128)(2,1)S(1)}, u32[]{:S(2)}, u32[]{:S(2)}) collective-permute-start(bf16[256,512]{1,0:T(8,128)(2,1)S(1)} %dynamic-slice_convert_fusion.3), channel_id=1, source_target_pairs={{0,48},{48,0},{16,32},{32,16},{8,24},{24,8},{40,56},{56,40},{1,49}... | collective-permute-start | bytes 786440 | tf_op jit(solution)/shard_map/ppermute | solution.py:58
  24.7 7.1 %collective-permute-start.10 = (bf16[256,512]{1,0:T(8,128)(2,1)S(1)}, bf16[256,512]{1,0:T(8,128)(2,1)S(1)}, u32[]{:S(2)}, u32[]{:S(2)}) collective-permute-start(bf16[256,512]{1,0:T(8,128)(2,1)S(1)} %dynamic-slice_convert_fusion.2), channel_id=1, source_target_pairs={{0,48},{48,0},{16,32},{32,16},{8,24},{24,8},{40,56},{56,40},{1,49}... | collective-permute-start | bytes 786440 | tf_op jit(solution)/shard_map/ppermute | solution.py:58
  27.4 10.9 %collective-permute-start.4 = (bf16[256,512]{1,0:T(8,128)(2,1)S(1)}, bf16[256,512]{1,0:T(8,128)(2,1)S(1)}, u32[]{:S(2)}, u32[]{:S(2)}) collective-permute-start(bf16[256,512]{1,0:T(8,128)(2,1)S(1)} %fusion.10), channel_id=1, source_target_pairs={{0,64},{64,0},{128,192},{192,128},{8,200},{200,8},{72,136},{136,72... | collective-permute-start | bytes 786440 | tf_op jit(solution)/shard_map/ppermute | solution.py:60
  31.9 11.9 %collective-permute-start.11 = (bf16[256,512]{1,0:T(8,128)(2,1)S(1)}, bf16[256,512]{1,0:T(8,128)(2,1)S(1)}, u32[]{:S(2)}, u32[]{:S(2)}) collective-permute-start(bf16[256,512]{1,0:T(8,128)(2,1)S(1)} %fusion.11), channel_id=1, source_target_pairs={{0,64},{64,0},{128,192},{192,128},{8,200},{200,8},{72,136},{136,72... | collective-permute-start | bytes 786440 | tf_op jit(solution)/shard_map/ppermute | solution.py:60
  38.4 10.6 %collective-permute-start.5 = (bf16[256,512]{1,0:T(8,128)(2,1)S(1)}, bf16[256,512]{1,0:T(8,128)(2,1)S(1)}, u32[]{:S(2)}, u32[]{:S(2)}) collective-permute-start(bf16[256,512]{1,0:T(8,128)(2,1)S(1)} %fusion.8), channel_id=1, source_target_pairs={{0,192},{192,0},{64,128},{128,64},{8,72},{72,8},{136,200},{200,136... | collective-permute-start | bytes 786440 | tf_op jit(solution)/shard_map/ppermute | solution.py:61
  42.6 22.2 %collective-permute-start.7 = (bf16[256,2048]{1,0:T(8,128)(2,1)}, bf16[256,2048]{1,0:T(8,128)(2,1)}, u32[]{:S(2)}, u32[]{:S(2)}) collective-permute-start(bf16[256,2048]{1,0:T(8,128)(2,1)} %param.5), channel_id=1, source_target_pairs={{0,8},{8,0},{1,9},{9,1},{2,10},{10,2},{3,11},{11,3},{4,12},{12,4},... | collective-permute-start | bytes 3145736 | tf_op jit(solution)/shard_map/ppermute | solution.py:49
  43.9 11.6 %collective-permute-start.12 = (bf16[256,512]{1,0:T(8,128)(2,1)S(1)}, bf16[256,512]{1,0:T(8,128)(2,1)S(1)}, u32[]{:S(2)}, u32[]{:S(2)}) collective-permute-start(bf16[256,512]{1,0:T(8,128)(2,1)S(1)} %fusion.9), channel_id=1, source_target_pairs={{0,192},{192,0},{64,128},{128,64},{8,72},{72,8},{136,200},{200,136... | collective-permute-start | bytes 786440 | tf_op jit(solution)/shard_map/ppermute | solution.py:61
  49.2 8.0 %collective-permute-start.6 = (bf16[256,512]{1,0:T(8,128)(2,1)S(1)}, bf16[256,512]{1,0:T(8,128)(2,1)S(1)}, u32[]{:S(2)}, u32[]{:S(2)}) collective-permute-start(bf16[256,512]{1,0:T(8,128)(2,1)S(1)} %add_convert_fusion.1), channel_id=1, source_target_pairs={{0,48},{48,0},{16,32},{32,16},{8,24},{24,8},{40,56},{56,40},{1,49}... | collective-permute-start | bytes 786440 | tf_op jit(solution)/shard_map/ppermute | solution.py:63
  55.6 5.6 %collective-permute-start.13 = (bf16[256,512]{1,0:T(8,128)(2,1)S(1)}, bf16[256,512]{1,0:T(8,128)(2,1)S(1)}, u32[]{:S(2)}, u32[]{:S(2)}) collective-permute-start(bf16[256,512]{1,0:T(8,128)(2,1)S(1)} %add_convert_fusion), channel_id=1, source_target_pairs={{0,48},{48,0},{16,32},{32,16},{8,24},{24,8},{40,56},{56,40},{1,49}... | collective-permute-start | bytes 786440 | tf_op jit(solution)/shard_map/ppermute | solution.py:63
  57.3 12.2 %collective-permute-start.8 = (bf16[256,1024]{1,0:T(8,128)(2,1)S(1)}, bf16[256,1024]{1,0:T(8,128)(2,1)S(1)}, u32[]{:S(2)}, u32[]{:S(2)}) collective-permute-start(bf16[256,1024]{1,0:T(8,128)(2,1)S(1)} %maximum_select_fusion.1), channel_id=1, source_target_pairs={{0,16},{16,0},{32,48},{48,32},{8,56},{56,8},{24,40},{40,24},{1,17}... | collective-permute-start | bytes 1572872 | tf_op jit(solution)/shard_map/ppermute | solution.py:65
  61.4 13.9 %collective-permute-start.14 = (bf16[256,1024]{1,0:T(8,128)(2,1)S(1)}, bf16[256,1024]{1,0:T(8,128)(2,1)}, u32[]{:S(2)}, u32[]{:S(2)}) collective-permute-start(bf16[256,1024]{1,0:T(8,128)(2,1)S(1)} %maximum_select_fusion.2), channel_id=1, source_target_pairs={{0,16},{16,0},{32,48},{48,32},{8,56},{56,8},{24,40},{40,24},{1,17}... | collective-permute-start | bytes 1572872 | tf_op jit(solution)/shard_map/ppermute | solution.py:65

commit v4 on v3

--- a/solution.py
+++ b/solution.py
@@ -34,6 +34,7 @@
     y, k = lax.axis_index("y"), lax.axis_index("core")
     p = jnp.where(k == 0, ((y + 1) // 2) % 2, y // 2)
     s = jnp.where(k == 0, y // 2, y % 2)
+    t = jnp.where(k == 0, s, 1 - s)
     n = 512 // CHUNKS
     r = 64 // CHUNKS
 
@@ -47,8 +48,9 @@
     q_mine = for_core(k)
     q_in = lax.ppermute(for_core(1 - k), "core", SWAP)
     s_in = lax.ppermute(slab, "core", SWAP)
-    both = jnp.where(k == 0, jnp.concatenate([slab, s_in]), jnp.concatenate([s_in, slab]))
-    s_kept, s_other = cut(both, p, 1024), cut(both, 1 - p, 1024)
+    both = jnp.concatenate([slab, s_in])
+    s_kept = cut(both, p, 1024)
+    s_second, s_third = cut(both, 2 * (1 - p) + t, 512), cut(both, 2 * (1 - p) + 1 - t, 512)
     outs = []
     for c in range(CHUNKS):
         part = dot(q_mine[c], gram) + dot(q_in[c], g_in)
@@ -62,10 +64,12 @@
         i0 = piece.astype(BF16)
         i1 = lax.ppermute(i0, ("y", "core"), STEP2)
         kept = jnp.where(s == 0, jnp.concatenate([i0, i1], axis=1), jnp.concatenate([i1, i0], axis=1))
-        other = lax.ppermute(kept, ("y", "core"), STEP1)
-        sc = dot_t(kept, s_kept) + dot_t(other, s_other)
+        i2 = lax.ppermute(i0, ("y", "core"), STEP1)
+        i3 = lax.ppermute(i1, ("y", "core"), STEP1)
+        sc = dot_t(kept, s_kept) + dot_t(i2, s_second) + dot_t(i3, s_third)
         outs.append(sc.astype(BF16).reshape(8, r, 2, 256).transpose(2, 0, 1, 3))
-    sc = jnp.stack(outs, axis=2).reshape(16, 64, 256)
+    sc = jnp.stack(outs, axis=2)
+    sc = jnp.where(k == 0, sc, sc[::-1]).reshape(16, 64, 256)
     sc = lax.all_to_all(sc, ("core", "x", "zl"), 0, 0, tiled=True)
     return sc.reshape(2, 8, 64, 256).astype(F32).sum(axis=1).astype(BF16).reshape(128, 256)
 

time: 96.2 us -> 93.8 us (0.975)
  waiting for transfers between devices: 32.2 us -> 27.9 us
  other arithmetic: 6.48 us -> 3.21 us
  local copies, waits for them, and re-layouts: 3.95 us -> 6.5 us
  matrix products: 7.68 us -> 10 us
  starting transfers between devices: 27.6 us -> 29.1 us
  blocking collectives: 17.8 us -> 16.4 us
    select_n x3 -> x1, other arithmetic: 3.39 us -> 0.12 us  [local(): sc = jnp.where(k == 0, sc, sc[::-1]).reshape(16, 64, 256)]
    dot_general x4 -> x6, matrix products: 2.97 us -> 5.33 us  [dot_t(): lax.dot_general(a, b, (((1,), (1,)), ((), ())), preferred_element_type=F32)]
    ppermute x2 -> x4, starting transfers between devices: 5.81 us -> 8.05 us  [the longest x2 5.64 us: local(): i2 = lax.ppermute(i0, ('y', 'core'), STEP1)]
    all_to_all x1, blocking collectives: 17.8 us -> 16.4 us  [local(): sc = lax.all_to_all(sc, ('core', 'x', 'zl'), 0, 0, tiled=True)]
    concatenate x0 -> x1, local copies, waits for them, and re-layouts: none -> 1.29 us  [local(): both = jnp.concatenate([slab, s_in])]
    ppermute x2, starting transfers between devices: 2.17 us -> 0.9 us  [local(): i1 = lax.ppermute(i0, ('y', 'core'), STEP2)]
    unnamed x9 -> x10, local copies, waits for them, and re-layouts: 2.19 us -> 3.45 us
    ppermute x2, waiting for transfers between devices: 8.78 us -> 7.57 us  [local(): lax.ppermute(piece.astype(BF16), ('zh', 'core'), STEP2).astype(F32)]
  transfers between devices with their start and end apart: 15 -> 17, of which waited for: 10 -> 11; matrix products, arithmetic and copies ran while one was open for 14% -> 16% of each run, Pallas kernels for 0% -> 0%
where the time goes in v4:
time: 93.8 us; the launch traced here: 93.5 us
  starting transfers between devices  29.1 us (31%)
  waiting for transfers between devices  27.9 us (30%)
  blocking collectives  16.4 us (17%)
  matrix products  10 us (11%)
  local copies, waits for them, and re-layouts  6.5 us (7%)
  other arithmetic  3.21 us (3%)
    all_to_all x1, blocking collectives, local(): sc = lax.all_to_all(sc, ('core', 'x', 'zl'), 0, 0, tiled=True)  16.4 us
    ppermute x2, waiting for transfers between devices, local(): lax.ppermute(cut(part, 1 - p, 1024).astype(BF16), ('y', 'core'), STEP1)  8.26 us
    ppermute x2, waiting for transfers between devices, local(): lax.ppermute(piece.astype(BF16), ('zh', 'core'), STEP2).astype(F32)  7.57 us
    ppermute x2, starting transfers between devices, local(): lax.ppermute(piece.astype(BF16), ('zh', 'core'), STEP1).astype(F32)  7.05 us
    ppermute x2, starting transfers between devices, local(): lax.ppermute(piece.astype(BF16), ('zh', 'core'), STEP2).astype(F32)  5.72 us
    ppermute x2, starting transfers between devices, local(): i2 = lax.ppermute(i0, ('y', 'core'), STEP1)  5.64 us
    dot_general x6, matrix products, dot_t(): lax.dot_general(a, b, (((1,), (1,)), ((), ())), preferred_element_type=F32)  5.33 us
    dot_general x4, matrix products, dot(): return jnp.dot(a, b, preferred_element_type=F32)  4.71 us
  transfers between devices with their start and end apart: 17, of which 11 were waited for; matrix products, arithmetic and copies ran while one was open for 16% of the time, Pallas kernels for 0%

profile of v4, /device:TPU:1, one launch (start us, length us, event | category | flops | bytes accessed | tf_op | source)
XLA Modules:
  0.0 93.5 jit_solution(6535685507311134456)
XLA Ops:
  0.0 3.2 %collective-permute-start.1 = (bf16[512,2048]{1,0:T(8,128)(2,1)}, bf16[512,2048]{1,0:T(8,128)(2,1)S(1)}, u32[]{:S(2)}, u32[]{:S(2)}) collective-permute-start(bf16[512,2048]{1,0:T(8,128)(2,1)} %param.4), channel_id=1, source_target_pairs={{0,8},{8,0},{1,9},{9,1},{2,10},{10,2},{3,11},{11,3},{4,12},{12,4},... | collective-permute-start | bytes 6291464 | tf_op jit(solution)/shard_map/ppermute | solution.py:41
  3.2 1.3 %constant_dynamic-slice_fusion = (bf16[8,1,2,32,512]{4,3,2,1,0:T(8,128)(2,1)S(1)}, bf16[2,8,32,512]{3,2,0,1:T(8,128)(2,1)S(1)}) fusion(bf16[8,2,2,32,512]{4,3,2,1,0:T(8,128)(2,1)} %bitcast.43, s32[]{:T(128)S(6)} %select_n.84, s32[]{:T(128)S(6)} %select_n.83), kind=kLoop, calls=%fused_computation.62 | loop fusion | bytes 2097160 | tf_op jit(solution)/shard_map/jit(dynamic_index_in_dim)/dynamic_slice | solution.py:45
  4.5 0.8 copy.7
  5.4 0.0 collective-permute-start
  5.4 0.0 copy-start
  5.4 2.4 %fusion.36 = f32[256,2048]{1,0:T(8,128)S(1)} fusion(bf16[256,512]{1,0:T(8,128)(2,1)S(1)} %bitcast.42, bf16[512,2048]{1,0:T(8,128)(2,1)} %param.4), kind=kOutput, calls=%fused_computation.67 | convolution fusion | flops 536870912 | bytes 4456448 | tf_op jit(solution)/shard_map/dot_general | solution.py:22
  7.9 0.7 fusion.35
  8.6 0.0 collective-permute-done
  8.7 0.0 collective-permute-done.1
  8.7 0.8 convolution_add_fusion
  9.4 0.1 dynamic-slice_convert_fusion
  9.5 1.1 %collective-permute-start.10 = (bf16[256,1024]{1,0:T(8,128)(2,1)S(1)}, bf16[256,1024]{1,0:T(8,128)(2,1)}, u32[]{:S(2)}, u32[]{:S(2)}) collective-permute-start(bf16[256,1024]{1,0:T(8,128)(2,1)S(1)} %dynamic-slice_convert_fusion), channel_id=1, source_target_pairs={{0,16},{16,0},{32,48},{48,32},{8,56},{56,8},{24,40},{40,24},{1,17}... | collective-permute-start | bytes 1572872 | tf_op jit(solution)/shard_map/ppermute | solution.py:57
  10.6 0.8 convolution_add_fusion.1
  11.4 1.3 %copy-done.1 = f32[256,2048]{1,0:T(8,128)} copy-done((f32[256,2048]{1,0:T(8,128)}, f32[256,2048]{1,0:T(8,128)S(1)}, u32[]{:S(2)}) %copy-start.1) | copy-done | bytes 2097176
  12.7 0.1 dynamic-slice_convert_fusion.1
  12.8 1.8 %collective-permute-start.2 = (bf16[256,1024]{1,0:T(8,128)(2,1)S(1)}, bf16[256,1024]{1,0:T(8,128)(2,1)S(1)}, u32[]{:S(2)}, u32[]{:S(2)}) collective-permute-start(bf16[256,1024]{1,0:T(8,128)(2,1)S(1)} %dynamic-slice_convert_fusion.1), channel_id=1, source_target_pairs={{0,16},{16,0},{32,48},{48,32},{8,56},{56,8},{24,40},{40,24},{1,17}... | collective-permute-start | bytes 1572872 | tf_op jit(solution)/shard_map/ppermute | solution.py:57
  14.5 4.4 %collective-permute-done.10 = bf16[256,1024]{1,0:T(8,128)(2,1)} collective-permute-done((bf16[256,1024]{1,0:T(8,128)(2,1)S(1)}, bf16[256,1024]{1,0:T(8,128)(2,1)}, u32[]{:S(2)}, u32[]{:S(2)}) %collective-permute-start.10) | collective-permute-done | bytes 524320 | tf_op jit(solution)/shard_map/ppermute | solution.py:57
  19.0 1.5 %convert_add_fusion = f32[256,1024]{1,0:T(8,128)S(1)} fusion(bf16[256,1024]{1,0:T(8,128)(2,1)} %collective-permute-done.10, f32[256,2048]{1,0:T(8,128)} %copy-done.3, s32[]{:T(128)S(6)} %select_n.88), kind=kLoop, calls=%fused_computation.8 | loop fusion | flops 524288 | bytes 2621444 | tf_op jit(solution)/shard_map/add | solution.py:58
  20.5 0.1 collective-permute-start.11
  20.6 3.8 %collective-permute-done.2 = bf16[256,1024]{1,0:T(8,128)(2,1)S(1)} collective-permute-done((bf16[256,1024]{1,0:T(8,128)(2,1)S(1)}, bf16[256,1024]{1,0:T(8,128)(2,1)S(1)}, u32[]{:S(2)}, u32[]{:S(2)}) %collective-permute-start.2) | collective-permute-done | bytes 524320 | tf_op jit(solution)/shard_map/ppermute | solution.py:57
  24.5 0.2 convert_add_fusion.1
  24.7 0.1 collective-permute-start.3
  24.8 2.5 %collective-permute-done.11 = bf16[256,512]{1,0:T(8,128)(2,1)S(1)} collective-permute-done((bf16[256,512]{1,0:T(8,128)(2,1)S(1)}, bf16[256,512]{1,0:T(8,128)(2,1)S(1)}, u32[]{:S(2)}, u32[]{:S(2)}) %collective-permute-start.11) | collective-permute-done | bytes 262176 | tf_op jit(solution)/shard_map/ppermute | solution.py:60
  27.3 0.1 fusion.25
  27.4 4.4 %collective-permute-start.12 = (bf16[256,512]{1,0:T(8,128)(2,1)S(1)}, bf16[256,512]{1,0:T(8,128)(2,1)S(1)}, u32[]{:S(2)}, u32[]{:S(2)}) collective-permute-start(bf16[256,512]{1,0:T(8,128)(2,1)S(1)} %fusion.25), channel_id=1, source_target_pairs={{0,64},{64,0},{128,192},{192,128},{8,200},{200,8},{72,136},{136,72... | collective-permute-start | bytes 786440 | tf_op jit(solution)/shard_map/ppermute | solution.py:62
  31.8 0.0 collective-permute-done.3
  31.8 0.1 fusion.24
  31.9 2.7 %collective-permute-start.4 = (bf16[256,512]{1,0:T(8,128)(2,1)S(1)}, bf16[256,512]{1,0:T(8,128)(2,1)S(1)}, u32[]{:S(2)}, u32[]{:S(2)}) collective-permute-start(bf16[256,512]{1,0:T(8,128)(2,1)S(1)} %fusion.24), channel_id=1, source_target_pairs={{0,64},{64,0},{128,192},{192,128},{8,200},{200,8},{72,136},{136,72... | collective-permute-start | bytes 786440 | tf_op jit(solution)/shard_map/ppermute | solution.py:62
  34.5 1.1 %collective-permute-start.7 = (bf16[256,2048]{1,0:T(8,128)(2,1)}, bf16[256,2048]{1,0:T(8,128)(2,1)}, u32[]{:S(2)}, u32[]{:S(2)}) collective-permute-start(bf16[256,2048]{1,0:T(8,128)(2,1)} %param.5), channel_id=1, source_target_pairs={{0,8},{8,0},{1,9},{9,1},{2,10},{10,2},{3,11},{11,3},{4,12},{12,4},... | collective-permute-start | bytes 3145736 | tf_op jit(solution)/shard_map/ppermute | solution.py:50
  35.7 2.6 %collective-permute-done.12 = bf16[256,512]{1,0:T(8,128)(2,1)S(1)} collective-permute-done((bf16[256,512]{1,0:T(8,128)(2,1)S(1)}, bf16[256,512]{1,0:T(8,128)(2,1)S(1)}, u32[]{:S(2)}, u32[]{:S(2)}) %collective-permute-start.12) | collective-permute-done | bytes 262176 | tf_op jit(solution)/shard_map/ppermute | solution.py:62
  38.3 0.1 fusion.23
  38.4 4.2 %collective-permute-start.13 = (bf16[256,512]{1,0:T(8,128)(2,1)S(1)}, bf16[256,512]{1,0:T(8,128)(2,1)S(1)}, u32[]{:S(2)}, u32[]{:S(2)}) collective-permute-start(bf16[256,512]{1,0:T(8,128)(2,1)S(1)} %fusion.23), channel_id=1, source_target_pairs={{0,192},{192,0},{64,128},{128,64},{8,72},{72,8},{136,200},{200,136... | collective-permute-start | bytes 786440 | tf_op jit(solution)/shard_map/ppermute | solution.py:63
  42.6 1.2 %collective-permute-done.4 = bf16[256,512]{1,0:T(8,128)(2,1)S(1)} collective-permute-done((bf16[256,512]{1,0:T(8,128)(2,1)S(1)}, bf16[256,512]{1,0:T(8,128)(2,1)S(1)}, u32[]{:S(2)}, u32[]{:S(2)}) %collective-permute-start.4) | collective-permute-done | bytes 262176 | tf_op jit(solution)/shard_map/ppermute | solution.py:62
  43.8 0.1 fusion.22
  43.9 1.5 %collective-permute-start.5 = (bf16[256,512]{1,0:T(8,128)(2,1)S(1)}, bf16[256,512]{1,0:T(8,128)(2,1)S(1)}, u32[]{:S(2)}, u32[]{:S(2)}) collective-permute-start(bf16[256,512]{1,0:T(8,128)(2,1)S(1)} %fusion.22), channel_id=1, source_target_pairs={{0,192},{192,0},{64,128},{128,64},{8,72},{72,8},{136,200},{200,136... | collective-permute-start | bytes 786440 | tf_op jit(solution)/shard_map/ppermute | solution.py:63
  45.4 3.6 %collective-permute-done.13 = bf16[256,512]{1,0:T(8,128)(2,1)S(1)} collective-permute-done((bf16[256,512]{1,0:T(8,128)(2,1)S(1)}, bf16[256,512]{1,0:T(8,128)(2,1)S(1)}, u32[]{:S(2)}, u32[]{:S(2)}) %collective-permute-start.13) | collective-permute-done | bytes 262176 | tf_op jit(solution)/shard_map/ppermute | solution.py:63
  49.0 0.1 add_convert_fusion
  49.2 2.3 %collective-permute-start.15 = (bf16[256,512]{1,0:T(8,128)(2,1)S(1)}, bf16[256,512]{1,0:T(8,128)(2,1)S(1)}, u32[]{:S(2)}, u32[]{:S(2)}) collective-permute-start(bf16[256,512]{1,0:T(8,128)(2,1)S(1)} %add_convert_fusion), channel_id=1, source_target_pairs={{0,16},{16,0},{32,48},{48,32},{8,56},{56,8},{24,40},{40,24},{1,17}... | collective-permute-start | bytes 786440 | tf_op jit(solution)/shard_map/ppermute | solution.py:67
  51.5 3.9 %collective-permute-done.5 = bf16[256,512]{1,0:T(8,128)(2,1)S(1)} collective-permute-done((bf16[256,512]{1,0:T(8,128)(2,1)S(1)}, bf16[256,512]{1,0:T(8,128)(2,1)S(1)}, u32[]{:S(2)}, u32[]{:S(2)}) %collective-permute-start.5) | collective-permute-done | bytes 262176 | tf_op jit(solution)/shard_map/ppermute | solution.py:63
  55.4 0.1 add_convert_fusion.1
  55.6 0.9 collective-permute-start.6
  56.5 1.3 %constant_dynamic-update-slice_fusion.1 = bf16[512,2048]{1,0:T(8,128)(2,1)S(1)} fusion(bf16[256,2048]{1,0:T(8,128)(2,1)} %param.5), kind=kLoop, calls=%fused_computation.55 | loop fusion | bytes 2097152
  57.8 1.3 %constant_dynamic-update-slice_fusion = bf16[512,2048]{1,0:T(8,128)(2,1)S(1)} fusion(bf16[512,2048]{1,0:T(8,128)(2,1)S(1)} %constant_dynamic-update-slice_fusion.1, bf16[256,2048]{1,0:T(8,128)(2,1)} %collective-permute-done.7), kind=kLoop, calls=%fused_computation.54 | loop fusion | bytes 2097152 | tf_op jit(solution)/shard_map/concatenate | solution.py:51
  59.1 3.3 %collective-permute-start.8 = (bf16[256,512]{1,0:T(8,128)(2,1)S(1)}, bf16[256,512]{1,0:T(8,128)(2,1)S(1)}, u32[]{:S(2)}, u32[]{:S(2)}) collective-permute-start(bf16[256,512]{1,0:T(8,128)(2,1)S(1)} %add_convert_fusion.1), channel_id=1, source_target_pairs={{0,16},{16,0},{32,48},{48,32},{8,56},{56,8},{24,40},{40,24},{1,17}... | collective-permute-start | bytes 786440 | tf_op jit(solution)/shard_map/ppermute | solution.py:67
  62.4 0.0 collective-permute-done.14
  62.4 0.1 collective-permute-start.16
  62.5 0.3 collective-permute-done.6
  62.8 2.3 %collective-permute-start.9 = (bf16[256,512]{1,0:T(8,128)(2,1)}, bf16[256,512]{1,0:T(8,128)(2,1)}, u32[]{:S(2)}, u32[]{:S(2)}) collective-permute-start(bf16[256,512]{1,0:T(8,128)(2,1)} %collective-permute-done.6), channel_id=1, source_target_pairs={{0,16},{16,0},{32,48},{48,32},{8,56},{56,8},{24,40},{40,24},{1,17}... | collective-permute-start | bytes 786440 | tf_op jit(solution)/shard_map/ppermute | solution.py:68
  65.1 0.3 fusion.18
  65.5 1.5 %convolution_add_fusion.2 = f32[256,512]{1,0:T(8,128)S(1)} fusion(f32[256,512]{1,0:T(8,128)S(1)} %fusion.18, bf16[512,2048]{1,0:T(8,128)(2,1)S(1)} %constant_dynamic-update-slice_fusion, s32[]{:T(128)S(6)} %select_n.88, bf16[256,512]{1,0:T(8,128)(2,1)} %collective-permute-done.14, bf16[256,512]{1,0:T(8,128)(2,1)S(1)} %add_convert_fusion, pred[]{:T(512)S(6)} %eq.14), kind=kOutput, calls=%fused_computation.2 | convolution fusion | flops 270925824 | bytes 2621445 | tf_op jit(solution)/shard_map/dot_general | solution.py:26
  67.0 2.4 %collective-permute-done.8 = bf16[256,512]{1,0:T(8,128)(2,1)S(1)} collective-permute-done((bf16[256,512]{1,0:T(8,128)(2,1)S(1)}, bf16[256,512]{1,0:T(8,128)(2,1)S(1)}, u32[]{:S(2)}, u32[]{:S(2)}) %collective-permute-start.8) | collective-permute-done | bytes 262176 | tf_op jit(solution)/shard_map/ppermute | solution.py:67
  69.4 0.3 fusion.20
  69.7 1.5 %convolution_add_fusion.3 = f32[256,512]{1,0:T(8,128)S(1)} fusion(f32[256,512]{1,0:T(8,128)S(1)} %fusion.20, bf16[512,2048]{1,0:T(8,128)(2,1)S(1)} %constant_dynamic-update-slice_fusion, s32[]{:T(128)S(6)} %select_n.88, bf16[256,512]{1,0:T(8,128)(2,1)} %collective-permute-done.6, bf16[256,512]{1,0:T(8,128)(2,1)S(1)} %add_convert_fusion.1, pred[]{:T(512)S(6)} %eq.14), kind=kOutput, calls=%fused_computation.3 | convolution fusion | flops 270925824 | bytes 2621445 | tf_op jit(solution)/shard_map/dot_general | solution.py:26
  71.2 0.6 collective-permute-done.16
  71.8 0.3 fusion.1
  72.2 0.1 reshape.29
  72.2 2.5 %collective-permute-done.9 = bf16[256,512]{1,0:T(8,128)(2,1)} collective-permute-done((bf16[256,512]{1,0:T(8,128)(2,1)}, bf16[256,512]{1,0:T(8,128)(2,1)}, u32[]{:S(2)}, u32[]{:S(2)}) %collective-permute-start.9) | collective-permute-done | bytes 262176 | tf_op jit(solution)/shard_map/ppermute | solution.py:68
  74.7 1.3 %fusion = bf16[256,512]{1,0:T(8,128)(2,1)S(1)} fusion(f32[256,512]{1,0:T(8,128)S(1)} %convolution_add_fusion.3, bf16[256,512]{1,0:T(8,128)(2,1)} %collective-permute-done.9, bf16[512,2048]{1,0:T(8,128)(2,1)S(1)} %constant_dynamic-update-slice_fusion, s32[]{:T(128)S(6)} %select_n.95), kind=kOutput, calls=%fused_computation.6 | convolution fusion | flops 134479872 | bytes 1572868 | tf_op jit(solution)/shard_map/dot_general | solution.py:26
  76.0 0.1 reshape.28
  76.1 0.1 copy_bitcast_fusion
  76.2 0.1 pad_maximum_fusion
  76.2 0.1 reverse_select_fusion
  76.4 16.4 %all_to_all.5 = bf16[16,64,256]{2,1,0:T(8,128)(2,1)S(1)} all-to-all(bf16[16,64,256]{2,1,0:T(8,128)(2,1)S(1)} %bitcast.40), channel_id=1, replica_groups=mesh['zh'=4,'y'=4,'core'=2,'x'=4,'zl'=2] {'core','x','zl'}, dimensions={0} | all-to-all | bytes 1048576 | tf_op jit(solution)/shard_map/all_to_all | solution.py:73
  92.8 0.7 bitcast_reduce_fusion
  (12 shorter events, 0.1 us)
Async XLA Ops:
  0.0 8.7 %collective-permute-start.1 = (bf16[512,2048]{1,0:T(8,128)(2,1)}, bf16[512,2048]{1,0:T(8,128)(2,1)S(1)}, u32[]{:S(2)}, u32[]{:S(2)}) collective-permute-start(bf16[512,2048]{1,0:T(8,128)(2,1)} %param.4), channel_id=1, source_target_pairs={{0,8},{8,0},{1,9},{9,1},{2,10},{10,2},{3,11},{11,3},{4,12},{12,4},... | collective-permute-start | bytes 6291464 | tf_op jit(solution)/shard_map/ppermute | solution.py:41
  5.4 3.3 %collective-permute-start = (bf16[2,256,512]{2,1,0:T(8,128)(2,1)}, bf16[2,256,512]{2,1,0:T(8,128)(2,1)S(1)}, u32[]{:S(2)}, u32[]{:S(2)}) collective-permute-start(bf16[2,256,512]{2,1,0:T(8,128)(2,1)} %bitcast.6), channel_id=1, source_target_pairs={{0,8},{8,0},{1,9},{9,1},{2,10},{10,2},{3,11},{11,3},{4,12},{12,4},... | collective-permute-start | bytes 1572872 | tf_op jit(solution)/shard_map/ppermute | solution.py:49
  5.4 2.5 %copy-start = (bf16[512,2048]{1,0:T(8,128)(2,1)S(1)}, bf16[512,2048]{1,0:T(8,128)(2,1)}, u32[]{:S(2)}) copy-start(bf16[512,2048]{1,0:T(8,128)(2,1)} %param.4) | copy-start | bytes 6291460
  9.4 2.0 %copy-start.3 = (f32[256,2048]{1,0:T(8,128)}, f32[256,2048]{1,0:T(8,128)S(1)}, u32[]{:S(2)}) copy-start(f32[256,2048]{1,0:T(8,128)S(1)} %convolution_add_fusion) | copy-start | bytes 6291460
  9.5 9.4 %collective-permute-start.10 = (bf16[256,1024]{1,0:T(8,128)(2,1)S(1)}, bf16[256,1024]{1,0:T(8,128)(2,1)}, u32[]{:S(2)}, u32[]{:S(2)}) collective-permute-start(bf16[256,1024]{1,0:T(8,128)(2,1)S(1)} %dynamic-slice_convert_fusion), channel_id=1, source_target_pairs={{0,16},{16,0},{32,48},{48,32},{8,56},{56,8},{24,40},{40,24},{1,17}... | collective-permute-start | bytes 1572872 | tf_op jit(solution)/shard_map/ppermute | solution.py:57
  11.4 1.3 %copy-start.1 = (f32[256,2048]{1,0:T(8,128)}, f32[256,2048]{1,0:T(8,128)S(1)}, u32[]{:S(2)}) copy-start(f32[256,2048]{1,0:T(8,128)S(1)} %convolution_add_fusion.1) | copy-start | bytes 6291460
  12.8 11.7 %collective-permute-start.2 = (bf16[256,1024]{1,0:T(8,128)(2,1)S(1)}, bf16[256,1024]{1,0:T(8,128)(2,1)S(1)}, u32[]{:S(2)}, u32[]{:S(2)}) collective-permute-start(bf16[256,1024]{1,0:T(8,128)(2,1)S(1)} %dynamic-slice_convert_fusion.1), channel_id=1, source_target_pairs={{0,16},{16,0},{32,48},{48,32},{8,56},{56,8},{24,40},{40,24},{1,17}... | collective-permute-start | bytes 1572872 | tf_op jit(solution)/shard_map/ppermute | solution.py:57
  14.5 9.9 %copy-start.2 = (f32[256,2048]{1,0:T(8,128)S(1)}, f32[256,2048]{1,0:T(8,128)}, u32[]{:S(2)}) copy-start(f32[256,2048]{1,0:T(8,128)} %copy-done.1) | copy-start | bytes 6291460
  20.5 6.8 %collective-permute-start.11 = (bf16[256,512]{1,0:T(8,128)(2,1)S(1)}, bf16[256,512]{1,0:T(8,128)(2,1)S(1)}, u32[]{:S(2)}, u32[]{:S(2)}) collective-permute-start(bf16[256,512]{1,0:T(8,128)(2,1)S(1)} %dynamic-slice_convert_fusion.2), channel_id=1, source_target_pairs={{0,48},{48,0},{16,32},{32,16},{8,24},{24,8},{40,56},{56,40},{1,49}... | collective-permute-start | bytes 786440 | tf_op jit(solution)/shard_map/ppermute | solution.py:60
  24.7 7.1 %collective-permute-start.3 = (bf16[256,512]{1,0:T(8,128)(2,1)S(1)}, bf16[256,512]{1,0:T(8,128)(2,1)S(1)}, u32[]{:S(2)}, u32[]{:S(2)}) collective-permute-start(bf16[256,512]{1,0:T(8,128)(2,1)S(1)} %dynamic-slice_convert_fusion.3), channel_id=1, source_target_pairs={{0,48},{48,0},{16,32},{32,16},{8,24},{24,8},{40,56},{56,40},{1,49}... | collective-permute-start | bytes 786440 | tf_op jit(solution)/shard_map/ppermute | solution.py:60
  27.4 10.9 %collective-permute-start.12 = (bf16[256,512]{1,0:T(8,128)(2,1)S(1)}, bf16[256,512]{1,0:T(8,128)(2,1)S(1)}, u32[]{:S(2)}, u32[]{:S(2)}) collective-permute-start(bf16[256,512]{1,0:T(8,128)(2,1)S(1)} %fusion.25), channel_id=1, source_target_pairs={{0,64},{64,0},{128,192},{192,128},{8,200},{200,8},{72,136},{136,72... | collective-permute-start | bytes 786440 | tf_op jit(solution)/shard_map/ppermute | solution.py:62
  31.9 11.9 %collective-permute-start.4 = (bf16[256,512]{1,0:T(8,128)(2,1)S(1)}, bf16[256,512]{1,0:T(8,128)(2,1)S(1)}, u32[]{:S(2)}, u32[]{:S(2)}) collective-permute-start(bf16[256,512]{1,0:T(8,128)(2,1)S(1)} %fusion.24), channel_id=1, source_target_pairs={{0,64},{64,0},{128,192},{192,128},{8,200},{200,8},{72,136},{136,72... | collective-permute-start | bytes 786440 | tf_op jit(solution)/shard_map/ppermute | solution.py:62
  34.5 23.3 %collective-permute-start.7 = (bf16[256,2048]{1,0:T(8,128)(2,1)}, bf16[256,2048]{1,0:T(8,128)(2,1)}, u32[]{:S(2)}, u32[]{:S(2)}) collective-permute-start(bf16[256,2048]{1,0:T(8,128)(2,1)} %param.5), channel_id=1, source_target_pairs={{0,8},{8,0},{1,9},{9,1},{2,10},{10,2},{3,11},{11,3},{4,12},{12,4},... | collective-permute-start | bytes 3145736 | tf_op jit(solution)/shard_map/ppermute | solution.py:50
  38.4 10.6 %collective-permute-start.13 = (bf16[256,512]{1,0:T(8,128)(2,1)S(1)}, bf16[256,512]{1,0:T(8,128)(2,1)S(1)}, u32[]{:S(2)}, u32[]{:S(2)}) collective-permute-start(bf16[256,512]{1,0:T(8,128)(2,1)S(1)} %fusion.23), channel_id=1, source_target_pairs={{0,192},{192,0},{64,128},{128,64},{8,72},{72,8},{136,200},{200,136... | collective-permute-start | bytes 786440 | tf_op jit(solution)/shard_map/ppermute | solution.py:63
  43.9 11.6 %collective-permute-start.5 = (bf16[256,512]{1,0:T(8,128)(2,1)S(1)}, bf16[256,512]{1,0:T(8,128)(2,1)S(1)}, u32[]{:S(2)}, u32[]{:S(2)}) collective-permute-start(bf16[256,512]{1,0:T(8,128)(2,1)S(1)} %fusion.22), channel_id=1, source_target_pairs={{0,192},{192,0},{64,128},{128,64},{8,72},{72,8},{136,200},{200,136... | collective-permute-start | bytes 786440 | tf_op jit(solution)/shard_map/ppermute | solution.py:63
  49.2 16.0 %collective-permute-start.15 = (bf16[256,512]{1,0:T(8,128)(2,1)S(1)}, bf16[256,512]{1,0:T(8,128)(2,1)S(1)}, u32[]{:S(2)}, u32[]{:S(2)}) collective-permute-start(bf16[256,512]{1,0:T(8,128)(2,1)S(1)} %add_convert_fusion), channel_id=1, source_target_pairs={{0,16},{16,0},{32,48},{48,32},{8,56},{56,8},{24,40},{40,24},{1,17}... | collective-permute-start | bytes 786440 | tf_op jit(solution)/shard_map/ppermute | solution.py:67
  51.5 10.9 %collective-permute-start.14 = (bf16[256,512]{1,0:T(8,128)(2,1)S(1)}, bf16[256,512]{1,0:T(8,128)(2,1)}, u32[]{:S(2)}, u32[]{:S(2)}) collective-permute-start(bf16[256,512]{1,0:T(8,128)(2,1)S(1)} %add_convert_fusion), channel_id=1, source_target_pairs={{0,48},{48,0},{16,32},{32,16},{8,24},{24,8},{40,56},{56,40},{1,49}... | collective-permute-start | bytes 786440 | tf_op jit(solution)/shard_map/ppermute | solution.py:65
  55.6 7.2 %collective-permute-start.6 = (bf16[256,512]{1,0:T(8,128)(2,1)S(1)}, bf16[256,512]{1,0:T(8,128)(2,1)}, u32[]{:S(2)}, u32[]{:S(2)}) collective-permute-start(bf16[256,512]{1,0:T(8,128)(2,1)S(1)} %add_convert_fusion.1), channel_id=1, source_target_pairs={{0,48},{48,0},{16,32},{32,16},{8,24},{24,8},{40,56},{56,40},{1,49}... | collective-permute-start | bytes 786440 | tf_op jit(solution)/shard_map/ppermute | solution.py:65
  59.1 10.3 %collective-permute-start.8 = (bf16[256,512]{1,0:T(8,128)(2,1)S(1)}, bf16[256,512]{1,0:T(8,128)(2,1)S(1)}, u32[]{:S(2)}, u32[]{:S(2)}) collective-permute-start(bf16[256,512]{1,0:T(8,128)(2,1)S(1)} %add_convert_fusion.1), channel_id=1, source_target_pairs={{0,16},{16,0},{32,48},{48,32},{8,56},{56,8},{24,40},{40,24},{1,17}... | collective-permute-start | bytes 786440 | tf_op jit(solution)/shard_map/ppermute | solution.py:67
  62.4 9.4 %collective-permute-start.16 = (bf16[256,512]{1,0:T(8,128)(2,1)}, bf16[256,512]{1,0:T(8,128)(2,1)S(1)}, u32[]{:S(2)}, u32[]{:S(2)}) collective-permute-start(bf16[256,512]{1,0:T(8,128)(2,1)} %collective-permute-done.14), channel_id=1, source_target_pairs={{0,16},{16,0},{32,48},{48,32},{8,56},{56,8},{24,40},{40,24},{1,17}... | collective-permute-start | bytes 786440 | tf_op jit(solution)/shard_map/ppermute | solution.py:68
  62.8 11.9 %collective-permute-start.9 = (bf16[256,512]{1,0:T(8,128)(2,1)}, bf16[256,512]{1,0:T(8,128)(2,1)}, u32[]{:S(2)}, u32[]{:S(2)}) collective-permute-start(bf16[256,512]{1,0:T(8,128)(2,1)} %collective-permute-done.6), channel_id=1, source_target_pairs={{0,16},{16,0},{32,48},{48,32},{8,56},{56,8},{24,40},{40,24},{1,17}... | collective-permute-start | bytes 786440 | tf_op jit(solution)/shard_map/ppermute | solution.py:68

commit v5 on v4

--- a/solution.py
+++ b/solution.py
@@ -64,8 +64,12 @@
         i0 = piece.astype(BF16)
         i1 = lax.ppermute(i0, ("y", "core"), STEP2)
         kept = jnp.where(s == 0, jnp.concatenate([i0, i1], axis=1), jnp.concatenate([i1, i0], axis=1))
-        i2 = lax.ppermute(i0, ("y", "core"), STEP1)
-        i3 = lax.ppermute(i1, ("y", "core"), STEP1)
+        if c < CHUNKS - 1:
+            i23 = lax.ppermute(jnp.concatenate([i0, i1], axis=1), ("y", "core"), STEP1)
+            i2, i3 = i23[:, :512], i23[:, 512:]
+        else:
+            i2 = lax.ppermute(i0, ("y", "core"), STEP1)
+            i3 = lax.ppermute(i1, ("y", "core"), STEP1)
         sc = dot_t(kept, s_kept) + dot_t(i2, s_second) + dot_t(i3, s_third)
         outs.append(sc.astype(BF16).reshape(8, r, 2, 256).transpose(2, 0, 1, 3))
     sc = jnp.stack(outs, axis=2)

time: 93.8 us -> 99.3 us (1.059)
  waiting for transfers between devices: 27.9 us -> 34 us
  starting transfers between devices: 29.1 us -> 24.6 us
  other arithmetic: 3.21 us -> 6.75 us
  local copies, waits for them, and re-layouts: 6.5 us -> 7.59 us
    ppermute x2 -> x1, waiting for transfers between devices: 3.06 us -> 9.5 us  [local(): i3 = lax.ppermute(i1, ('y', 'core'), STEP1)]
    ppermute x2, waiting for transfers between devices: 0.27 us -> 4.33 us  [local(): i1 = lax.ppermute(i0, ('y', 'core'), STEP2)]
    ppermute x2 -> x1, starting transfers between devices: 2.41 us -> 0.01 us  [local(): i3 = lax.ppermute(i1, ('y', 'core'), STEP1)]
    ppermute x2 -> x1, waiting for transfers between devices: 2.39 us -> 0.01 us  [local(): i2 = lax.ppermute(i0, ('y', 'core'), STEP1)]
    ppermute x2 -> x1, starting transfers between devices: 5.64 us -> 3.3 us  [local(): i2 = lax.ppermute(i0, ('y', 'core'), STEP1)]
    ppermute x2, waiting for transfers between devices: 7.57 us -> 5.65 us  [local(): lax.ppermute(piece.astype(BF16), ('zh', 'core'), STEP2).astype(F32)]
    convert_element_type x2, other arithmetic: 0.28 us -> 2.18 us  [local(): i0 = piece.astype(BF16)]
    unnamed x10 -> x20, local copies, waits for them, and re-layouts: 3.45 us -> 4.54 us
  transfers between devices with their start and end apart: 17 -> 16, of which waited for: 11 -> 9; matrix products, arithmetic and copies ran while one was open for 16% -> 17% of each run, Pallas kernels for 0% -> 0%
where the time goes in v5:
time: 99.3 us; the launch traced here: 99 us
  waiting for transfers between devices  34 us (34%)
  starting transfers between devices  24.6 us (25%)
  blocking collectives  16.4 us (17%)
  matrix products  9.27 us (9%)
  local copies, waits for them, and re-layouts  7.59 us (8%)
  other arithmetic  6.75 us (7%)
    all_to_all x1, blocking collectives, local(): sc = lax.all_to_all(sc, ('core', 'x', 'zl'), 0, 0, tiled=True)  16.4 us
    ppermute x1, waiting for transfers between devices, local(): i3 = lax.ppermute(i1, ('y', 'core'), STEP1)  9.5 us
    ppermute x2, waiting for transfers between devices, local(): lax.ppermute(cut(part, 1 - p, 1024).astype(BF16), ('y', 'core'), STEP1)  8.23 us
    ppermute x2, starting transfers between devices, local(): lax.ppermute(piece.astype(BF16), ('zh', 'core'), STEP1).astype(F32)  7.05 us
    ppermute x2, waiting for transfers between devices, local(): lax.ppermute(piece.astype(BF16), ('zh', 'core'), STEP2).astype(F32)  5.65 us
    ppermute x2, starting transfers between devices, local(): lax.ppermute(piece.astype(BF16), ('zh', 'core'), STEP2).astype(F32)  5.63 us
    dot_general x4, matrix products, dot(): return jnp.dot(a, b, preferred_element_type=F32)  4.71 us
    dot_general x6, matrix products, dot_t(): lax.dot_general(a, b, (((1,), (1,)), ((), ())), preferred_element_type=F32)  4.56 us
  transfers between devices with their start and end apart: 16, of which 9 were waited for; matrix products, arithmetic and copies ran while one was open for 17% of the time, Pallas kernels for 0%

profile of v5, /device:TPU:1, one launch (start us, length us, event | category | flops | bytes accessed | tf_op | source)
XLA Modules:
  0.0 99.0 jit_solution(18438676310021336462)
XLA Ops:
  0.0 3.2 %collective-permute-start.1 = (bf16[512,2048]{1,0:T(8,128)(2,1)}, bf16[512,2048]{1,0:T(8,128)(2,1)S(1)}, u32[]{:S(2)}, u32[]{:S(2)}) collective-permute-start(bf16[512,2048]{1,0:T(8,128)(2,1)} %param.4), channel_id=1, source_target_pairs={{0,8},{8,0},{1,9},{9,1},{2,10},{10,2},{3,11},{11,3},{4,12},{12,4},... | collective-permute-start | bytes 6291464 | tf_op jit(solution)/shard_map/ppermute | solution.py:41
  3.2 1.3 %constant_dynamic-slice_fusion = (bf16[8,1,2,32,512]{4,3,2,1,0:T(8,128)(2,1)S(1)}, bf16[2,8,32,512]{3,2,0,1:T(8,128)(2,1)S(1)}) fusion(bf16[8,2,2,32,512]{4,3,2,1,0:T(8,128)(2,1)} %bitcast.41, s32[]{:T(128)S(6)} %select_n.84, s32[]{:T(128)S(6)} %select_n.83), kind=kLoop, calls=%fused_computation.63 | loop fusion | bytes 2097160 | tf_op jit(solution)/shard_map/jit(dynamic_index_in_dim)/dynamic_slice | solution.py:45
  4.5 0.8 copy.7
  5.4 0.0 collective-permute-start
  5.4 0.0 copy-start
  5.4 2.4 %fusion.37 = f32[256,2048]{1,0:T(8,128)S(1)} fusion(bf16[256,512]{1,0:T(8,128)(2,1)S(1)} %bitcast.40, bf16[512,2048]{1,0:T(8,128)(2,1)} %param.4), kind=kOutput, calls=%fused_computation.68 | convolution fusion | flops 536870912 | bytes 4456448 | tf_op jit(solution)/shard_map/dot_general | solution.py:22
  7.9 0.7 fusion.36
  8.6 0.0 collective-permute-done
  8.7 0.0 collective-permute-done.1
  8.7 0.8 convolution_add_fusion.1
  9.4 0.1 dynamic-slice_convert_fusion.1
  9.5 1.1 %collective-permute-start.2 = (bf16[256,1024]{1,0:T(8,128)(2,1)S(1)}, bf16[256,1024]{1,0:T(8,128)(2,1)}, u32[]{:S(2)}, u32[]{:S(2)}) collective-permute-start(bf16[256,1024]{1,0:T(8,128)(2,1)S(1)} %dynamic-slice_convert_fusion.1), channel_id=1, source_target_pairs={{0,16},{16,0},{32,48},{48,32},{8,56},{56,8},{24,40},{40,24},{1,17}... | collective-permute-start | bytes 1572872 | tf_op jit(solution)/shard_map/ppermute | solution.py:57
  10.6 0.8 convolution_add_fusion
  11.4 1.3 %copy-done.1 = f32[256,2048]{1,0:T(8,128)} copy-done((f32[256,2048]{1,0:T(8,128)}, f32[256,2048]{1,0:T(8,128)S(1)}, u32[]{:S(2)}) %copy-start.1) | copy-done | bytes 2097176
  12.7 0.1 dynamic-slice_convert_fusion
  12.8 1.8 %collective-permute-start.9 = (bf16[256,1024]{1,0:T(8,128)(2,1)S(1)}, bf16[256,1024]{1,0:T(8,128)(2,1)S(1)}, u32[]{:S(2)}, u32[]{:S(2)}) collective-permute-start(bf16[256,1024]{1,0:T(8,128)(2,1)S(1)} %dynamic-slice_convert_fusion), channel_id=1, source_target_pairs={{0,16},{16,0},{32,48},{48,32},{8,56},{56,8},{24,40},{40,24},{1,17}... | collective-permute-start | bytes 1572872 | tf_op jit(solution)/shard_map/ppermute | solution.py:57
  14.6 4.4 %collective-permute-done.2 = bf16[256,1024]{1,0:T(8,128)(2,1)} collective-permute-done((bf16[256,1024]{1,0:T(8,128)(2,1)S(1)}, bf16[256,1024]{1,0:T(8,128)(2,1)}, u32[]{:S(2)}, u32[]{:S(2)}) %collective-permute-start.2) | collective-permute-done | bytes 524320 | tf_op jit(solution)/shard_map/ppermute | solution.py:57
  19.0 1.5 %convert_add_fusion.1 = f32[256,1024]{1,0:T(8,128)S(1)} fusion(bf16[256,1024]{1,0:T(8,128)(2,1)} %collective-permute-done.2, f32[256,2048]{1,0:T(8,128)} %copy-done.3, s32[]{:T(128)S(6)} %select_n.88), kind=kLoop, calls=%fused_computation.10 | loop fusion | flops 524288 | bytes 2621444 | tf_op jit(solution)/shard_map/add | solution.py:58
  20.5 0.1 collective-permute-start.3
  20.6 3.8 %collective-permute-done.9 = bf16[256,1024]{1,0:T(8,128)(2,1)S(1)} collective-permute-done((bf16[256,1024]{1,0:T(8,128)(2,1)S(1)}, bf16[256,1024]{1,0:T(8,128)(2,1)S(1)}, u32[]{:S(2)}, u32[]{:S(2)}) %collective-permute-start.9) | collective-permute-done | bytes 524320 | tf_op jit(solution)/shard_map/ppermute | solution.py:57
  24.5 0.2 convert_add_fusion
  24.7 0.1 collective-permute-start.10
  24.8 2.5 %collective-permute-done.3 = bf16[256,512]{1,0:T(8,128)(2,1)S(1)} collective-permute-done((bf16[256,512]{1,0:T(8,128)(2,1)S(1)}, bf16[256,512]{1,0:T(8,128)(2,1)S(1)}, u32[]{:S(2)}, u32[]{:S(2)}) %collective-permute-start.3) | collective-permute-done | bytes 262176 | tf_op jit(solution)/shard_map/ppermute | solution.py:60
  27.3 0.1 fusion.25
  27.4 4.4 %collective-permute-start.4 = (bf16[256,512]{1,0:T(8,128)(2,1)S(1)}, bf16[256,512]{1,0:T(8,128)(2,1)S(1)}, u32[]{:S(2)}, u32[]{:S(2)}) collective-permute-start(bf16[256,512]{1,0:T(8,128)(2,1)S(1)} %fusion.25), channel_id=1, source_target_pairs={{0,64},{64,0},{128,192},{192,128},{8,200},{200,8},{72,136},{136,72... | collective-permute-start | bytes 786440 | tf_op jit(solution)/shard_map/ppermute | solution.py:62
  31.8 0.1 fusion.26
  31.9 2.7 %collective-permute-start.11 = (bf16[256,512]{1,0:T(8,128)(2,1)S(1)}, bf16[256,512]{1,0:T(8,128)(2,1)S(1)}, u32[]{:S(2)}, u32[]{:S(2)}) collective-permute-start(bf16[256,512]{1,0:T(8,128)(2,1)S(1)} %fusion.26), channel_id=1, source_target_pairs={{0,64},{64,0},{128,192},{192,128},{8,200},{200,8},{72,136},{136,72... | collective-permute-start | bytes 786440 | tf_op jit(solution)/shard_map/ppermute | solution.py:62
  34.5 1.1 %collective-permute-start.7 = (bf16[256,2048]{1,0:T(8,128)(2,1)}, bf16[256,2048]{1,0:T(8,128)(2,1)}, u32[]{:S(2)}, u32[]{:S(2)}) collective-permute-start(bf16[256,2048]{1,0:T(8,128)(2,1)} %param.5), channel_id=1, source_target_pairs={{0,8},{8,0},{1,9},{9,1},{2,10},{10,2},{3,11},{11,3},{4,12},{12,4},... | collective-permute-start | bytes 3145736 | tf_op jit(solution)/shard_map/ppermute | solution.py:50
  35.7 2.6 %collective-permute-done.4 = bf16[256,512]{1,0:T(8,128)(2,1)S(1)} collective-permute-done((bf16[256,512]{1,0:T(8,128)(2,1)S(1)}, bf16[256,512]{1,0:T(8,128)(2,1)S(1)}, u32[]{:S(2)}, u32[]{:S(2)}) %collective-permute-start.4) | collective-permute-done | bytes 262176 | tf_op jit(solution)/shard_map/ppermute | solution.py:62
  38.3 0.1 fusion.21
  38.4 4.2 %collective-permute-start.5 = (bf16[256,512]{1,0:T(8,128)(2,1)S(1)}, bf16[256,512]{1,0:T(8,128)(2,1)}, u32[]{:S(2)}, u32[]{:S(2)}) collective-permute-start(bf16[256,512]{1,0:T(8,128)(2,1)S(1)} %fusion.21), channel_id=1, source_target_pairs={{0,192},{192,0},{64,128},{128,64},{8,72},{72,8},{136,200},{200,136... | collective-permute-start | bytes 786440 | tf_op jit(solution)/shard_map/ppermute | solution.py:63
  42.6 1.2 %collective-permute-done.11 = bf16[256,512]{1,0:T(8,128)(2,1)S(1)} collective-permute-done((bf16[256,512]{1,0:T(8,128)(2,1)S(1)}, bf16[256,512]{1,0:T(8,128)(2,1)S(1)}, u32[]{:S(2)}, u32[]{:S(2)}) %collective-permute-start.11) | collective-permute-done | bytes 262176 | tf_op jit(solution)/shard_map/ppermute | solution.py:62
  43.8 0.8 fusion.22
  44.5 1.4 %collective-permute-start.12 = (bf16[256,512]{1,0:T(8,128)(2,1)}, bf16[256,512]{1,0:T(8,128)(2,1)}, u32[]{:S(2)}, u32[]{:S(2)}) collective-permute-start(bf16[256,512]{1,0:T(8,128)(2,1)} %fusion.22), channel_id=1, source_target_pairs={{0,192},{192,0},{64,128},{128,64},{8,72},{72,8},{136,200},{200,136... | collective-permute-start | bytes 786440 | tf_op jit(solution)/shard_map/ppermute | solution.py:63
  46.0 2.3 %constant_dynamic-update-slice_fusion.1 = bf16[512,2048]{1,0:T(8,128)(2,1)} fusion(bf16[256,2048]{1,0:T(8,128)(2,1)} %param.5), kind=kLoop, calls=%fused_computation.56 | loop fusion | bytes 2097152
  48.3 0.7 collective-permute-done.5
  49.0 1.1 %add_convert_fusion.1 = bf16[256,512]{1,0:T(8,128)(2,1)S(1)} fusion(bf16[256,512]{1,0:T(8,128)(2,1)} %collective-permute-done.5, bf16[256,512]{1,0:T(8,128)(2,1)S(1)} %collective-permute-done.4, bf16[256,512]{1,0:T(8,128)(2,1)S(1)} %collective-permute-done.3, f32[256,1024]{1,0:T(8,128)S(1)} %convert_add_fusion.1, s32[]{:T(128)S(6)} %select_n.90), kind=kLoop, calls=%fused_computation.31 | loop fusion | flops 917504 | bytes 1572868 | tf_op jit(solution)/shard_map/convert_element_type | solution.py:64
  50.1 0.7 collective-permute-start.6
  50.9 5.0 %collective-permute-done.12 = bf16[256,512]{1,0:T(8,128)(2,1)} collective-permute-done((bf16[256,512]{1,0:T(8,128)(2,1)}, bf16[256,512]{1,0:T(8,128)(2,1)}, u32[]{:S(2)}, u32[]{:S(2)}) %collective-permute-start.12) | collective-permute-done | bytes 262176 | tf_op jit(solution)/shard_map/ppermute | solution.py:63
  55.8 1.1 %add_convert_fusion = bf16[256,512]{1,0:T(8,128)(2,1)S(1)} fusion(bf16[256,512]{1,0:T(8,128)(2,1)} %collective-permute-done.12, bf16[256,512]{1,0:T(8,128)(2,1)S(1)} %collective-permute-done.11, bf16[256,512]{1,0:T(8,128)(2,1)S(1)} %collective-permute-done.10, f32[256,1024]{1,0:T(8,128)S(1)} %convert_add_fusion, s32[]{:T(128)S(6)} %select_n.90), kind=kLoop, calls=%fused_computation.27 | loop fusion | flops 917504 | bytes 1572868 | tf_op jit(solution)/shard_map/convert_element_type | solution.py:64
  56.9 3.3 %collective-permute-start.14 = (bf16[256,512]{1,0:T(8,128)(2,1)S(1)}, bf16[256,512]{1,0:T(8,128)(2,1)S(1)}, u32[]{:S(2)}, u32[]{:S(2)}) collective-permute-start(bf16[256,512]{1,0:T(8,128)(2,1)S(1)} %add_convert_fusion), channel_id=1, source_target_pairs={{0,16},{16,0},{32,48},{48,32},{8,56},{56,8},{24,40},{40,24},{1,17}... | collective-permute-start | bytes 786440 | tf_op jit(solution)/shard_map/ppermute | solution.py:71
  60.2 0.0 collective-permute-start.13
  60.2 0.0 collective-permute-done.7
  60.2 1.3 %constant_dynamic-update-slice_fusion = bf16[512,2048]{1,0:T(8,128)(2,1)S(1)} fusion(bf16[512,2048]{1,0:T(8,128)(2,1)S(1)} %copy-done.4, bf16[256,2048]{1,0:T(8,128)(2,1)} %collective-permute-done.7), kind=kLoop, calls=%fused_computation.55 | loop fusion | bytes 2097152 | tf_op jit(solution)/shard_map/concatenate | solution.py:51
  61.5 0.0 collective-permute-done.6
  61.5 1.0 pad_maximum_fusion
  62.5 0.5 collective-permute-start.8
  63.0 4.3 %collective-permute-done.13 = bf16[256,512]{1,0:T(8,128)(2,1)S(1)} collective-permute-done((bf16[256,512]{1,0:T(8,128)(2,1)S(1)}, bf16[256,512]{1,0:T(8,128)(2,1)S(1)}, u32[]{:S(2)}, u32[]{:S(2)}) %collective-permute-start.13) | collective-permute-done | bytes 262176 | tf_op jit(solution)/shard_map/ppermute | solution.py:65
  67.3 0.0 collective-permute-start.15
  67.3 0.0 collective-permute-done.14
  67.3 0.3 fusion.17
  67.7 0.5 convolution_add_fusion.2
  68.2 9.5 %collective-permute-done.15 = bf16[256,512]{1,0:T(8,128)(2,1)S(1)} collective-permute-done((bf16[256,512]{1,0:T(8,128)(2,1)S(1)}, bf16[256,512]{1,0:T(8,128)(2,1)S(1)}, u32[]{:S(2)}, u32[]{:S(2)}) %collective-permute-start.15) | collective-permute-done | bytes 262176 | tf_op jit(solution)/shard_map/ppermute | solution.py:72
  77.7 0.3 fusion.1
  78.0 0.1 reshape.29
  78.1 1.5 %fusion.15 = f32[256,512]{1,0:T(8,128)S(1)} fusion(bf16[512,2048]{1,0:T(8,128)(2,1)} %copy-done.5, s32[]{:T(128)S(6)} %select_n.95, bf16[256,1024]{1,0:T(8,128)(2,1)S(1)} %collective-permute-done.8), kind=kOutput, calls=%fused_computation.39 | convolution fusion | flops 134217728 | bytes 1310724 | tf_op jit(solution)/shard_map/dot_general | solution.py:26
  79.6 1.4 %fusion.19 = f32[256,512]{1,0:T(8,128)S(1)} fusion(bf16[512,2048]{1,0:T(8,128)(2,1)} %copy-done.5, s32[]{:T(128)S(6)} %select_n.94, bf16[256,1024]{1,0:T(8,128)(2,1)S(1)} %collective-permute-done.8), kind=kOutput, calls=%fused_computation.43 | convolution fusion | flops 134217728 | bytes 1310724 | tf_op jit(solution)/shard_map/dot_general | solution.py:26
  81.1 0.5 fusion.2
  81.6 0.1 reshape.28
  81.6 0.1 copy_bitcast_fusion
  81.7 0.1 pad_maximum_fusion.1
  81.8 0.1 reverse_select_fusion
  81.9 16.4 %all_to_all.5 = bf16[16,64,256]{2,1,0:T(8,128)(2,1)S(1)} all-to-all(bf16[16,64,256]{2,1,0:T(8,128)(2,1)S(1)} %bitcast.38), channel_id=1, replica_groups=mesh['zh'=4,'y'=4,'core'=2,'x'=4,'zl'=2] {'core','x','zl'}, dimensions={0} | all-to-all | bytes 1048576 | tf_op jit(solution)/shard_map/all_to_all | solution.py:77
  98.3 0.7 bitcast_reduce_fusion
  (21 shorter events, 0.2 us)
Async XLA Ops:
  0.0 8.7 %collective-permute-start.1 = (bf16[512,2048]{1,0:T(8,128)(2,1)}, bf16[512,2048]{1,0:T(8,128)(2,1)S(1)}, u32[]{:S(2)}, u32[]{:S(2)}) collective-permute-start(bf16[512,2048]{1,0:T(8,128)(2,1)} %param.4), channel_id=1, source_target_pairs={{0,8},{8,0},{1,9},{9,1},{2,10},{10,2},{3,11},{11,3},{4,12},{12,4},... | collective-permute-start | bytes 6291464 | tf_op jit(solution)/shard_map/ppermute | solution.py:41
  5.4 3.3 %collective-permute-start = (bf16[2,256,512]{2,1,0:T(8,128)(2,1)}, bf16[2,256,512]{2,1,0:T(8,128)(2,1)S(1)}, u32[]{:S(2)}, u32[]{:S(2)}) collective-permute-start(bf16[2,256,512]{2,1,0:T(8,128)(2,1)} %bitcast.6), channel_id=1, source_target_pairs={{0,8},{8,0},{1,9},{9,1},{2,10},{10,2},{3,11},{11,3},{4,12},{12,4},... | collective-permute-start | bytes 1572872 | tf_op jit(solution)/shard_map/ppermute | solution.py:49
  5.4 2.5 %copy-start = (bf16[512,2048]{1,0:T(8,128)(2,1)S(1)}, bf16[512,2048]{1,0:T(8,128)(2,1)}, u32[]{:S(2)}) copy-start(bf16[512,2048]{1,0:T(8,128)(2,1)} %param.4) | copy-start | bytes 6291460
  9.4 2.0 %copy-start.3 = (f32[256,2048]{1,0:T(8,128)}, f32[256,2048]{1,0:T(8,128)S(1)}, u32[]{:S(2)}) copy-start(f32[256,2048]{1,0:T(8,128)S(1)} %convolution_add_fusion.1) | copy-start | bytes 6291460
  9.5 9.4 %collective-permute-start.2 = (bf16[256,1024]{1,0:T(8,128)(2,1)S(1)}, bf16[256,1024]{1,0:T(8,128)(2,1)}, u32[]{:S(2)}, u32[]{:S(2)}) collective-permute-start(bf16[256,1024]{1,0:T(8,128)(2,1)S(1)} %dynamic-slice_convert_fusion.1), channel_id=1, source_target_pairs={{0,16},{16,0},{32,48},{48,32},{8,56},{56,8},{24,40},{40,24},{1,17}... | collective-permute-start | bytes 1572872 | tf_op jit(solution)/shard_map/ppermute | solution.py:57
  11.4 1.3 %copy-start.1 = (f32[256,2048]{1,0:T(8,128)}, f32[256,2048]{1,0:T(8,128)S(1)}, u32[]{:S(2)}) copy-start(f32[256,2048]{1,0:T(8,128)S(1)} %convolution_add_fusion) | copy-start | bytes 6291460
  12.8 11.7 %collective-permute-start.9 = (bf16[256,1024]{1,0:T(8,128)(2,1)S(1)}, bf16[256,1024]{1,0:T(8,128)(2,1)S(1)}, u32[]{:S(2)}, u32[]{:S(2)}) collective-permute-start(bf16[256,1024]{1,0:T(8,128)(2,1)S(1)} %dynamic-slice_convert_fusion), channel_id=1, source_target_pairs={{0,16},{16,0},{32,48},{48,32},{8,56},{56,8},{24,40},{40,24},{1,17}... | collective-permute-start | bytes 1572872 | tf_op jit(solution)/shard_map/ppermute | solution.py:57
  14.6 9.9 %copy-start.2 = (f32[256,2048]{1,0:T(8,128)S(1)}, f32[256,2048]{1,0:T(8,128)}, u32[]{:S(2)}) copy-start(f32[256,2048]{1,0:T(8,128)} %copy-done.1) | copy-start | bytes 6291460
  20.5 6.8 %collective-permute-start.3 = (bf16[256,512]{1,0:T(8,128)(2,1)S(1)}, bf16[256,512]{1,0:T(8,128)(2,1)S(1)}, u32[]{:S(2)}, u32[]{:S(2)}) collective-permute-start(bf16[256,512]{1,0:T(8,128)(2,1)S(1)} %dynamic-slice_convert_fusion.3), channel_id=1, source_target_pairs={{0,48},{48,0},{16,32},{32,16},{8,24},{24,8},{40,56},{56,40},{1,49}... | collective-permute-start | bytes 786440 | tf_op jit(solution)/shard_map/ppermute | solution.py:60
  24.7 7.1 %collective-permute-start.10 = (bf16[256,512]{1,0:T(8,128)(2,1)S(1)}, bf16[256,512]{1,0:T(8,128)(2,1)S(1)}, u32[]{:S(2)}, u32[]{:S(2)}) collective-permute-start(bf16[256,512]{1,0:T(8,128)(2,1)S(1)} %dynamic-slice_convert_fusion.2), channel_id=1, source_target_pairs={{0,48},{48,0},{16,32},{32,16},{8,24},{24,8},{40,56},{56,40},{1,49}... | collective-permute-start | bytes 786440 | tf_op jit(solution)/shard_map/ppermute | solution.py:60
  27.4 10.9 %collective-permute-start.4 = (bf16[256,512]{1,0:T(8,128)(2,1)S(1)}, bf16[256,512]{1,0:T(8,128)(2,1)S(1)}, u32[]{:S(2)}, u32[]{:S(2)}) collective-permute-start(bf16[256,512]{1,0:T(8,128)(2,1)S(1)} %fusion.25), channel_id=1, source_target_pairs={{0,64},{64,0},{128,192},{192,128},{8,200},{200,8},{72,136},{136,72... | collective-permute-start | bytes 786440 | tf_op jit(solution)/shard_map/ppermute | solution.py:62
  31.9 11.9 %collective-permute-start.11 = (bf16[256,512]{1,0:T(8,128)(2,1)S(1)}, bf16[256,512]{1,0:T(8,128)(2,1)S(1)}, u32[]{:S(2)}, u32[]{:S(2)}) collective-permute-start(bf16[256,512]{1,0:T(8,128)(2,1)S(1)} %fusion.26), channel_id=1, source_target_pairs={{0,64},{64,0},{128,192},{192,128},{8,200},{200,8},{72,136},{136,72... | collective-permute-start | bytes 786440 | tf_op jit(solution)/shard_map/ppermute | solution.py:62
  34.5 25.7 %collective-permute-start.7 = (bf16[256,2048]{1,0:T(8,128)(2,1)}, bf16[256,2048]{1,0:T(8,128)(2,1)}, u32[]{:S(2)}, u32[]{:S(2)}) collective-permute-start(bf16[256,2048]{1,0:T(8,128)(2,1)} %param.5), channel_id=1, source_target_pairs={{0,8},{8,0},{1,9},{9,1},{2,10},{10,2},{3,11},{11,3},{4,12},{12,4},... | collective-permute-start | bytes 3145736 | tf_op jit(solution)/shard_map/ppermute | solution.py:50
  38.4 10.6 %collective-permute-start.5 = (bf16[256,512]{1,0:T(8,128)(2,1)S(1)}, bf16[256,512]{1,0:T(8,128)(2,1)}, u32[]{:S(2)}, u32[]{:S(2)}) collective-permute-start(bf16[256,512]{1,0:T(8,128)(2,1)S(1)} %fusion.21), channel_id=1, source_target_pairs={{0,192},{192,0},{64,128},{128,64},{8,72},{72,8},{136,200},{200,136... | collective-permute-start | bytes 786440 | tf_op jit(solution)/shard_map/ppermute | solution.py:63
  44.5 11.3 %collective-permute-start.12 = (bf16[256,512]{1,0:T(8,128)(2,1)}, bf16[256,512]{1,0:T(8,128)(2,1)}, u32[]{:S(2)}, u32[]{:S(2)}) collective-permute-start(bf16[256,512]{1,0:T(8,128)(2,1)} %fusion.22), channel_id=1, source_target_pairs={{0,192},{192,0},{64,128},{128,64},{8,72},{72,8},{136,200},{200,136... | collective-permute-start | bytes 786440 | tf_op jit(solution)/shard_map/ppermute | solution.py:63
  48.3 11.9 %copy-start.4 = (bf16[512,2048]{1,0:T(8,128)(2,1)S(1)}, bf16[512,2048]{1,0:T(8,128)(2,1)}, u32[]{:S(2)}) copy-start(bf16[512,2048]{1,0:T(8,128)(2,1)} %constant_dynamic-update-slice_fusion.1) | copy-start | bytes 6291460
  50.1 11.4 %collective-permute-start.6 = (bf16[256,512]{1,0:T(8,128)(2,1)S(1)}, bf16[256,512]{1,0:T(8,128)(2,1)S(1)}, u32[]{:S(2)}, u32[]{:S(2)}) collective-permute-start(bf16[256,512]{1,0:T(8,128)(2,1)S(1)} %add_convert_fusion.1), channel_id=1, source_target_pairs={{0,48},{48,0},{16,32},{32,16},{8,24},{24,8},{40,56},{56,40},{1,49}... | collective-permute-start | bytes 786440 | tf_op jit(solution)/shard_map/ppermute | solution.py:65
  56.9 10.4 %collective-permute-start.14 = (bf16[256,512]{1,0:T(8,128)(2,1)S(1)}, bf16[256,512]{1,0:T(8,128)(2,1)S(1)}, u32[]{:S(2)}, u32[]{:S(2)}) collective-permute-start(bf16[256,512]{1,0:T(8,128)(2,1)S(1)} %add_convert_fusion), channel_id=1, source_target_pairs={{0,16},{16,0},{32,48},{48,32},{8,56},{56,8},{24,40},{40,24},{1,17}... | collective-permute-start | bytes 786440 | tf_op jit(solution)/shard_map/ppermute | solution.py:71
  60.2 7.1 %collective-permute-start.13 = (bf16[256,512]{1,0:T(8,128)(2,1)S(1)}, bf16[256,512]{1,0:T(8,128)(2,1)S(1)}, u32[]{:S(2)}, u32[]{:S(2)}) collective-permute-start(bf16[256,512]{1,0:T(8,128)(2,1)S(1)} %add_convert_fusion), channel_id=1, source_target_pairs={{0,48},{48,0},{16,32},{32,16},{8,24},{24,8},{40,56},{56,40},{1,49}... | collective-permute-start | bytes 786440 | tf_op jit(solution)/shard_map/ppermute | solution.py:65
  61.5 16.2 %copy-start.5 = (bf16[512,2048]{1,0:T(8,128)(2,1)}, bf16[512,2048]{1,0:T(8,128)(2,1)S(1)}, u32[]{:S(2)}) copy-start(bf16[512,2048]{1,0:T(8,128)(2,1)S(1)} %constant_dynamic-update-slice_fusion) | copy-start | bytes 6291460
  61.5 6.6 %copy-start.7 = (bf16[256,512]{1,0:T(8,128)(2,1)}, bf16[256,512]{1,0:T(8,128)(2,1)S(1)}, u32[]{:S(2)}) copy-start(bf16[256,512]{1,0:T(8,128)(2,1)S(1)} %collective-permute-done.6) | copy-start | bytes 786436
  62.5 15.6 %collective-permute-start.8 = (bf16[256,1024]{1,0:T(8,128)(2,1)}, bf16[256,1024]{1,0:T(8,128)(2,1)S(1)}, u32[]{:S(2)}, u32[]{:S(2)}) collective-permute-start(bf16[256,1024]{1,0:T(8,128)(2,1)} %pad_maximum_fusion), channel_id=1, source_target_pairs={{0,16},{16,0},{32,48},{48,32},{8,56},{56,8},{24,40},{40,24},{1,17}... | collective-permute-start | bytes 1572872 | tf_op jit(solution)/shard_map/ppermute | solution.py:68
  67.3 10.4 %collective-permute-start.15 = (bf16[256,512]{1,0:T(8,128)(2,1)S(1)}, bf16[256,512]{1,0:T(8,128)(2,1)S(1)}, u32[]{:S(2)}, u32[]{:S(2)}) collective-permute-start(bf16[256,512]{1,0:T(8,128)(2,1)S(1)} %collective-permute-done.13), channel_id=1, source_target_pairs={{0,16},{16,0},{32,48},{48,32},{8,56},{56,8},{24,40},{40,24},{1,17}... | collective-permute-start | bytes 786440 | tf_op jit(solution)/shard_map/ppermute | solution.py:72
  78.0 3.0 %copy-start.6 = (bf16[512,2048]{1,0:T(8,128)(2,1)S(1)}, bf16[512,2048]{1,0:T(8,128)(2,1)}, u32[]{:S(2)}) copy-start(bf16[512,2048]{1,0:T(8,128)(2,1)} %copy-done.5) | copy-start | bytes 6291460
  78.1 2.9 %copy-start.8 = (bf16[256,512]{1,0:T(8,128)(2,1)S(1)}, bf16[256,512]{1,0:T(8,128)(2,1)}, u32[]{:S(2)}) copy-start(bf16[256,512]{1,0:T(8,128)(2,1)} %copy-done.7) | copy-start | bytes 786436

commit v6 on v4

--- a/solution.py
+++ b/solution.py
@@ -66,7 +66,7 @@
         kept = jnp.where(s == 0, jnp.concatenate([i0, i1], axis=1), jnp.concatenate([i1, i0], axis=1))
         i2 = lax.ppermute(i0, ("y", "core"), STEP1)
         i3 = lax.ppermute(i1, ("y", "core"), STEP1)
-        sc = dot_t(kept, s_kept) + dot_t(i2, s_second) + dot_t(i3, s_third)
+        sc = dot_t(i3, s_third) + (dot_t(i2, s_second) + dot_t(kept, s_kept))
         outs.append(sc.astype(BF16).reshape(8, r, 2, 256).transpose(2, 0, 1, 3))
     sc = jnp.stack(outs, axis=2)
     sc = jnp.where(k == 0, sc, sc[::-1]).reshape(16, 64, 256)

time: 93.8 us -> 94 us (level)
  waiting for transfers between devices: 27.9 us -> 30.3 us
  starting transfers between devices: 29.1 us -> 27.9 us
    ppermute x2, starting transfers between devices: 5.64 us -> 3.42 us  [local(): i2 = lax.ppermute(i0, ('y', 'core'), STEP1)]
    ppermute x2, waiting for transfers between devices: 3.06 us -> 4.86 us  [local(): i3 = lax.ppermute(i1, ('y', 'core'), STEP1)]
    ppermute x2, waiting for transfers between devices: 7.57 us -> 9.3 us  [local(): lax.ppermute(piece.astype(BF16), ('zh', 'core'), STEP2).astype(F32)]
    dot_general x6, matrix products: 5.33 us -> 4.38 us  [dot_t(): lax.dot_general(a, b, (((1,), (1,)), ((), ())), preferred_element_type=F32)]
  transfers between devices with their start and end apart: 17 -> 17, of which waited for: 11 -> 10; matrix products, arithmetic and copies ran while one was open for 16% -> 16% of each run, Pallas kernels for 0% -> 0%
where the time goes in v6:
time: 94 us; the launch traced here: 93.7 us
  waiting for transfers between devices  30.3 us (32%)
  starting transfers between devices  27.9 us (30%)
  blocking collectives  16.4 us (17%)
  matrix products  9.09 us (10%)
  local copies, waits for them, and re-layouts  6.5 us (7%)
  other arithmetic  3.21 us (3%)
    all_to_all x1, blocking collectives, local(): sc = lax.all_to_all(sc, ('core', 'x', 'zl'), 0, 0, tiled=True)  16.4 us
    ppermute x2, waiting for transfers between devices, local(): lax.ppermute(piece.astype(BF16), ('zh', 'core'), STEP2).astype(F32)  9.3 us
    ppermute x2, waiting for transfers between devices, local(): lax.ppermute(cut(part, 1 - p, 1024).astype(BF16), ('y', 'core'), STEP1)  8.26 us
    ppermute x2, starting transfers between devices, local(): lax.ppermute(piece.astype(BF16), ('zh', 'core'), STEP1).astype(F32)  7.05 us
    ppermute x2, starting transfers between devices, local(): lax.ppermute(piece.astype(BF16), ('zh', 'core'), STEP2).astype(F32)  5.72 us
    ppermute x2, waiting for transfers between devices, local(): i3 = lax.ppermute(i1, ('y', 'core'), STEP1)  4.86 us
    dot_general x4, matrix products, dot(): return jnp.dot(a, b, preferred_element_type=F32)  4.71 us
    dot_general x6, matrix products, dot_t(): lax.dot_general(a, b, (((1,), (1,)), ((), ())), preferred_element_type=F32)  4.38 us
  transfers between devices with their start and end apart: 17, of which 10 were waited for; matrix products, arithmetic and copies ran while one was open for 16% of the time, Pallas kernels for 0%

profile of v6, /device:TPU:1, one launch (start us, length us, event | category | flops | bytes accessed | tf_op | source)
XLA Modules:
  0.0 93.7 jit_solution(15430416264183609807)
XLA Ops:
  0.0 3.2 %collective-permute-start.1 = (bf16[512,2048]{1,0:T(8,128)(2,1)}, bf16[512,2048]{1,0:T(8,128)(2,1)S(1)}, u32[]{:S(2)}, u32[]{:S(2)}) collective-permute-start(bf16[512,2048]{1,0:T(8,128)(2,1)} %param.4), channel_id=1, source_target_pairs={{0,8},{8,0},{1,9},{9,1},{2,10},{10,2},{3,11},{11,3},{4,12},{12,4},... | collective-permute-start | bytes 6291464 | tf_op jit(solution)/shard_map/ppermute | solution.py:41
  3.2 1.3 %constant_dynamic-slice_fusion = (bf16[8,1,2,32,512]{4,3,2,1,0:T(8,128)(2,1)S(1)}, bf16[2,8,32,512]{3,2,0,1:T(8,128)(2,1)S(1)}) fusion(bf16[8,2,2,32,512]{4,3,2,1,0:T(8,128)(2,1)} %bitcast.43, s32[]{:T(128)S(6)} %select_n.80, s32[]{:T(128)S(6)} %select_n.79), kind=kLoop, calls=%fused_computation.62 | loop fusion | bytes 2097160 | tf_op jit(solution)/shard_map/jit(dynamic_index_in_dim)/dynamic_slice | solution.py:45
  4.5 0.8 copy.7
  5.4 0.0 collective-permute-start
  5.4 0.0 copy-start
  5.4 2.4 %fusion.36 = f32[256,2048]{1,0:T(8,128)S(1)} fusion(bf16[256,512]{1,0:T(8,128)(2,1)S(1)} %bitcast.42, bf16[512,2048]{1,0:T(8,128)(2,1)} %param.4), kind=kOutput, calls=%fused_computation.67 | convolution fusion | flops 536870912 | bytes 4456448 | tf_op jit(solution)/shard_map/dot_general | solution.py:22
  7.9 0.7 fusion.35
  8.6 0.0 collective-permute-done
  8.7 0.8 convolution_add_fusion
  9.4 0.1 dynamic-slice_convert_fusion
  9.5 1.1 %collective-permute-start.10 = (bf16[256,1024]{1,0:T(8,128)(2,1)S(1)}, bf16[256,1024]{1,0:T(8,128)(2,1)}, u32[]{:S(2)}, u32[]{:S(2)}) collective-permute-start(bf16[256,1024]{1,0:T(8,128)(2,1)S(1)} %dynamic-slice_convert_fusion), channel_id=1, source_target_pairs={{0,16},{16,0},{32,48},{48,32},{8,56},{56,8},{24,40},{40,24},{1,17}... | collective-permute-start | bytes 1572872 | tf_op jit(solution)/shard_map/ppermute | solution.py:57
  10.6 0.8 convolution_add_fusion.1
  11.4 1.3 %copy-done.1 = f32[256,2048]{1,0:T(8,128)} copy-done((f32[256,2048]{1,0:T(8,128)}, f32[256,2048]{1,0:T(8,128)S(1)}, u32[]{:S(2)}) %copy-start.1) | copy-done | bytes 2097176
  12.7 0.1 dynamic-slice_convert_fusion.1
  12.8 1.8 %collective-permute-start.2 = (bf16[256,1024]{1,0:T(8,128)(2,1)S(1)}, bf16[256,1024]{1,0:T(8,128)(2,1)S(1)}, u32[]{:S(2)}, u32[]{:S(2)}) collective-permute-start(bf16[256,1024]{1,0:T(8,128)(2,1)S(1)} %dynamic-slice_convert_fusion.1), channel_id=1, source_target_pairs={{0,16},{16,0},{32,48},{48,32},{8,56},{56,8},{24,40},{40,24},{1,17}... | collective-permute-start | bytes 1572872 | tf_op jit(solution)/shard_map/ppermute | solution.py:57
  14.5 4.4 %collective-permute-done.10 = bf16[256,1024]{1,0:T(8,128)(2,1)} collective-permute-done((bf16[256,1024]{1,0:T(8,128)(2,1)S(1)}, bf16[256,1024]{1,0:T(8,128)(2,1)}, u32[]{:S(2)}, u32[]{:S(2)}) %collective-permute-start.10) | collective-permute-done | bytes 524320 | tf_op jit(solution)/shard_map/ppermute | solution.py:57
  19.0 1.5 %convert_add_fusion = f32[256,1024]{1,0:T(8,128)S(1)} fusion(bf16[256,1024]{1,0:T(8,128)(2,1)} %collective-permute-done.10, f32[256,2048]{1,0:T(8,128)} %copy-done.3, s32[]{:T(128)S(6)} %select_n.85), kind=kLoop, calls=%fused_computation.8 | loop fusion | flops 524288 | bytes 2621444 | tf_op jit(solution)/shard_map/add | solution.py:58
  20.5 0.1 collective-permute-start.11
  20.6 3.8 %collective-permute-done.2 = bf16[256,1024]{1,0:T(8,128)(2,1)S(1)} collective-permute-done((bf16[256,1024]{1,0:T(8,128)(2,1)S(1)}, bf16[256,1024]{1,0:T(8,128)(2,1)S(1)}, u32[]{:S(2)}, u32[]{:S(2)}) %collective-permute-start.2) | collective-permute-done | bytes 524320 | tf_op jit(solution)/shard_map/ppermute | solution.py:57
  24.5 0.2 convert_add_fusion.1
  24.7 0.1 collective-permute-start.3
  24.8 2.5 %collective-permute-done.11 = bf16[256,512]{1,0:T(8,128)(2,1)S(1)} collective-permute-done((bf16[256,512]{1,0:T(8,128)(2,1)S(1)}, bf16[256,512]{1,0:T(8,128)(2,1)S(1)}, u32[]{:S(2)}, u32[]{:S(2)}) %collective-permute-start.11) | collective-permute-done | bytes 262176 | tf_op jit(solution)/shard_map/ppermute | solution.py:60
  27.3 0.1 fusion.25
  27.4 4.4 %collective-permute-start.12 = (bf16[256,512]{1,0:T(8,128)(2,1)S(1)}, bf16[256,512]{1,0:T(8,128)(2,1)S(1)}, u32[]{:S(2)}, u32[]{:S(2)}) collective-permute-start(bf16[256,512]{1,0:T(8,128)(2,1)S(1)} %fusion.25), channel_id=1, source_target_pairs={{0,64},{64,0},{128,192},{192,128},{8,200},{200,8},{72,136},{136,72... | collective-permute-start | bytes 786440 | tf_op jit(solution)/shard_map/ppermute | solution.py:62
  31.8 0.0 collective-permute-done.3
  31.8 0.1 fusion.24
  31.9 2.7 %collective-permute-start.4 = (bf16[256,512]{1,0:T(8,128)(2,1)S(1)}, bf16[256,512]{1,0:T(8,128)(2,1)S(1)}, u32[]{:S(2)}, u32[]{:S(2)}) collective-permute-start(bf16[256,512]{1,0:T(8,128)(2,1)S(1)} %fusion.24), channel_id=1, source_target_pairs={{0,64},{64,0},{128,192},{192,128},{8,200},{200,8},{72,136},{136,72... | collective-permute-start | bytes 786440 | tf_op jit(solution)/shard_map/ppermute | solution.py:62
  34.5 1.1 %collective-permute-start.8 = (bf16[256,2048]{1,0:T(8,128)(2,1)}, bf16[256,2048]{1,0:T(8,128)(2,1)}, u32[]{:S(2)}, u32[]{:S(2)}) collective-permute-start(bf16[256,2048]{1,0:T(8,128)(2,1)} %param.5), channel_id=1, source_target_pairs={{0,8},{8,0},{1,9},{9,1},{2,10},{10,2},{3,11},{11,3},{4,12},{12,4},... | collective-permute-start | bytes 3145736 | tf_op jit(solution)/shard_map/ppermute | solution.py:50
  35.7 2.6 %collective-permute-done.12 = bf16[256,512]{1,0:T(8,128)(2,1)S(1)} collective-permute-done((bf16[256,512]{1,0:T(8,128)(2,1)S(1)}, bf16[256,512]{1,0:T(8,128)(2,1)S(1)}, u32[]{:S(2)}, u32[]{:S(2)}) %collective-permute-start.12) | collective-permute-done | bytes 262176 | tf_op jit(solution)/shard_map/ppermute | solution.py:62
  38.3 0.1 fusion.23
  38.4 4.2 %collective-permute-start.13 = (bf16[256,512]{1,0:T(8,128)(2,1)S(1)}, bf16[256,512]{1,0:T(8,128)(2,1)S(1)}, u32[]{:S(2)}, u32[]{:S(2)}) collective-permute-start(bf16[256,512]{1,0:T(8,128)(2,1)S(1)} %fusion.23), channel_id=1, source_target_pairs={{0,192},{192,0},{64,128},{128,64},{8,72},{72,8},{136,200},{200,136... | collective-permute-start | bytes 786440 | tf_op jit(solution)/shard_map/ppermute | solution.py:63
  42.6 1.2 %collective-permute-done.4 = bf16[256,512]{1,0:T(8,128)(2,1)S(1)} collective-permute-done((bf16[256,512]{1,0:T(8,128)(2,1)S(1)}, bf16[256,512]{1,0:T(8,128)(2,1)S(1)}, u32[]{:S(2)}, u32[]{:S(2)}) %collective-permute-start.4) | collective-permute-done | bytes 262176 | tf_op jit(solution)/shard_map/ppermute | solution.py:62
  43.8 0.1 fusion.22
  43.9 1.5 %collective-permute-start.5 = (bf16[256,512]{1,0:T(8,128)(2,1)S(1)}, bf16[256,512]{1,0:T(8,128)(2,1)S(1)}, u32[]{:S(2)}, u32[]{:S(2)}) collective-permute-start(bf16[256,512]{1,0:T(8,128)(2,1)S(1)} %fusion.22), channel_id=1, source_target_pairs={{0,192},{192,0},{64,128},{128,64},{8,72},{72,8},{136,200},{200,136... | collective-permute-start | bytes 786440 | tf_op jit(solution)/shard_map/ppermute | solution.py:63
  45.4 3.6 %collective-permute-done.13 = bf16[256,512]{1,0:T(8,128)(2,1)S(1)} collective-permute-done((bf16[256,512]{1,0:T(8,128)(2,1)S(1)}, bf16[256,512]{1,0:T(8,128)(2,1)S(1)}, u32[]{:S(2)}, u32[]{:S(2)}) %collective-permute-start.13) | collective-permute-done | bytes 262176 | tf_op jit(solution)/shard_map/ppermute | solution.py:63
  49.0 0.1 add_convert_fusion
  49.2 0.6 collective-permute-start.14
  49.8 5.7 %collective-permute-done.5 = bf16[256,512]{1,0:T(8,128)(2,1)S(1)} collective-permute-done((bf16[256,512]{1,0:T(8,128)(2,1)S(1)}, bf16[256,512]{1,0:T(8,128)(2,1)S(1)}, u32[]{:S(2)}, u32[]{:S(2)}) %collective-permute-start.5) | collective-permute-done | bytes 262176 | tf_op jit(solution)/shard_map/ppermute | solution.py:63
  55.4 0.1 add_convert_fusion.1
  55.6 0.9 collective-permute-start.6
  56.5 1.3 %constant_dynamic-update-slice_fusion.1 = bf16[512,2048]{1,0:T(8,128)(2,1)S(1)} fusion(bf16[256,2048]{1,0:T(8,128)(2,1)} %param.5), kind=kLoop, calls=%fused_computation.55 | loop fusion | bytes 2097152
  57.8 3.1 %collective-permute-start.16 = (bf16[256,512]{1,0:T(8,128)(2,1)S(1)}, bf16[256,512]{1,0:T(8,128)(2,1)S(1)}, u32[]{:S(2)}, u32[]{:S(2)}) collective-permute-start(bf16[256,512]{1,0:T(8,128)(2,1)S(1)} %add_convert_fusion), channel_id=1, source_target_pairs={{0,16},{16,0},{32,48},{48,32},{8,56},{56,8},{24,40},{40,24},{1,17}... | collective-permute-start | bytes 786440 | tf_op jit(solution)/shard_map/ppermute | solution.py:67
  60.9 1.3 %constant_dynamic-update-slice_fusion = bf16[512,2048]{1,0:T(8,128)(2,1)S(1)} fusion(bf16[512,2048]{1,0:T(8,128)(2,1)S(1)} %constant_dynamic-update-slice_fusion.1, bf16[256,2048]{1,0:T(8,128)(2,1)} %collective-permute-done.8), kind=kLoop, calls=%fused_computation.54 | loop fusion | bytes 2097152 | tf_op jit(solution)/shard_map/concatenate | solution.py:51
  62.2 0.3 collective-permute-start.9
  62.5 0.0 collective-permute-done.14
  62.5 2.7 %collective-permute-start.15 = (bf16[256,512]{1,0:T(8,128)(2,1)}, bf16[256,512]{1,0:T(8,128)(2,1)S(1)}, u32[]{:S(2)}, u32[]{:S(2)}) collective-permute-start(bf16[256,512]{1,0:T(8,128)(2,1)} %collective-permute-done.14), channel_id=1, source_target_pairs={{0,16},{16,0},{32,48},{48,32},{8,56},{56,8},{24,40},{40,24},{1,17}... | collective-permute-start | bytes 786440 | tf_op jit(solution)/shard_map/ppermute | solution.py:68
  65.2 0.1 collective-permute-start.7
  65.3 1.5 %fusion.2 = f32[256,512]{1,0:T(8,128)S(1)} fusion(bf16[512,2048]{1,0:T(8,128)(2,1)S(1)} %constant_dynamic-update-slice_fusion, s32[]{:T(128)S(6)} %select_n.85, bf16[256,512]{1,0:T(8,128)(2,1)} %collective-permute-done.14, bf16[256,512]{1,0:T(8,128)(2,1)S(1)} %add_convert_fusion, pred[]{:T(512)S(6)} %eq.14), kind=kOutput, calls=%fused_computation.12 | convolution fusion | flops 270794752 | bytes 2097157 | tf_op jit(solution)/shard_map/dot_general | solution.py:26
  66.8 0.0 collective-permute-done.16
  66.8 0.3 convolution_add_fusion.2
  67.2 1.5 %fusion.4 = f32[256,512]{1,0:T(8,128)S(1)} fusion(bf16[512,2048]{1,0:T(8,128)(2,1)S(1)} %constant_dynamic-update-slice_fusion, s32[]{:T(128)S(6)} %select_n.85, bf16[256,512]{1,0:T(8,128)(2,1)} %collective-permute-done.6, bf16[256,512]{1,0:T(8,128)(2,1)S(1)} %add_convert_fusion.1, pred[]{:T(512)S(6)} %eq.14), kind=kOutput, calls=%fused_computation.14 | convolution fusion | flops 270794752 | bytes 2097157 | tf_op jit(solution)/shard_map/dot_general | solution.py:26
  68.7 1.6 %collective-permute-done.9 = bf16[256,512]{1,0:T(8,128)(2,1)S(1)} collective-permute-done((bf16[256,512]{1,0:T(8,128)(2,1)S(1)}, bf16[256,512]{1,0:T(8,128)(2,1)S(1)}, u32[]{:S(2)}, u32[]{:S(2)}) %collective-permute-start.9) | collective-permute-done | bytes 262176 | tf_op jit(solution)/shard_map/ppermute | solution.py:67
  70.3 0.3 convolution_add_fusion.4
  70.7 2.5 %collective-permute-done.15 = bf16[256,512]{1,0:T(8,128)(2,1)S(1)} collective-permute-done((bf16[256,512]{1,0:T(8,128)(2,1)}, bf16[256,512]{1,0:T(8,128)(2,1)S(1)}, u32[]{:S(2)}, u32[]{:S(2)}) %collective-permute-start.15) | collective-permute-done | bytes 262176 | tf_op jit(solution)/shard_map/ppermute | solution.py:68
  73.1 0.3 fusion.1
  73.5 0.1 reshape.29
  73.5 2.4 %collective-permute-done.7 = bf16[256,512]{1,0:T(8,128)(2,1)S(1)} collective-permute-done((bf16[256,512]{1,0:T(8,128)(2,1)}, bf16[256,512]{1,0:T(8,128)(2,1)S(1)}, u32[]{:S(2)}, u32[]{:S(2)}) %collective-permute-start.7) | collective-permute-done | bytes 262176 | tf_op jit(solution)/shard_map/ppermute | solution.py:68
  75.9 0.3 fusion
  76.3 0.1 reshape.28
  76.4 0.1 copy_bitcast_fusion
  76.5 0.1 pad_maximum_fusion
  76.5 0.1 reverse_select_fusion
  76.6 16.4 %all_to_all.5 = bf16[16,64,256]{2,1,0:T(8,128)(2,1)S(1)} all-to-all(bf16[16,64,256]{2,1,0:T(8,128)(2,1)S(1)} %bitcast.40), channel_id=1, replica_groups=mesh['zh'=4,'y'=4,'core'=2,'x'=4,'zl'=2] {'core','x','zl'}, dimensions={0} | all-to-all | bytes 1048576 | tf_op jit(solution)/shard_map/all_to_all | solution.py:73
  93.0 0.7 bitcast_reduce_fusion
  (12 shorter events, 0.1 us)
Async XLA Ops:
  0.0 8.7 %collective-permute-start.1 = (bf16[512,2048]{1,0:T(8,128)(2,1)}, bf16[512,2048]{1,0:T(8,128)(2,1)S(1)}, u32[]{:S(2)}, u32[]{:S(2)}) collective-permute-start(bf16[512,2048]{1,0:T(8,128)(2,1)} %param.4), channel_id=1, source_target_pairs={{0,8},{8,0},{1,9},{9,1},{2,10},{10,2},{3,11},{11,3},{4,12},{12,4},... | collective-permute-start | bytes 6291464 | tf_op jit(solution)/shard_map/ppermute | solution.py:41
  5.4 3.3 %collective-permute-start = (bf16[2,256,512]{2,1,0:T(8,128)(2,1)}, bf16[2,256,512]{2,1,0:T(8,128)(2,1)S(1)}, u32[]{:S(2)}, u32[]{:S(2)}) collective-permute-start(bf16[2,256,512]{2,1,0:T(8,128)(2,1)} %bitcast.6), channel_id=1, source_target_pairs={{0,8},{8,0},{1,9},{9,1},{2,10},{10,2},{3,11},{11,3},{4,12},{12,4},... | collective-permute-start | bytes 1572872 | tf_op jit(solution)/shard_map/ppermute | solution.py:49
  5.4 2.5 %copy-start = (bf16[512,2048]{1,0:T(8,128)(2,1)S(1)}, bf16[512,2048]{1,0:T(8,128)(2,1)}, u32[]{:S(2)}) copy-start(bf16[512,2048]{1,0:T(8,128)(2,1)} %param.4) | copy-start | bytes 6291460
  9.4 2.0 %copy-start.3 = (f32[256,2048]{1,0:T(8,128)}, f32[256,2048]{1,0:T(8,128)S(1)}, u32[]{:S(2)}) copy-start(f32[256,2048]{1,0:T(8,128)S(1)} %convolution_add_fusion) | copy-start | bytes 6291460
  9.5 9.4 %collective-permute-start.10 = (bf16[256,1024]{1,0:T(8,128)(2,1)S(1)}, bf16[256,1024]{1,0:T(8,128)(2,1)}, u32[]{:S(2)}, u32[]{:S(2)}) collective-permute-start(bf16[256,1024]{1,0:T(8,128)(2,1)S(1)} %dynamic-slice_convert_fusion), channel_id=1, source_target_pairs={{0,16},{16,0},{32,48},{48,32},{8,56},{56,8},{24,40},{40,24},{1,17}... | collective-permute-start | bytes 1572872 | tf_op jit(solution)/shard_map/ppermute | solution.py:57
  11.4 1.3 %copy-start.1 = (f32[256,2048]{1,0:T(8,128)}, f32[256,2048]{1,0:T(8,128)S(1)}, u32[]{:S(2)}) copy-start(f32[256,2048]{1,0:T(8,128)S(1)} %convolution_add_fusion.1) | copy-start | bytes 6291460
  12.8 11.7 %collective-permute-start.2 = (bf16[256,1024]{1,0:T(8,128)(2,1)S(1)}, bf16[256,1024]{1,0:T(8,128)(2,1)S(1)}, u32[]{:S(2)}, u32[]{:S(2)}) collective-permute-start(bf16[256,1024]{1,0:T(8,128)(2,1)S(1)} %dynamic-slice_convert_fusion.1), channel_id=1, source_target_pairs={{0,16},{16,0},{32,48},{48,32},{8,56},{56,8},{24,40},{40,24},{1,17}... | collective-permute-start | bytes 1572872 | tf_op jit(solution)/shard_map/ppermute | solution.py:57
  14.5 9.9 %copy-start.2 = (f32[256,2048]{1,0:T(8,128)S(1)}, f32[256,2048]{1,0:T(8,128)}, u32[]{:S(2)}) copy-start(f32[256,2048]{1,0:T(8,128)} %copy-done.1) | copy-start | bytes 6291460
  20.5 6.8 %collective-permute-start.11 = (bf16[256,512]{1,0:T(8,128)(2,1)S(1)}, bf16[256,512]{1,0:T(8,128)(2,1)S(1)}, u32[]{:S(2)}, u32[]{:S(2)}) collective-permute-start(bf16[256,512]{1,0:T(8,128)(2,1)S(1)} %dynamic-slice_convert_fusion.2), channel_id=1, source_target_pairs={{0,48},{48,0},{16,32},{32,16},{8,24},{24,8},{40,56},{56,40},{1,49}... | collective-permute-start | bytes 786440 | tf_op jit(solution)/shard_map/ppermute | solution.py:60
  24.7 7.1 %collective-permute-start.3 = (bf16[256,512]{1,0:T(8,128)(2,1)S(1)}, bf16[256,512]{1,0:T(8,128)(2,1)S(1)}, u32[]{:S(2)}, u32[]{:S(2)}) collective-permute-start(bf16[256,512]{1,0:T(8,128)(2,1)S(1)} %dynamic-slice_convert_fusion.3), channel_id=1, source_target_pairs={{0,48},{48,0},{16,32},{32,16},{8,24},{24,8},{40,56},{56,40},{1,49}... | collective-permute-start | bytes 786440 | tf_op jit(solution)/shard_map/ppermute | solution.py:60
  27.4 10.9 %collective-permute-start.12 = (bf16[256,512]{1,0:T(8,128)(2,1)S(1)}, bf16[256,512]{1,0:T(8,128)(2,1)S(1)}, u32[]{:S(2)}, u32[]{:S(2)}) collective-permute-start(bf16[256,512]{1,0:T(8,128)(2,1)S(1)} %fusion.25), channel_id=1, source_target_pairs={{0,64},{64,0},{128,192},{192,128},{8,200},{200,8},{72,136},{136,72... | collective-permute-start | bytes 786440 | tf_op jit(solution)/shard_map/ppermute | solution.py:62
  31.9 11.9 %collective-permute-start.4 = (bf16[256,512]{1,0:T(8,128)(2,1)S(1)}, bf16[256,512]{1,0:T(8,128)(2,1)S(1)}, u32[]{:S(2)}, u32[]{:S(2)}) collective-permute-start(bf16[256,512]{1,0:T(8,128)(2,1)S(1)} %fusion.24), channel_id=1, source_target_pairs={{0,64},{64,0},{128,192},{192,128},{8,200},{200,8},{72,136},{136,72... | collective-permute-start | bytes 786440 | tf_op jit(solution)/shard_map/ppermute | solution.py:62
  34.5 26.4 %collective-permute-start.8 = (bf16[256,2048]{1,0:T(8,128)(2,1)}, bf16[256,2048]{1,0:T(8,128)(2,1)}, u32[]{:S(2)}, u32[]{:S(2)}) collective-permute-start(bf16[256,2048]{1,0:T(8,128)(2,1)} %param.5), channel_id=1, source_target_pairs={{0,8},{8,0},{1,9},{9,1},{2,10},{10,2},{3,11},{11,3},{4,12},{12,4},... | collective-permute-start | bytes 3145736 | tf_op jit(solution)/shard_map/ppermute | solution.py:50
  38.4 10.6 %collective-permute-start.13 = (bf16[256,512]{1,0:T(8,128)(2,1)S(1)}, bf16[256,512]{1,0:T(8,128)(2,1)S(1)}, u32[]{:S(2)}, u32[]{:S(2)}) collective-permute-start(bf16[256,512]{1,0:T(8,128)(2,1)S(1)} %fusion.23), channel_id=1, source_target_pairs={{0,192},{192,0},{64,128},{128,64},{8,72},{72,8},{136,200},{200,136... | collective-permute-start | bytes 786440 | tf_op jit(solution)/shard_map/ppermute | solution.py:63
  43.9 11.6 %collective-permute-start.5 = (bf16[256,512]{1,0:T(8,128)(2,1)S(1)}, bf16[256,512]{1,0:T(8,128)(2,1)S(1)}, u32[]{:S(2)}, u32[]{:S(2)}) collective-permute-start(bf16[256,512]{1,0:T(8,128)(2,1)S(1)} %fusion.22), channel_id=1, source_target_pairs={{0,192},{192,0},{64,128},{128,64},{8,72},{72,8},{136,200},{200,136... | collective-permute-start | bytes 786440 | tf_op jit(solution)/shard_map/ppermute | solution.py:63
  49.2 13.4 %collective-permute-start.14 = (bf16[256,512]{1,0:T(8,128)(2,1)S(1)}, bf16[256,512]{1,0:T(8,128)(2,1)}, u32[]{:S(2)}, u32[]{:S(2)}) collective-permute-start(bf16[256,512]{1,0:T(8,128)(2,1)S(1)} %add_convert_fusion), channel_id=1, source_target_pairs={{0,48},{48,0},{16,32},{32,16},{8,24},{24,8},{40,56},{56,40},{1,49}... | collective-permute-start | bytes 786440 | tf_op jit(solution)/shard_map/ppermute | solution.py:65
  55.6 9.6 %collective-permute-start.6 = (bf16[256,512]{1,0:T(8,128)(2,1)S(1)}, bf16[256,512]{1,0:T(8,128)(2,1)}, u32[]{:S(2)}, u32[]{:S(2)}) collective-permute-start(bf16[256,512]{1,0:T(8,128)(2,1)S(1)} %add_convert_fusion.1), channel_id=1, source_target_pairs={{0,48},{48,0},{16,32},{32,16},{8,24},{24,8},{40,56},{56,40},{1,49}... | collective-permute-start | bytes 786440 | tf_op jit(solution)/shard_map/ppermute | solution.py:65
  57.8 9.0 %collective-permute-start.16 = (bf16[256,512]{1,0:T(8,128)(2,1)S(1)}, bf16[256,512]{1,0:T(8,128)(2,1)S(1)}, u32[]{:S(2)}, u32[]{:S(2)}) collective-permute-start(bf16[256,512]{1,0:T(8,128)(2,1)S(1)} %add_convert_fusion), channel_id=1, source_target_pairs={{0,16},{16,0},{32,48},{48,32},{8,56},{56,8},{24,40},{40,24},{1,17}... | collective-permute-start | bytes 786440 | tf_op jit(solution)/shard_map/ppermute | solution.py:67
  62.2 8.1 %collective-permute-start.9 = (bf16[256,512]{1,0:T(8,128)(2,1)S(1)}, bf16[256,512]{1,0:T(8,128)(2,1)S(1)}, u32[]{:S(2)}, u32[]{:S(2)}) collective-permute-start(bf16[256,512]{1,0:T(8,128)(2,1)S(1)} %add_convert_fusion.1), channel_id=1, source_target_pairs={{0,16},{16,0},{32,48},{48,32},{8,56},{56,8},{24,40},{40,24},{1,17}... | collective-permute-start | bytes 786440 | tf_op jit(solution)/shard_map/ppermute | solution.py:67
  62.5 10.6 %collective-permute-start.15 = (bf16[256,512]{1,0:T(8,128)(2,1)}, bf16[256,512]{1,0:T(8,128)(2,1)S(1)}, u32[]{:S(2)}, u32[]{:S(2)}) collective-permute-start(bf16[256,512]{1,0:T(8,128)(2,1)} %collective-permute-done.14), channel_id=1, source_target_pairs={{0,16},{16,0},{32,48},{48,32},{8,56},{56,8},{24,40},{40,24},{1,17}... | collective-permute-start | bytes 786440 | tf_op jit(solution)/shard_map/ppermute | solution.py:68
  65.2 10.7 %collective-permute-start.7 = (bf16[256,512]{1,0:T(8,128)(2,1)}, bf16[256,512]{1,0:T(8,128)(2,1)S(1)}, u32[]{:S(2)}, u32[]{:S(2)}) collective-permute-start(bf16[256,512]{1,0:T(8,128)(2,1)} %collective-permute-done.6), channel_id=1, source_target_pairs={{0,16},{16,0},{32,48},{48,32},{8,56},{56,8},{24,40},{40,24},{1,17}... | collective-permute-start | bytes 786440 | tf_op jit(solution)/shard_map/ppermute | solution.py:68
